TPU v7x, 32 devices: a whole 2x2x4 slice. The times are simulated.
32 devices in a mesh: row: 4 (over y, x), mode: 8 (over z, core).
Axes of the slice: x: 2, y: 2, z: 4, core: 2. Of those that a mesh axis runs over, the one named last changes fastest.
Arguments:
- transfer_matrix: float32 [2, 768, 49152], P(None, 'row', 'mode'), may hold values from -0.01953125 to 0.01953125
- probes: float32 [2, 49152, 256], P(None, ('mode', 'row')), may hold values from -6 to 6
- intensity: float32 [768, 256], P('row'), may hold values from 0.25 to 4
Outputs:
- gradient: float32 [2, 768, 49152], P(None, 'row', 'mode')
All inputs are finite; a program needn't handle non-finite values.
Results may differ from a plain program's by a relative error of at most 0.00012.
Values sent between devices are 32-bit elements; how exact they have to be, the bound alone decides.
No kernel may reach another device: no remote copies, remote signals or barrier semaphores. Data moves between devices by JAX's collectives and lax.ppermute only.
A program may use at most 64 MiB of HBM per device.

v0:
```python
import functools

import jax
import jax.numpy as jnp
from jax import lax
from jax.experimental import pallas as pl
from jax.experimental.pallas import tpu as pltpu
from jax.sharding import PartitionSpec as P

LANES = 128
LAST_PROBES = 64
MIB = 1024 * 1024
VMEM = pl.BlockSpec(memory_space=pltpu.VMEM)
SMEM = pl.BlockSpec(memory_space=pltpu.SMEM)
COST = pl.CostEstimate(flops=1000, bytes_accessed=1000, transcendentals=0)


def halves(value):
    high = value.astype(jnp.bfloat16)
    return high, (value - high.astype(jnp.float32)).astype(jnp.bfloat16)


def dot(left, right, dimension=0):
    return lax.dot_general(
        left, right, (((1,), (dimension,)), ((), ())), preferred_element_type=jnp.float32
    )


def params(mib):
    return pltpu.CompilerParams(vmem_limit_bytes=mib * MIB)


def in_order(value, *earlier):
    return lax.optimization_barrier((value, *earlier))[0]


def groups(low, high):
    cuts = [low, *range(low // LANES * LANES + LANES, high, LANES), high]
    return list(zip(cuts, cuts[1:]))


def group_widths(low, high):
    return [end - start for start, end in groups(low, high)]


def chunk_kernel(low, high, probes_ref, *refs):
    outs, (slots_ref, done_ref, slot_done_ref) = refs[:2], refs[2:]
    half = outs[0].shape[0]
    copies, later = [], []
    for which, out_ref in enumerate(outs):
        place = 0
        modes = pl.ds(which * half, half)
        for start, end in groups(low, high):
            block = pl.ds(start // LANES * LANES, LANES)
            for part in range(2):
                if end - start == LANES:
                    target = out_ref.at[:, pl.ds(place + part * LANES, LANES)]
                    copy = pltpu.make_async_copy(
                        probes_ref.at[part, modes, block], target, done_ref.at[len(copies)]
                    )
                    copies.append(copy)
                else:
                    slot = 2 * which + part
                    copy = pltpu.make_async_copy(
                        probes_ref.at[part, modes, block], slots_ref.at[slot], slot_done_ref.at[slot]
                    )
                    later.append((copy, out_ref, slot, place + part * (end - start), start, end))
                copy.start()
            place += 2 * (end - start)
    for copy, out_ref, slot, place, start, end in later:
        copy.wait()
        first = start % LANES
        out_ref[:, place : place + end - start] = slots_ref[slot, :, first : first + end - start]
    for copy in copies:
        copy.wait()


def probe_chunk(probes, low, high):
    half, width = probes.shape[1] // 2, high - low
    whole = sum(size == LANES for size in group_widths(low, high))
    return pl.pallas_call(
        functools.partial(chunk_kernel, low, high),
        in_specs=[pl.BlockSpec(memory_space=pl.ANY)],
        out_specs=[VMEM, VMEM],
        out_shape=[jax.ShapeDtypeStruct((half, 2 * width), jnp.float32)] * 2,
        scratch_shapes=[
            pltpu.VMEM((4, half, LANES), jnp.float32),
            pltpu.SemaphoreType.DMA((max(4 * whole, 1),)),
            pltpu.SemaphoreType.DMA((4,)),
        ],
        compiler_params=params(8),
        cost_estimate=COST,
    )(probes)


def matrix_kernel(order_ref, matrix_ref, high_ref, low_ref):
    high_ref[...], low_ref[...] = halves(matrix_ref[...].reshape(high_ref.shape))


def matrix_halves(matrix, order, half):
    _, rows, modes = matrix.shape
    out = jax.ShapeDtypeStruct((2 * rows, modes), jnp.bfloat16)
    spec = pl.BlockSpec((2 * rows, half), lambda i, _: (0, i))
    return pl.pallas_call(
        matrix_kernel,
        grid_spec=pltpu.PrefetchScalarGridSpec(
            num_scalar_prefetch=1,
            grid=(modes // half,),
            in_specs=[pl.BlockSpec((2, rows, half), lambda i, order_ref: (0, 0, order_ref[i]))],
            out_specs=[spec, spec],
        ),
        out_shape=[out, out],
        compiler_params=params(12),
        cost_estimate=COST,
    )(order, matrix)


def packed_shape(rows, width):
    return rows * width // LANES, LANES


def packed(value):
    rows, width = value.shape
    blocks = [value[:, i : i + LANES] for i in range(0, width, LANES)]
    left = blocks[-1].shape[1]
    if left < LANES:
        fold = rows * left // LANES
        blocks[-1] = jnp.concatenate(
            [blocks[-1][i : i + fold] for i in range(0, rows, fold)], axis=1
        )
    return jnp.concatenate(blocks, axis=0)


def unpacked(value, rows):
    whole, left = divmod(value.shape[0], rows)
    blocks = [value[i * rows : (i + 1) * rows] for i in range(whole)]
    if left:
        width = left * LANES // rows
        folded = value[whole * rows :]
        blocks.append(
            jnp.concatenate([folded[:, i : i + width] for i in range(0, LANES, width)], axis=0)
        )
    return jnp.concatenate(blocks, axis=1)


def fields_kernel(first, widths, has_total, last, *refs):
    refs = list(refs)
    core_ref = refs.pop(0)
    total_ref = refs.pop(0) if has_total else None
    high_ref, low_ref = refs[:2]
    outs = refs[-2:] if last else refs[-1:]
    total = None
    for place, piece in enumerate(refs[2 : -len(outs)], first):
        size = piece.shape[0]
        modes = slice(place * size, (place + 1) * size)
        high, low = halves(piece[...])
        product = dot(high_ref[:, modes], jnp.concatenate([high, low], axis=1))
        middle = product.shape[1] // 2
        product = product[:, :middle] + (product[:, middle:] + dot(low_ref[:, modes], high))
        total = product if total is None else total + product
    rows = total.shape[0] // 2
    real, imag = [], []
    start = 0
    for width in widths:
        middle, end = start + width, start + 2 * width
        real.append(total[:rows, start:middle] - total[rows:, middle:end])
        imag.append(total[:rows, middle:end] + total[rows:, start:middle])
        start = end
    real, imag = jnp.concatenate(real, axis=1), jnp.concatenate(imag, axis=1)
    if has_total:
        real, imag = real + total_ref[0], imag + total_ref[1]
    if last:
        first_core = core_ref[0] == 0
        real, imag = packed(real), packed(imag)
        outs[0][...] = jnp.where(first_core, real, imag)
        outs[1][...] = jnp.where(first_core, imag, real)
    else:
        outs[0][0], outs[0][1] = real, imag


def add_fields(matrix, pieces, first, widths, core, total=None, last=False):
    rows = matrix[0].shape[0] // 2
    size, width = pieces[0].shape[0], sum(widths)
    shape = packed_shape(rows, width) if last else (2, rows, width)
    out = jax.ShapeDtypeStruct(shape, jnp.float32)
    totals = [] if total is None else [total]
    count = len(pieces)
    return pl.pallas_call(
        functools.partial(fields_kernel, first, widths, total is not None, last),
        in_specs=[SMEM] + [VMEM] * (len(totals) + 2 + count),
        out_specs=[VMEM, VMEM] if last else VMEM,
        out_shape=[out, out] if last else out,
        compiler_params=params(12),
        cost_estimate=COST,
    )(core, *totals, *matrix, *pieces)


def residual(core_ref, kept_ref, other_ref, measured_ref, scale):
    first_core = core_ref[0] == 0
    rows = measured_ref.shape[0]
    kept, other = unpacked(kept_ref[...], rows), unpacked(other_ref[...], rows)
    real, imag = jnp.where(first_core, kept, other), jnp.where(first_core, other, kept)
    excess = real * real + imag * imag - measured_ref[...]
    real, imag = excess * real * scale, excess * imag * scale
    above, below = [], []
    for start, end in groups(0, real.shape[1]):
        above += [real[:, start:end], imag[:, start:end]]
        below += [imag[:, start:end], -real[:, start:end]]
    return jnp.concatenate(
        [jnp.concatenate(above, axis=1), jnp.concatenate(below, axis=1)], axis=0
    )


def gradient_tiles(chunks, scale, core_ref, refs):
    residuals = [residual(core_ref, *refs[3 * c : 3 * c + 3], scale) for c in range(chunks)]
    high, low = halves(jnp.concatenate(residuals, axis=1))
    left = jnp.concatenate([high, high, low], axis=1)
    for pieces in zip(*[iter(refs[3 * chunks :])] * chunks):
        high, low = halves(jnp.concatenate([piece[...] for piece in pieces], axis=1))
        product = dot(left, jnp.concatenate([high, low, high], axis=1), 1)
        yield product.reshape(2, product.shape[0] // 2, product.shape[1])


def part_kernel(chunks, scale, core_ref, *refs):
    out_ref = refs[-1]
    for place, product in enumerate(gradient_tiles(chunks, scale, core_ref, refs[:-1])):
        size = product.shape[2]
        out_ref[:, :, place * size : (place + 1) * size] = product


def last_kernel(chunks, scale, has_part, core_ref, order_ref, *refs):
    part_ref = refs[0] if has_part else None
    out_ref, slots_ref, done_ref = refs[-3:]
    copies = []
    for product in gradient_tiles(chunks, scale, core_ref, refs[has_part:-3]):
        slot, size = len(copies), product.shape[2]
        if has_part:
            product = product + part_ref[:, :, slot * size : (slot + 1) * size]
        slots_ref[slot] = product
        column = pl.multiple_of(order_ref[slot] * size, size)
        copies.append(
            pltpu.make_async_copy(
                slots_ref.at[slot], out_ref.at[:, :, pl.ds(column, size)], done_ref.at[slot]
            )
        )
        copies[-1].start()
    for copy in copies:
        copy.wait()


def add_gradient(core, order, sums, chunks, places, count, part=None, last=False):
    rows = sums[0][-1].shape[0]
    size, width = chunks[0][places[0]].shape[0], sum(measured.shape[1] for _, _, measured in sums)
    modes = len(places) * size
    operands = [value for chunk_sums in sums for value in chunk_sums]
    operands += [chunk[place] for place in places for chunk in chunks]
    options = dict(
        out_shape=jax.ShapeDtypeStruct((2, rows, modes), jnp.float32),
        cost_estimate=COST,
    )
    if not last:
        return pl.pallas_call(
            functools.partial(part_kernel, len(chunks), 1.0 / count),
            in_specs=[SMEM] + [VMEM] * len(operands),
            out_specs=VMEM,
            compiler_params=params(12),
            **options,
        )(core, *operands)
    if part is not None:
        operands.insert(0, part)
    return pl.pallas_call(
        functools.partial(last_kernel, len(chunks), 1.0 / count, part is not None),
        in_specs=[SMEM, SMEM] + [VMEM] * len(operands),
        out_specs=pl.BlockSpec(memory_space=pl.ANY),
        scratch_shapes=[
            pltpu.VMEM((len(places), 2, rows, size), jnp.float32),
            pltpu.SemaphoreType.DMA((len(places),)),
        ],
        compiler_params=params(20),
        **options,
    )(core, order, *operands)


def exchange(value, axis, size, mask):
    return lax.ppermute(value, axis, [(i, i ^ mask) for i in range(size)])


def mode_exchange(value, modes, mask):
    return exchange(value, "mode", modes, mask)


def square_body(row_size, mode_size, transfer_matrix, probes, intensity):
    half, count = probes.shape[1] // 2, probes.shape[2]
    row = lax.axis_index("row")
    core = (lax.axis_index("mode") % 2).astype(jnp.int32)[None]
    near = [(0, 0), (0, 1), (1, 0), (2, 1)]
    side = [(1, 1), (2, 0)]
    far = [(3, 0), (3, 1)]
    order = jnp.stack([(row ^ mask) * 2 + which for mask, which in near + side + far]).astype(jnp.int32)

    links = {
        1: [((0, 0), (1, 0)), ((0, 1), (1, 1)), ((2, 1), (3, 1))],
        2: [((0, 1), (2, 1)), ((0, 0), (2, 0)), ((1, 0), (3, 0))],
    }
    cut = count - 2 * LAST_PROBES
    spans = [(0, cut)] if cut else []
    spans += [(cut, cut + LAST_PROBES), (cut + LAST_PROBES, count)]
    ended = {1: [], 2: []}

    def send(chunk, step, *earlier):
        for mask, transfers in links.items():
            source, target = transfers[step]
            value = in_order(chunk[source], *ended[mask][-2:-1], *earlier)
            chunk[target] = exchange(value, "row", row_size, mask)
            ended[mask].append(chunk[target])

    def fields(chunk, places, first, **options):
        pieces = [chunk[place] for place in places]
        return add_fields(matrix, pieces, first, widths, core, **options)

    transfer_matrix = pltpu.with_memory_space_constraint(transfer_matrix, pltpu.HBM)
    probes = pltpu.with_memory_space_constraint(probes, pltpu.HBM)
    chunks = [dict(zip(near[:2], probe_chunk(probes, *span))) for span in spans]
    matrix = matrix_halves(transfer_matrix, order, half)
    places = near + side + far
    bits = [1 << bit for bit in range(1, mode_size.bit_length() - 1)]
    sums, waits = [], []
    part = None

    def tied(chunk, places, *earlier):
        for place in places:
            chunk[place] = in_order(chunk[place], *earlier)

    for c, (low, high) in enumerate(spans):
        chunk, widths = chunks[c], group_widths(low, high)
        last = c == len(spans) - 1
        send(chunk, 0, *waits)
        send(chunk, 1, *(sums[-1:] if c else []))
        if c:
            total = sums[-1]
            if not last:
                near_total = fields(chunk, near, 0)
                total = in_order(total, near_total)
            arrived = mode_exchange(total, mode_size, bits[0])
            if part is not None:
                arrived = in_order(arrived, part)
            total = total + arrived
            if last:
                tied(chunk, near[2:], total)
                near_total = fields(chunk, near, 0)
        else:
            near_total = fields(chunk, near, 0)
        send(chunk, 2, *([near_total] if c else matrix), *([] if part is None else [part]))
        if c:
            tied(chunk, side, total)
            if last:
                total = in_order(total, near_total)
                for mask in bits[1:]:
                    total = total + mode_exchange(total, mode_size, mask)
                tied(chunk, side, total)
        side_total = fields(chunk, side, len(near), total=near_total)
        if c:
            if not last:
                total = in_order(total, side_total)
                for mask in bits[1:]:
                    total = total + mode_exchange(total, mode_size, mask)
            tied(chunk, far, total)
            other = mode_exchange(total, mode_size, 1)
            if last:
                tied(chunk, far, other)
            sums[-1] = total, other, intensity[:, slice(*spans[c - 1])]
        if c == 1 and cut:
            part = add_gradient(core, order, sums, chunks[:1], places, count)
        kept, sent = fields(chunk, far, len(near + side), total=side_total, last=True)
        waits = [side_total, *(chunks[c + 1][place] for place in near[:2])] if not last else []
        sums.append(kept + mode_exchange(sent, mode_size, 1))
    arrived = [mode_exchange(sums[-1], mode_size, mask) for mask in range(2, mode_size, 2)]
    total = sum(arrived, sums[-1])
    sums[-1] = total, mode_exchange(total, mode_size, 1), intensity[:, slice(*spans[-1])]
    start = 1 if cut else 0
    return add_gradient(core, order, sums[start:], chunks[start:], places, count, part, True)


def plain_body(transfer_matrix, probes, intensity):
    dot = functools.partial(
        jnp.einsum, precision=lax.Precision.HIGHEST, preferred_element_type=jnp.float32
    )
    strip = lax.all_gather(probes, "row", axis=1, tiled=True)
    products = dot("amn,bnp->abmp", transfer_matrix, strip)
    fields = jnp.stack([products[0, 0] - products[1, 1], products[0, 1] + products[1, 0]])
    fields = lax.psum(fields, "mode")
    excess = fields[0] * fields[0] + fields[1] * fields[1] - intensity
    residual = excess[None] * fields / probes.shape[2]
    products = dot("amp,bnp->abmn", residual, strip)
    return jnp.stack([products[0, 0] + products[1, 1], products[1, 0] - products[0, 1]])


def solution(mesh):
    in_specs = (P(None, "row", "mode"), P(None, ("mode", "row"), None), P("row", None))
    out_specs = P(None, "row", "mode")
    row_size, mode_size = mesh.shape["row"], mesh.shape["mode"]

    def body(transfer_matrix, probes, intensity):
        square = (
            row_size == 4
            and mode_size & (mode_size - 1) == 0
            and mode_size > 1
            and probes.shape[1] % (2 * LANES) == 0
            and probes.shape[2] % LANES == 0
            and probes.shape[2] >= 2 * LAST_PROBES
            and transfer_matrix.shape[1] % 16 == 0
        )
        if square:
            return square_body(row_size, mode_size, transfer_matrix, probes, intensity)
        return plain_body(transfer_matrix, probes, intensity)

    return jax.shard_map(body, mesh=mesh, in_specs=in_specs, out_specs=out_specs, check_vma=False)
```

profile of v0, /device:TPU:0, one launch (start us, length us, event | category | flops | bytes accessed | tf_op | source)
XLA Modules:
  0.0 127.5 jit_solution(6502316981268800513)
XLA Ops:
  1.4 3.0 %collective-permute-start = (f32[768,256]{1,0:T(8,128)S(1)}, f32[768,256]{1,0:T(8,128)S(1)}, u32[]{:S(2)}, u32[]{:S(2)}) collective-permute-start(f32[768,256]{1,0:T(8,128)S(1)} %get-tuple-element.53.refs_3_), channel_id=1, source_target_pairs={{0,8},{8,0},{16,24},{24,16},{1,9},{9,1},{17,25},{25,17},{2,10},{10... | collective-permute-start | bytes 2359304 | tf_op jit(solution)/shard_map/ppermute | solution.py:285
  6.6 7.2 %shard_map.37 = (bf16[384,6144]{1,0:T(8,128)(2,1)S(1)}, bf16[384,6144]{1,0:T(8,128)(2,1)S(1)}) custom-call(s32[8]{0:T(128)S(1)} %stack.35.order_ref, f32[2,192,6144]{2,1,0:T(8,128)} %matrix_ref.1), custom_call_target="tpu_custom_call" | custom-call | flops 1000 | bytes 1000 | tf_op jit(solution)/shard_map/pallas_call | solution.py:104
  13.9 2.2 %copy-done = bf16[384,6144]{1,0:T(8,128)(2,1)} copy-done((bf16[384,6144]{1,0:T(8,128)(2,1)}, bf16[384,6144]{1,0:T(8,128)(2,1)S(1)}, u32[]{:S(2)}) %copy-start) | copy-done | bytes 4718616
  16.1 2.2 %copy-done.2 = bf16[384,6144]{1,0:T(8,128)(2,1)} copy-done((bf16[384,6144]{1,0:T(8,128)(2,1)}, bf16[384,6144]{1,0:T(8,128)(2,1)S(1)}, u32[]{:S(2)}) %copy-start.2) | copy-done | bytes 4718616
  18.2 4.6 %collective-permute-done.refs_5_ = f32[768,256]{1,0:T(8,128)S(1)} collective-permute-done((f32[768,256]{1,0:T(8,128)S(1)}, f32[768,256]{1,0:T(8,128)S(1)}, u32[]{:S(2)}, u32[]{:S(2)}) %collective-permute-start) | collective-permute-done | bytes 786464 | tf_op jit(solution)/shard_map/ppermute | solution.py:285
  22.8 2.1 %collective-permute-done.1.refs_6_ = f32[768,256]{1,0:T(8,128)S(1)} collective-permute-done((f32[768,256]{1,0:T(8,128)S(1)}, f32[768,256]{1,0:T(8,128)S(1)}, u32[]{:S(2)}, u32[]{:S(2)}) %collective-permute-start.1) | collective-permute-done | bytes 786464 | tf_op jit(solution)/shard_map/ppermute | solution.py:285
  27.0 1.6 %shard_map.42 = (f32[768,128]{1,0:T(8,128)S(1)}, f32[768,128]{1,0:T(8,128)S(1)}) custom-call(f32[2,1536,256]{2,1,0:T(8,128)} %probes_ref.5), custom_call_target="tpu_custom_call" | custom-call | flops 1000 | bytes 1000 | tf_op jit(solution)/shard_map/pallas_call | solution.py:81
  29.3 2.3 %copy-done.1 = bf16[384,6144]{1,0:T(8,128)(2,1)S(1)} copy-done((bf16[384,6144]{1,0:T(8,128)(2,1)S(1)}, bf16[384,6144]{1,0:T(8,128)(2,1)}, u32[]{:S(2)}) %copy-start.1) | copy-done | bytes 4718616
  31.6 2.3 %copy-done.3 = bf16[384,6144]{1,0:T(8,128)(2,1)S(1)} copy-done((bf16[384,6144]{1,0:T(8,128)(2,1)S(1)}, bf16[384,6144]{1,0:T(8,128)(2,1)}, u32[]{:S(2)}) %copy-start.3) | copy-done | bytes 4718616
  34.0 2.0 %shard_map.39.refs_1_ = f32[2,192,128]{2,1,0:T(8,128)S(1)} custom-call(s32[1]{0:T(128)} %bitcast.refs_0_.core_ref, bf16[384,6144]{1,0:T(8,128)(2,1)S(1)} %copy-done.1, bf16[384,6144]{1,0:T(8,128)(2,1)S(1)} %copy-done.3, f32[768,256]{1,0:T(8,128)S(1)} %get-tuple-element.53.refs_3_, f32[768,256]{1,0:T(8,128)S(1)} %get-tuple-element.54.refs_4_, ...), custom_call_target="tpu_custom_call" | custom-call | flops 1000 | bytes 1000 | tf_op jit(solution)/shard_map/pallas_call | solution.py:188
  36.0 3.8 %collective-permute-done.2.refs_4_.refs_7_ = f32[768,256]{1,0:T(8,128)} collective-permute-done((f32[768,256]{1,0:T(8,128)S(1)}, f32[768,256]{1,0:T(8,128)}, u32[]{:S(2)}, u32[]{:S(2)}) %collective-permute-start.2) | collective-permute-done | bytes 786464 | tf_op jit(solution)/shard_map/ppermute | solution.py:285
  39.8 2.1 %collective-permute-done.3.refs_5_.refs_8_ = f32[768,256]{1,0:T(8,128)} collective-permute-done((f32[768,256]{1,0:T(8,128)S(1)}, f32[768,256]{1,0:T(8,128)}, u32[]{:S(2)}, u32[]{:S(2)}) %collective-permute-start.3) | collective-permute-done | bytes 786464 | tf_op jit(solution)/shard_map/ppermute | solution.py:285
  41.9 2.5 %shard_map.40.refs_1_ = f32[2,192,128]{2,1,0:T(8,128)S(1)} custom-call(s32[1]{0:T(128)} %bitcast.refs_0_.core_ref, f32[2,192,128]{2,1,0:T(8,128)S(1)} %shard_map.39.refs_1_, bf16[384,6144]{1,0:T(8,128)(2,1)S(1)} %copy-done.1, bf16[384,6144]{1,0:T(8,128)(2,1)S(1)} %copy-done.3, f32[768,256]{1,0:T(8,128)} %collective-permute-done.2.refs_4_.refs_7_, ...), custom_call_target="tpu_custom_call" | custom-call | flops 1000 | bytes 1000 | tf_op jit(solution)/shard_map/pallas_call | solution.py:188
  44.4 2.0 %collective-permute-start.8 = (f32[768,128]{1,0:T(8,128)S(1)}, f32[768,128]{1,0:T(8,128)S(1)}, u32[]{:S(2)}, u32[]{:S(2)}) collective-permute-start(f32[768,128]{1,0:T(8,128)S(1)} %copy-done.5), channel_id=1, source_target_pairs={{0,16},{8,24},{16,0},{24,8},{1,17},{9,25},{17,1},{25,9},{2,18},{10... | collective-permute-start | bytes 1179656 | tf_op jit(solution)/shard_map/ppermute | solution.py:285
  46.4 12.3 %collective-permute-done.4.refs_4_.refs_9_ = f32[768,256]{1,0:T(8,128)} collective-permute-done((f32[768,256]{1,0:T(8,128)S(1)}, f32[768,256]{1,0:T(8,128)}, u32[]{:S(2)}, u32[]{:S(2)}) %collective-permute-start.4) | collective-permute-done | bytes 786464 | tf_op jit(solution)/shard_map/ppermute | solution.py:285
  58.7 2.5 %shard_map.41 = (f32[192,128]{1,0:T(8,128)S(1)}, f32[192,128]{1,0:T(8,128)S(1)}) custom-call(s32[1]{0:T(128)} %bitcast.refs_0_.core_ref, f32[2,192,128]{2,1,0:T(8,128)S(1)} %shard_map.40.refs_1_, bf16[384,6144]{1,0:T(8,128)(2,1)S(1)} %copy-done.1, bf16[384,6144]{1,0:T(8,128)(2,1)S(1)} %copy-done.3, f32[768,256]{1,0:T(8,128)} %collective-permute-done.4.refs_4_.refs_9_, ...), custom_call_target="tpu_custom_call" | custom-call | flops 1000 | bytes 1000 | tf_op jit(solution)/shard_map/pallas_call | solution.py:188
  62.7 2.0 %collective-permute-start.11 = (f32[768,128]{1,0:T(8,128)S(1)}, f32[768,128]{1,0:T(8,128)S(1)}, u32[]{:S(2)}, u32[]{:S(2)}) collective-permute-start(f32[768,128]{1,0:T(8,128)S(1)} %get-tuple-element.66.refs_3_.refs_7_), channel_id=1, source_target_pairs={{0,16},{8,24},{16,0},{24,8},{1,17},{9,25},{17,1},{25,9},{2,18},{10... | collective-permute-start | bytes 1179656 | tf_op jit(solution)/shard_map/ppermute | solution.py:285
  65.6 1.5 %shard_map.43.refs_1_ = f32[2,192,64]{2,1,0:T(8,128)S(1)} custom-call(s32[1]{0:T(128)} %bitcast.refs_0_.core_ref, bf16[384,6144]{1,0:T(8,128)(2,1)S(1)} %copy-done.1, bf16[384,6144]{1,0:T(8,128)(2,1)S(1)} %copy-done.3, f32[768,128]{1,0:T(8,128)S(1)} %get-tuple-element.66.refs_3_.refs_7_, f32[768,128]{1,0:T(8,128)S(1)} %copy-done.5, ...), custom_call_target="tpu_custom_call" | custom-call | flops 1000 | bytes 1000 | tf_op jit(solution)/shard_map/pallas_call | solution.py:188
  67.2 1.5 %collective-permute-start.14 = (f32[768,128]{1,0:T(8,128)S(1)}, f32[768,128]{1,0:T(8,128)S(1)}, u32[]{:S(2)}, u32[]{:S(2)}) collective-permute-start(f32[768,128]{1,0:T(8,128)S(1)} %collective-permute-done.7.refs_5_.refs_11_), channel_id=1, source_target_pairs={{0,16},{8,24},{16,0},{24,8},{1,17},{9,25},{17,1},{25,9},{2,18},{10... | collective-permute-start | bytes 1179656 | tf_op jit(solution)/shard_map/ppermute | solution.py:285
  68.7 1.6 %collective-permute-start.9 = (f32[192,128]{1,0:T(8,128)S(1)}, f32[192,128]{1,0:T(8,128)S(1)}, u32[]{:S(2)}, u32[]{:S(2)}) collective-permute-start(f32[192,128]{1,0:T(8,128)S(1)} %add.51), channel_id=1, source_target_pairs={{0,2},{1,3},{2,0},{3,1},{4,6},{5,7},{6,4},{7,5},{8,10},{9,11},{10,... | collective-permute-start | bytes 294920 | tf_op jit(solution)/shard_map/ppermute | solution.py:285
  75.6 2.1 %collective-permute-start.18 = (f32[768,128]{1,0:T(8,128)S(1)}, f32[768,128]{1,0:T(8,128)S(1)}, u32[]{:S(2)}, u32[]{:S(2)}) collective-permute-start(f32[768,128]{1,0:T(8,128)S(1)} %get-tuple-element.86.refs_3_.refs_8_), channel_id=1, source_target_pairs={{0,8},{8,0},{16,24},{24,16},{1,9},{9,1},{17,25},{25,17},{2,10},{10... | collective-permute-start | bytes 1179656 | tf_op jit(solution)/shard_map/ppermute | solution.py:285
  79.2 2.6 %collective-permute-start.12 = (f32[192,128]{1,0:T(8,128)S(1)}, f32[192,128]{1,0:T(8,128)S(1)}, u32[]{:S(2)}, u32[]{:S(2)}) collective-permute-start(f32[192,128]{1,0:T(8,128)S(1)} %add.52), channel_id=1, source_target_pairs={{0,4},{1,5},{2,6},{3,7},{4,0},{5,1},{6,2},{7,3},{8,12},{9,13},{10,... | collective-permute-start | bytes 294920 | tf_op jit(solution)/shard_map/ppermute | solution.py:285
  81.8 2.9 %collective-permute-done.12 = f32[192,128]{1,0:T(8,128)S(1)} collective-permute-done((f32[192,128]{1,0:T(8,128)S(1)}, f32[192,128]{1,0:T(8,128)S(1)}, u32[]{:S(2)}, u32[]{:S(2)}) %collective-permute-start.12) | collective-permute-done | bytes 98336 | tf_op jit(solution)/shard_map/ppermute | solution.py:285
  87.2 1.7 %collective-permute-start.17 = (f32[96,128]{1,0:T(8,128)S(1)}, f32[96,128]{1,0:T(8,128)S(1)}, u32[]{:S(2)}, u32[]{:S(2)}) collective-permute-start(f32[96,128]{1,0:T(8,128)S(1)} %add.54), channel_id=1, source_target_pairs={{0,2},{1,3},{2,0},{3,1},{4,6},{5,7},{6,4},{7,5},{8,10},{9,11},{10,... | collective-permute-start | bytes 147464 | tf_op jit(solution)/shard_map/ppermute | solution.py:285
  90.6 5.7 %shard_map.45.refs_0_ = f32[2,192,6144]{2,1,0:T(8,128)S(1)} custom-call(s32[1]{0:T(128)} %bitcast.refs_0_.core_ref, f32[192,128]{1,0:T(8,128)S(1)} %add.53.refs_0_, f32[192,128]{1,0:T(8,128)S(1)} %collective-permute-done.13.refs_1_, f32[192,128]{1,0:T(8,128)S(1)} %slice.9.refs_2_, f32[768,256]{1,0:T(8,128)S(1)} %get-tuple-element.53.refs_3_, ...), custom_call_target="tpu_custom_call" | custom-call | flops 1000 | bytes 1000 | tf_op jit(solution)/shard_map/pallas_call | solution.py:262
  100.5 3.4 %collective-permute-start.20 = (f32[96,128]{1,0:T(8,128)S(1)}, f32[96,128]{1,0:T(8,128)S(1)}, u32[]{:S(2)}, u32[]{:S(2)}) collective-permute-start(f32[96,128]{1,0:T(8,128)S(1)} %add.55), channel_id=1, source_target_pairs={{0,4},{1,5},{2,6},{3,7},{4,0},{5,1},{6,2},{7,3},{8,12},{9,13},{10,... | collective-permute-start | bytes 147464 | tf_op jit(solution)/shard_map/ppermute | solution.py:285
  103.9 2.1 %collective-permute-done.20 = f32[96,128]{1,0:T(8,128)S(1)} collective-permute-done((f32[96,128]{1,0:T(8,128)S(1)}, f32[96,128]{1,0:T(8,128)S(1)}, u32[]{:S(2)}, u32[]{:S(2)}) %collective-permute-start.20) | collective-permute-done | bytes 49184 | tf_op jit(solution)/shard_map/ppermute | solution.py:285
  107.1 1.7 %collective-permute-done.24.refs_4_.refs_20_ = f32[768,128]{1,0:T(8,128)S(1)} collective-permute-done((f32[768,128]{1,0:T(8,128)S(1)}, f32[768,128]{1,0:T(8,128)S(1)}, u32[]{:S(2)}, u32[]{:S(2)}) %collective-permute-start.24) | collective-permute-done | bytes 393248 | tf_op jit(solution)/shard_map/ppermute | solution.py:285
  111.6 3.2 %collective-permute-start.29 = (f32[96,128]{1,0:T(8,128)S(1)}, f32[96,128]{1,0:T(8,128)S(1)}, u32[]{:S(2)}, u32[]{:S(2)}) collective-permute-start(f32[96,128]{1,0:T(8,128)S(1)} %add.57), channel_id=1, source_target_pairs={{0,6},{1,7},{2,4},{3,5},{4,2},{5,3},{6,0},{7,1},{8,14},{9,15},{10,... | collective-permute-start | bytes 147464 | tf_op jit(solution)/shard_map/ppermute | solution.py:285
  116.0 1.6 %collective-permute-done.29 = f32[96,128]{1,0:T(8,128)S(1)} collective-permute-done((f32[96,128]{1,0:T(8,128)S(1)}, f32[96,128]{1,0:T(8,128)S(1)}, u32[]{:S(2)}, u32[]{:S(2)}) %collective-permute-start.29) | collective-permute-done | bytes 49184 | tf_op jit(solution)/shard_map/ppermute | solution.py:285
  117.6 2.4 %collective-permute-done.28 = f32[96,128]{1,0:T(8,128)S(1)} collective-permute-done((f32[96,128]{1,0:T(8,128)S(1)}, f32[96,128]{1,0:T(8,128)S(1)}, u32[]{:S(2)}, u32[]{:S(2)}) %collective-permute-start.28) | collective-permute-done | bytes 49184 | tf_op jit(solution)/shard_map/ppermute | solution.py:285
  121.3 6.0 %shard_map.51 = f32[2,192,6144]{2,1,0:T(8,128)} custom-call(s32[1]{0:T(128)} %bitcast.refs_0_.core_ref, s32[8]{0:T(128)S(1)} %stack.35.order_ref, f32[2,192,6144]{2,1,0:T(8,128)S(1)} %shard_map.45.refs_0_, f32[96,128]{1,0:T(8,128)S(1)} %add.56.refs_1_, f32[96,128]{1,0:T(8,128)S(1)} %collective-permute-done.21.refs_2_, ...), custom_call_target="tpu_custom_call" | custom-call | flops 1000 | bytes 1000 | tf_op jit(solution)/shard_map/pallas_call | solution.py:271
  (80 shorter events, 30.4 us)
Async XLA Ops:
  1.4 21.4 %collective-permute-start = (f32[768,256]{1,0:T(8,128)S(1)}, f32[768,256]{1,0:T(8,128)S(1)}, u32[]{:S(2)}, u32[]{:S(2)}) collective-permute-start(f32[768,256]{1,0:T(8,128)S(1)} %get-tuple-element.53.refs_3_), channel_id=1, source_target_pairs={{0,8},{8,0},{16,24},{24,16},{1,9},{9,1},{17,25},{25,17},{2,10},{10... | collective-permute-start | bytes 2359304 | tf_op jit(solution)/shard_map/ppermute | solution.py:285
  4.4 20.5 %collective-permute-start.1 = (f32[768,256]{1,0:T(8,128)S(1)}, f32[768,256]{1,0:T(8,128)S(1)}, u32[]{:S(2)}, u32[]{:S(2)}) collective-permute-start(f32[768,256]{1,0:T(8,128)S(1)} %get-tuple-element.54.refs_4_), channel_id=1, source_target_pairs={{0,16},{8,24},{16,0},{24,8},{1,17},{9,25},{17,1},{25,9},{2,18},{10... | collective-permute-start | bytes 2359304 | tf_op jit(solution)/shard_map/ppermute | solution.py:285
  6.0 33.8 %collective-permute-start.2 = (f32[768,256]{1,0:T(8,128)S(1)}, f32[768,256]{1,0:T(8,128)}, u32[]{:S(2)}, u32[]{:S(2)}) collective-permute-start(f32[768,256]{1,0:T(8,128)S(1)} %get-tuple-element.54.refs_4_), channel_id=1, source_target_pairs={{0,8},{8,0},{16,24},{24,16},{1,9},{9,1},{17,25},{25,17},{2,10},{10... | collective-permute-start | bytes 2359304 | tf_op jit(solution)/shard_map/ppermute | solution.py:285
  6.5 35.4 %collective-permute-start.3 = (f32[768,256]{1,0:T(8,128)S(1)}, f32[768,256]{1,0:T(8,128)}, u32[]{:S(2)}, u32[]{:S(2)}) collective-permute-start(f32[768,256]{1,0:T(8,128)S(1)} %get-tuple-element.53.refs_3_), channel_id=1, source_target_pairs={{0,16},{8,24},{16,0},{24,8},{1,17},{9,25},{17,1},{25,9},{2,18},{10... | collective-permute-start | bytes 2359304 | tf_op jit(solution)/shard_map/ppermute | solution.py:285
  24.9 33.8 %collective-permute-start.4 = (f32[768,256]{1,0:T(8,128)S(1)}, f32[768,256]{1,0:T(8,128)}, u32[]{:S(2)}, u32[]{:S(2)}) collective-permute-start(f32[768,256]{1,0:T(8,128)S(1)} %collective-permute-done.refs_5_), channel_id=1, source_target_pairs={{0,16},{8,24},{16,0},{24,8},{1,17},{9,25},{17,1},{25,9},{2,18},{10... | collective-permute-start | bytes 2359304 | tf_op jit(solution)/shard_map/ppermute | solution.py:285
  26.4 32.3 %collective-permute-start.5 = (f32[768,256]{1,0:T(8,128)S(1)}, f32[768,256]{1,0:T(8,128)}, u32[]{:S(2)}, u32[]{:S(2)}) collective-permute-start(f32[768,256]{1,0:T(8,128)S(1)} %collective-permute-done.1.refs_6_), channel_id=1, source_target_pairs={{0,8},{8,0},{16,24},{24,16},{1,9},{9,1},{17,25},{25,17},{2,10},{10... | collective-permute-start | bytes 2359304 | tf_op jit(solution)/shard_map/ppermute | solution.py:285
  44.3 20.4 %collective-permute-start.7 = (f32[768,128]{1,0:T(8,128)S(1)}, f32[768,128]{1,0:T(8,128)S(1)}, u32[]{:S(2)}, u32[]{:S(2)}) collective-permute-start(f32[768,128]{1,0:T(8,128)S(1)} %get-tuple-element.66.refs_3_.refs_7_), channel_id=1, source_target_pairs={{0,8},{8,0},{16,24},{24,16},{1,9},{9,1},{17,25},{25,17},{2,10},{10... | collective-permute-start | bytes 1179656 | tf_op jit(solution)/shard_map/ppermute | solution.py:285
  44.4 21.2 %collective-permute-start.8 = (f32[768,128]{1,0:T(8,128)S(1)}, f32[768,128]{1,0:T(8,128)S(1)}, u32[]{:S(2)}, u32[]{:S(2)}) collective-permute-start(f32[768,128]{1,0:T(8,128)S(1)} %copy-done.5), channel_id=1, source_target_pairs={{0,16},{8,24},{16,0},{24,8},{1,17},{9,25},{17,1},{25,9},{2,18},{10... | collective-permute-start | bytes 1179656 | tf_op jit(solution)/shard_map/ppermute | solution.py:285
  61.2 1.4 %collective-permute-start.6 = (f32[192,128]{1,0:T(8,128)S(1)}, f32[192,128]{1,0:T(8,128)S(1)}, u32[]{:S(2)}, u32[]{:S(2)}) collective-permute-start(f32[192,128]{1,0:T(8,128)S(1)} %get-tuple-element.58), channel_id=1, source_target_pairs={{0,1},{1,0},{2,3},{3,2},{4,5},{5,4},{6,7},{7,6},{8,9},{9,8},{10,11... | collective-permute-start | bytes 294920 | tf_op jit(solution)/shard_map/ppermute | solution.py:285
  62.6 12.0 %collective-permute-start.10 = (f32[768,128]{1,0:T(8,128)S(1)}, f32[768,128]{1,0:T(8,128)S(1)}, u32[]{:S(2)}, u32[]{:S(2)}) collective-permute-start(f32[768,128]{1,0:T(8,128)S(1)} %copy-done.5), channel_id=1, source_target_pairs={{0,8},{8,0},{16,24},{24,16},{1,9},{9,1},{17,25},{25,17},{2,10},{10... | collective-permute-start | bytes 1179656 | tf_op jit(solution)/shard_map/ppermute | solution.py:285
  62.7 12.0 %collective-permute-start.11 = (f32[768,128]{1,0:T(8,128)S(1)}, f32[768,128]{1,0:T(8,128)S(1)}, u32[]{:S(2)}, u32[]{:S(2)}) collective-permute-start(f32[768,128]{1,0:T(8,128)S(1)} %get-tuple-element.66.refs_3_.refs_7_), channel_id=1, source_target_pairs={{0,16},{8,24},{16,0},{24,8},{1,17},{9,25},{17,1},{25,9},{2,18},{10... | collective-permute-start | bytes 1179656 | tf_op jit(solution)/shard_map/ppermute | solution.py:285
  67.2 17.6 %collective-permute-start.14 = (f32[768,128]{1,0:T(8,128)S(1)}, f32[768,128]{1,0:T(8,128)S(1)}, u32[]{:S(2)}, u32[]{:S(2)}) collective-permute-start(f32[768,128]{1,0:T(8,128)S(1)} %collective-permute-done.7.refs_5_.refs_11_), channel_id=1, source_target_pairs={{0,16},{8,24},{16,0},{24,8},{1,17},{9,25},{17,1},{25,9},{2,18},{10... | collective-permute-start | bytes 1179656 | tf_op jit(solution)/shard_map/ppermute | solution.py:285
  68.7 4.6 %collective-permute-start.9 = (f32[192,128]{1,0:T(8,128)S(1)}, f32[192,128]{1,0:T(8,128)S(1)}, u32[]{:S(2)}, u32[]{:S(2)}) collective-permute-start(f32[192,128]{1,0:T(8,128)S(1)} %add.51), channel_id=1, source_target_pairs={{0,2},{1,3},{2,0},{3,1},{4,6},{5,7},{6,4},{7,5},{8,10},{9,11},{10,... | collective-permute-start | bytes 294920 | tf_op jit(solution)/shard_map/ppermute | solution.py:285
  70.3 14.5 %collective-permute-start.15 = (f32[768,128]{1,0:T(8,128)S(1)}, f32[768,128]{1,0:T(8,128)S(1)}, u32[]{:S(2)}, u32[]{:S(2)}) collective-permute-start(f32[768,128]{1,0:T(8,128)S(1)} %collective-permute-done.8.refs_6_.refs_13_), channel_id=1, source_target_pairs={{0,8},{8,0},{16,24},{24,16},{1,9},{9,1},{17,25},{25,17},{2,10},{10... | collective-permute-start | bytes 1179656 | tf_op jit(solution)/shard_map/ppermute | solution.py:285
  73.3 15.6 %copy-start.6 = (f32[192,256]{1,0:T(8,128)S(1)}, f32[192,256]{1,0:T(8,128)}, u32[]{:S(2)}) copy-start(f32[192,256]{1,0:T(8,128)} %param.5) | copy-start | bytes 589828
  75.6 20.8 %collective-permute-start.18 = (f32[768,128]{1,0:T(8,128)S(1)}, f32[768,128]{1,0:T(8,128)S(1)}, u32[]{:S(2)}, u32[]{:S(2)}) collective-permute-start(f32[768,128]{1,0:T(8,128)S(1)} %get-tuple-element.86.refs_3_.refs_8_), channel_id=1, source_target_pairs={{0,8},{8,0},{16,24},{24,16},{1,9},{9,1},{17,25},{25,17},{2,10},{10... | collective-permute-start | bytes 1179656 | tf_op jit(solution)/shard_map/ppermute | solution.py:285
  77.6 18.7 %collective-permute-start.19 = (f32[768,128]{1,0:T(8,128)S(1)}, f32[768,128]{1,0:T(8,128)S(1)}, u32[]{:S(2)}, u32[]{:S(2)}) collective-permute-start(f32[768,128]{1,0:T(8,128)S(1)} %get-tuple-element.83.refs_4_.refs_10_), channel_id=1, source_target_pairs={{0,16},{8,24},{16,0},{24,8},{1,17},{9,25},{17,1},{25,9},{2,18},{10... | collective-permute-start | bytes 1179656 | tf_op jit(solution)/shard_map/ppermute | solution.py:285
  79.2 5.5 %collective-permute-start.12 = (f32[192,128]{1,0:T(8,128)S(1)}, f32[192,128]{1,0:T(8,128)S(1)}, u32[]{:S(2)}, u32[]{:S(2)}) collective-permute-start(f32[192,128]{1,0:T(8,128)S(1)} %add.52), channel_id=1, source_target_pairs={{0,4},{1,5},{2,6},{3,7},{4,0},{5,1},{6,2},{7,3},{8,12},{9,13},{10,... | collective-permute-start | bytes 294920 | tf_op jit(solution)/shard_map/ppermute | solution.py:285
  84.7 4.8 %collective-permute-start.13 = (f32[192,128]{1,0:T(8,128)S(1)}, f32[192,128]{1,0:T(8,128)S(1)}, u32[]{:S(2)}, u32[]{:S(2)}) collective-permute-start(f32[192,128]{1,0:T(8,128)S(1)} %add.53.refs_0_), channel_id=1, source_target_pairs={{0,1},{1,0},{2,3},{3,2},{4,5},{5,4},{6,7},{7,6},{8,9},{9,8},{10,11... | collective-permute-start | bytes 294920 | tf_op jit(solution)/shard_map/ppermute | solution.py:285
  85.8 1.4 %collective-permute-start.16 = (f32[96,128]{1,0:T(8,128)S(1)}, f32[96,128]{1,0:T(8,128)S(1)}, u32[]{:S(2)}, u32[]{:S(2)}) collective-permute-start(f32[96,128]{1,0:T(8,128)S(1)} %get-tuple-element.74), channel_id=1, source_target_pairs={{0,1},{1,0},{2,3},{3,2},{4,5},{5,4},{6,7},{7,6},{8,9},{9,8},{10,11... | collective-permute-start | bytes 147464 | tf_op jit(solution)/shard_map/ppermute | solution.py:285
  87.2 9.1 %collective-permute-start.17 = (f32[96,128]{1,0:T(8,128)S(1)}, f32[96,128]{1,0:T(8,128)S(1)}, u32[]{:S(2)}, u32[]{:S(2)}) collective-permute-start(f32[96,128]{1,0:T(8,128)S(1)} %add.54), channel_id=1, source_target_pairs={{0,2},{1,3},{2,0},{3,1},{4,6},{5,7},{6,4},{7,5},{8,10},{9,11},{10,... | collective-permute-start | bytes 147464 | tf_op jit(solution)/shard_map/ppermute | solution.py:285
  88.9 17.2 %collective-permute-start.22 = (f32[768,128]{1,0:T(8,128)S(1)}, f32[768,128]{1,0:T(8,128)S(1)}, u32[]{:S(2)}, u32[]{:S(2)}) collective-permute-start(f32[768,128]{1,0:T(8,128)S(1)} %get-tuple-element.83.refs_4_.refs_10_), channel_id=1, source_target_pairs={{0,8},{8,0},{16,24},{24,16},{1,9},{9,1},{17,25},{25,17},{2,10},{10... | collective-permute-start | bytes 1179656 | tf_op jit(solution)/shard_map/ppermute | solution.py:285
  89.6 16.7 %collective-permute-start.23 = (f32[768,128]{1,0:T(8,128)S(1)}, f32[768,128]{1,0:T(8,128)S(1)}, u32[]{:S(2)}, u32[]{:S(2)}) collective-permute-start(f32[768,128]{1,0:T(8,128)S(1)} %get-tuple-element.86.refs_3_.refs_8_), channel_id=1, source_target_pairs={{0,16},{8,24},{16,0},{24,8},{1,17},{9,25},{17,1},{25,9},{2,18},{10... | collective-permute-start | bytes 1179656 | tf_op jit(solution)/shard_map/ppermute | solution.py:285
  98.0 10.9 %collective-permute-start.24 = (f32[768,128]{1,0:T(8,128)S(1)}, f32[768,128]{1,0:T(8,128)S(1)}, u32[]{:S(2)}, u32[]{:S(2)}) collective-permute-start(f32[768,128]{1,0:T(8,128)S(1)} %collective-permute-done.18.refs_5_.refs_12_), channel_id=1, source_target_pairs={{0,16},{8,24},{16,0},{24,8},{1,17},{9,25},{17,1},{25,9},{2,18},{10... | collective-permute-start | bytes 1179656 | tf_op jit(solution)/shard_map/ppermute | solution.py:285
  99.0 10.3 %collective-permute-start.25 = (f32[768,128]{1,0:T(8,128)S(1)}, f32[768,128]{1,0:T(8,128)S(1)}, u32[]{:S(2)}, u32[]{:S(2)}) collective-permute-start(f32[768,128]{1,0:T(8,128)S(1)} %collective-permute-done.19.refs_6_.refs_14_), channel_id=1, source_target_pairs={{0,8},{8,0},{16,24},{24,16},{1,9},{9,1},{17,25},{25,17},{2,10},{10... | collective-permute-start | bytes 1179656 | tf_op jit(solution)/shard_map/ppermute | solution.py:285
  100.5 5.4 %collective-permute-start.20 = (f32[96,128]{1,0:T(8,128)S(1)}, f32[96,128]{1,0:T(8,128)S(1)}, u32[]{:S(2)}, u32[]{:S(2)}) collective-permute-start(f32[96,128]{1,0:T(8,128)S(1)} %add.55), channel_id=1, source_target_pairs={{0,4},{1,5},{2,6},{3,7},{4,0},{5,1},{6,2},{7,3},{8,12},{9,13},{10,... | collective-permute-start | bytes 147464 | tf_op jit(solution)/shard_map/ppermute | solution.py:285
  105.9 2.9 %collective-permute-start.21 = (f32[96,128]{1,0:T(8,128)S(1)}, f32[96,128]{1,0:T(8,128)S(1)}, u32[]{:S(2)}, u32[]{:S(2)}) collective-permute-start(f32[96,128]{1,0:T(8,128)S(1)} %add.56.refs_1_), channel_id=1, source_target_pairs={{0,1},{1,0},{2,3},{3,2},{4,5},{5,4},{6,7},{7,6},{8,9},{9,8},{10,11... | collective-permute-start | bytes 147464 | tf_op jit(solution)/shard_map/ppermute | solution.py:285
  110.2 1.3 %collective-permute-start.26 = (f32[96,128]{1,0:T(8,128)S(1)}, f32[96,128]{1,0:T(8,128)S(1)}, u32[]{:S(2)}, u32[]{:S(2)}) collective-permute-start(f32[96,128]{1,0:T(8,128)S(1)} %get-tuple-element.96), channel_id=1, source_target_pairs={{0,1},{1,0},{2,3},{3,2},{4,5},{5,4},{6,7},{7,6},{8,9},{9,8},{10,11... | collective-permute-start | bytes 147464 | tf_op jit(solution)/shard_map/ppermute | solution.py:285
  111.6 6.0 %collective-permute-start.29 = (f32[96,128]{1,0:T(8,128)S(1)}, f32[96,128]{1,0:T(8,128)S(1)}, u32[]{:S(2)}, u32[]{:S(2)}) collective-permute-start(f32[96,128]{1,0:T(8,128)S(1)} %add.57), channel_id=1, source_target_pairs={{0,6},{1,7},{2,4},{3,5},{4,2},{5,3},{6,0},{7,1},{8,14},{9,15},{10,... | collective-permute-start | bytes 147464 | tf_op jit(solution)/shard_map/ppermute | solution.py:285
  114.7 5.2 %collective-permute-start.28 = (f32[96,128]{1,0:T(8,128)S(1)}, f32[96,128]{1,0:T(8,128)S(1)}, u32[]{:S(2)}, u32[]{:S(2)}) collective-permute-start(f32[96,128]{1,0:T(8,128)S(1)} %add.57), channel_id=1, source_target_pairs={{0,4},{1,5},{2,6},{3,7},{4,0},{5,1},{6,2},{7,3},{8,12},{9,13},{10,... | collective-permute-start | bytes 147464 | tf_op jit(solution)/shard_map/ppermute | solution.py:285
  115.1 4.9 %collective-permute-start.27 = (f32[96,128]{1,0:T(8,128)S(1)}, f32[96,128]{1,0:T(8,128)S(1)}, u32[]{:S(2)}, u32[]{:S(2)}) collective-permute-start(f32[96,128]{1,0:T(8,128)S(1)} %add.57), channel_id=1, source_target_pairs={{0,2},{1,3},{2,0},{3,1},{4,6},{5,7},{6,4},{7,5},{8,10},{9,11},{10,... | collective-permute-start | bytes 147464 | tf_op jit(solution)/shard_map/ppermute | solution.py:285
  120.0 1.3 %collective-permute-start.30 = (f32[96,128]{1,0:T(8,128)S(1)}, f32[96,128]{1,0:T(8,128)S(1)}, u32[]{:S(2)}, u32[]{:S(2)}) collective-permute-start(f32[96,128]{1,0:T(8,128)S(1)} %add_add_fusion.refs_4_), channel_id=1, source_target_pairs={{0,1},{1,0},{2,3},{3,2},{4,5},{5,4},{6,7},{7,6},{8,9},{9,8},{10,11... | collective-permute-start | bytes 147464 | tf_op jit(solution)/shard_map/ppermute | solution.py:285
  (10 other events, 56.4 us)
where the time goes:
time: 128 us; the launch traced here: 127 us
  waiting for transfers between devices  43.8 us (34%)
  Pallas kernels  37.1 us (29%)
  starting transfers between devices  36 us (28%)
  local copies, waits for them, and re-layouts  9.99 us (8%)
    ppermute x31, waiting for transfers between devices, exchange(): return lax.ppermute(value, axis, [(i, i ^ mask) for i in range(size)])  43.8 us
    ppermute x31, starting transfers between devices, exchange(): return lax.ppermute(value, axis, [(i, i ^ mask) for i in range(size)])  36 us
    pallas_call x9, Pallas kernels, add_fields(): pl.pallas_call(functools.partial(fields_kernel, first, widths, total is n...  13.7 us
    unnamed x22, local copies, waits for them, and re-layouts  9.82 us
    pallas_call x1, Pallas kernels, matrix_halves(): pl.pallas_call(matrix_kernel, grid_spec=pltpu.PrefetchScalarGridSpec(num_...  7.24 us
    pallas_call x1, Pallas kernels, add_gradient(): pl.pallas_call(functools.partial(last_kernel, len(chunks), 1.0 / count, p...  6.04 us
    pallas_call x1, Pallas kernels, add_gradient(): pl.pallas_call(functools.partial(part_kernel, len(chunks), 1.0 / count),...  5.71 us
    pallas_call x3, Pallas kernels, probe_chunk(): pl.pallas_call(functools.partial(chunk_kernel, low, high), in_specs=[pl.B...  4.45 us
  transfers between devices with their start and end apart: 31, of which 19 were waited for; matrix products, arithmetic and copies ran while one was open for 0% of the time, Pallas kernels for 23%

commit v1 on v0

--- a/solution.py
+++ b/solution.py
@@ -211,32 +211,44 @@
     )
 
 
-def gradient_tiles(chunks, scale, core_ref, refs):
-    residuals = [residual(core_ref, *refs[3 * c : 3 * c + 3], scale) for c in range(chunks)]
-    high, low = halves(jnp.concatenate(residuals, axis=1))
+def gradient_tiles(scale, core_ref, sums, pieces):
+    high, low = halves(residual(core_ref, *sums, scale))
     left = jnp.concatenate([high, high, low], axis=1)
-    for pieces in zip(*[iter(refs[3 * chunks :])] * chunks):
-        high, low = halves(jnp.concatenate([piece[...] for piece in pieces], axis=1))
+    for place, piece in enumerate(pieces):
+        high, low = halves(piece[...])
         product = dot(left, jnp.concatenate([high, low, high], axis=1), 1)
-        yield product.reshape(2, product.shape[0] // 2, product.shape[1])
-
-
-def part_kernel(chunks, scale, core_ref, *refs):
+        size = product.shape[1]
+        yield product.reshape(2, -1, size), slice(place * size, (place + 1) * size)
+
+
+def part_kernel(scale, has_part, core_ref, *refs):
     out_ref = refs[-1]
-    for place, product in enumerate(gradient_tiles(chunks, scale, core_ref, refs[:-1])):
-        size = product.shape[2]
-        out_ref[:, :, place * size : (place + 1) * size] = product
-
-
-def last_kernel(chunks, scale, has_part, core_ref, order_ref, *refs):
     part_ref = refs[0] if has_part else None
-    out_ref, slots_ref, done_ref = refs[-3:]
+    sums, pieces = refs[has_part : has_part + 3], refs[has_part + 3 : -1]
+    for product, modes in gradient_tiles(scale, core_ref, sums, pieces):
+        out_ref[:, :, modes] = product + part_ref[:, :, modes] if has_part else product
+
+
+def gradient_part(core, sums, pieces, count, part=None):
+    operands = [*sums, *pieces] if part is None else [part, *sums, *pieces]
+    modes = len(pieces) * pieces[0].shape[0]
+    return pl.pallas_call(
+        functools.partial(part_kernel, 1.0 / count, part is not None),
+        in_specs=[SMEM] + [VMEM] * len(operands),
+        out_specs=VMEM,
+        out_shape=jax.ShapeDtypeStruct((2, sums[-1].shape[0], modes), jnp.float32),
+        input_output_aliases={} if part is None else {1: 0},
+        compiler_params=params(12),
+        cost_estimate=COST,
+    )(core, *operands)
+
+
+def last_kernel(scale, core_ref, order_ref, part_ref, *refs):
+    pieces, (out_ref, slots_ref, done_ref) = refs[3:-3], refs[-3:]
     copies = []
-    for product in gradient_tiles(chunks, scale, core_ref, refs[has_part:-3]):
+    for product, modes in gradient_tiles(scale, core_ref, refs[:3], pieces):
         slot, size = len(copies), product.shape[2]
-        if has_part:
-            product = product + part_ref[:, :, slot * size : (slot + 1) * size]
-        slots_ref[slot] = product
+        slots_ref[slot] = product + part_ref[:, :, modes]
         column = pl.multiple_of(order_ref[slot] * size, size)
         copies.append(
             pltpu.make_async_copy(
@@ -248,36 +260,17 @@
         copy.wait()
 
 
-def add_gradient(core, order, sums, chunks, places, count, part=None, last=False):
-    rows = sums[0][-1].shape[0]
-    size, width = chunks[0][places[0]].shape[0], sum(measured.shape[1] for _, _, measured in sums)
-    modes = len(places) * size
-    operands = [value for chunk_sums in sums for value in chunk_sums]
-    operands += [chunk[place] for place in places for chunk in chunks]
-    options = dict(
-        out_shape=jax.ShapeDtypeStruct((2, rows, modes), jnp.float32),
-        cost_estimate=COST,
-    )
-    if not last:
-        return pl.pallas_call(
-            functools.partial(part_kernel, len(chunks), 1.0 / count),
-            in_specs=[SMEM] + [VMEM] * len(operands),
-            out_specs=VMEM,
-            compiler_params=params(12),
-            **options,
-        )(core, *operands)
-    if part is not None:
-        operands.insert(0, part)
+def last_gradient(core, order, part, sums, pieces, count):
+    operands = [part, *sums, *pieces]
+    slots = (len(pieces), 2, part.shape[1], pieces[0].shape[0])
     return pl.pallas_call(
-        functools.partial(last_kernel, len(chunks), 1.0 / count, part is not None),
+        functools.partial(last_kernel, 1.0 / count),
         in_specs=[SMEM, SMEM] + [VMEM] * len(operands),
         out_specs=pl.BlockSpec(memory_space=pl.ANY),
-        scratch_shapes=[
-            pltpu.VMEM((len(places), 2, rows, size), jnp.float32),
-            pltpu.SemaphoreType.DMA((len(places),)),
-        ],
+        out_shape=jax.ShapeDtypeStruct(part.shape, jnp.float32),
+        scratch_shapes=[pltpu.VMEM(slots, jnp.float32), pltpu.SemaphoreType.DMA(slots[:1])],
         compiler_params=params(20),
-        **options,
+        cost_estimate=COST,
     )(core, order, *operands)
 
 
@@ -370,15 +363,17 @@
                 tied(chunk, far, other)
             sums[-1] = total, other, intensity[:, slice(*spans[c - 1])]
         if c == 1 and cut:
-            part = add_gradient(core, order, sums, chunks[:1], places, count)
+            part = gradient_part(core, sums[0], [chunks[0][place] for place in places], count)
         kept, sent = fields(chunk, far, len(near + side), total=side_total, last=True)
         waits = [side_total, *(chunks[c + 1][place] for place in near[:2])] if not last else []
         sums.append(kept + mode_exchange(sent, mode_size, 1))
     arrived = [mode_exchange(sums[-1], mode_size, mask) for mask in range(2, mode_size, 2)]
-    total = sum(arrived, sums[-1])
+    pieces = [[chunk[place] for place in places] for chunk in chunks[-2:]]
+    before = in_order(sums[-2][0], sums[-1]), *sums[-2][1:]
+    part = gradient_part(core, before, pieces[0], count, part)
+    total = sum((in_order(value, part) for value in arrived), sums[-1])
     sums[-1] = total, mode_exchange(total, mode_size, 1), intensity[:, slice(*spans[-1])]
-    start = 1 if cut else 0
-    return add_gradient(core, order, sums[start:], chunks[start:], places, count, part, True)
+    return last_gradient(core, order, part, sums[-1], pieces[1], count)
 
 
 def plain_body(transfer_matrix, probes, intensity):

time: 128 us -> 127 us (level)
  waiting for transfers between devices: 43.8 us -> 40.9 us
  Pallas kernels: 37.1 us -> 38.9 us
    ppermute x31, waiting for transfers between devices: 43.8 us -> 40.9 us  [exchange(): return lax.ppermute(value, axis, [(i, i ^ mask) for i in range(size)])]
    pallas_call x2 -> x3, Pallas kernels: 11.7 us -> 13.5 us  [the longest x2 8.59 us: gradient_part(): pl.pallas_call(functools.partial(part_kernel, 1.0 / count, part is not No...]
  transfers between devices with their start and end apart: 31 -> 31, of which waited for: 19 -> 18; matrix products, arithmetic and copies ran while one was open for 0% -> 0% of each run, Pallas kernels for 23% -> 25%
where the time goes in v1:
time: 127 us; the launch traced here: 126 us
  waiting for transfers between devices  40.9 us (32%)
  Pallas kernels  38.9 us (31%)
  starting transfers between devices  36 us (28%)
  local copies, waits for them, and re-layouts  9.99 us (8%)
    ppermute x31, waiting for transfers between devices, exchange(): return lax.ppermute(value, axis, [(i, i ^ mask) for i in range(size)])  40.9 us
    ppermute x31, starting transfers between devices, exchange(): return lax.ppermute(value, axis, [(i, i ^ mask) for i in range(size)])  36 us
    pallas_call x9, Pallas kernels, add_fields(): pl.pallas_call(functools.partial(fields_kernel, first, widths, total is n...  13.7 us
    unnamed x22, local copies, waits for them, and re-layouts  9.82 us
    pallas_call x2, Pallas kernels, gradient_part(): pl.pallas_call(functools.partial(part_kernel, 1.0 / count, part is not No...  8.59 us
    pallas_call x1, Pallas kernels, matrix_halves(): pl.pallas_call(matrix_kernel, grid_spec=pltpu.PrefetchScalarGridSpec(num_...  7.24 us
    pallas_call x1, Pallas kernels, last_gradient(): pl.pallas_call(functools.partial(last_kernel, 1.0 / count), in_specs=[SME...  4.94 us
    pallas_call x3, Pallas kernels, probe_chunk(): pl.pallas_call(functools.partial(chunk_kernel, low, high), in_specs=[pl.B...  4.45 us
  transfers between devices with their start and end apart: 31, of which 18 were waited for; matrix products, arithmetic and copies ran while one was open for 0% of the time, Pallas kernels for 25%

profile of v1, /device:TPU:0, one launch (start us, length us, event | category | flops | bytes accessed | tf_op | source)
XLA Modules:
  0.0 126.4 jit_solution(308543317866036714)
XLA Ops:
  1.4 3.0 %collective-permute-start = (f32[768,256]{1,0:T(8,128)S(1)}, f32[768,256]{1,0:T(8,128)S(1)}, u32[]{:S(2)}, u32[]{:S(2)}) collective-permute-start(f32[768,256]{1,0:T(8,128)S(1)} %get-tuple-element.57.refs_3_), channel_id=1, source_target_pairs={{0,8},{8,0},{16,24},{24,16},{1,9},{9,1},{17,25},{25,17},{2,10},{10... | collective-permute-start | bytes 2359304 | tf_op jit(solution)/shard_map/ppermute | solution.py:278
  6.6 7.2 %shard_map.37 = (bf16[384,6144]{1,0:T(8,128)(2,1)S(1)}, bf16[384,6144]{1,0:T(8,128)(2,1)S(1)}) custom-call(s32[8]{0:T(128)S(1)} %stack.35.order_ref, f32[2,192,6144]{2,1,0:T(8,128)} %matrix_ref.1), custom_call_target="tpu_custom_call" | custom-call | flops 1000 | bytes 1000 | tf_op jit(solution)/shard_map/pallas_call | solution.py:104
  13.9 2.2 %copy-done = bf16[384,6144]{1,0:T(8,128)(2,1)} copy-done((bf16[384,6144]{1,0:T(8,128)(2,1)}, bf16[384,6144]{1,0:T(8,128)(2,1)S(1)}, u32[]{:S(2)}) %copy-start) | copy-done | bytes 4718616
  16.1 2.2 %copy-done.2 = bf16[384,6144]{1,0:T(8,128)(2,1)} copy-done((bf16[384,6144]{1,0:T(8,128)(2,1)}, bf16[384,6144]{1,0:T(8,128)(2,1)S(1)}, u32[]{:S(2)}) %copy-start.2) | copy-done | bytes 4718616
  18.2 4.6 %collective-permute-done.refs_5_ = f32[768,256]{1,0:T(8,128)S(1)} collective-permute-done((f32[768,256]{1,0:T(8,128)S(1)}, f32[768,256]{1,0:T(8,128)S(1)}, u32[]{:S(2)}, u32[]{:S(2)}) %collective-permute-start) | collective-permute-done | bytes 786464 | tf_op jit(solution)/shard_map/ppermute | solution.py:278
  22.8 2.1 %collective-permute-done.1.refs_6_ = f32[768,256]{1,0:T(8,128)S(1)} collective-permute-done((f32[768,256]{1,0:T(8,128)S(1)}, f32[768,256]{1,0:T(8,128)S(1)}, u32[]{:S(2)}, u32[]{:S(2)}) %collective-permute-start.1) | collective-permute-done | bytes 786464 | tf_op jit(solution)/shard_map/ppermute | solution.py:278
  27.0 1.6 %shard_map.42 = (f32[768,128]{1,0:T(8,128)S(1)}, f32[768,128]{1,0:T(8,128)S(1)}) custom-call(f32[2,1536,256]{2,1,0:T(8,128)} %probes_ref.5), custom_call_target="tpu_custom_call" | custom-call | flops 1000 | bytes 1000 | tf_op jit(solution)/shard_map/pallas_call | solution.py:81
  29.3 2.3 %copy-done.1 = bf16[384,6144]{1,0:T(8,128)(2,1)S(1)} copy-done((bf16[384,6144]{1,0:T(8,128)(2,1)S(1)}, bf16[384,6144]{1,0:T(8,128)(2,1)}, u32[]{:S(2)}) %copy-start.1) | copy-done | bytes 4718616
  31.6 2.3 %copy-done.3 = bf16[384,6144]{1,0:T(8,128)(2,1)S(1)} copy-done((bf16[384,6144]{1,0:T(8,128)(2,1)S(1)}, bf16[384,6144]{1,0:T(8,128)(2,1)}, u32[]{:S(2)}) %copy-start.3) | copy-done | bytes 4718616
  34.0 2.0 %shard_map.39.refs_1_ = f32[2,192,128]{2,1,0:T(8,128)S(1)} custom-call(s32[1]{0:T(128)} %bitcast.refs_0_.core_ref, bf16[384,6144]{1,0:T(8,128)(2,1)S(1)} %copy-done.1, bf16[384,6144]{1,0:T(8,128)(2,1)S(1)} %copy-done.3, f32[768,256]{1,0:T(8,128)S(1)} %get-tuple-element.57.refs_3_, f32[768,256]{1,0:T(8,128)S(1)} %get-tuple-element.58.refs_4_, ...), custom_call_target="tpu_custom_call" | custom-call | flops 1000 | bytes 1000 | tf_op jit(solution)/shard_map/pallas_call | solution.py:188
  36.0 3.8 %collective-permute-done.2.refs_4_.refs_7_ = f32[768,256]{1,0:T(8,128)} collective-permute-done((f32[768,256]{1,0:T(8,128)S(1)}, f32[768,256]{1,0:T(8,128)}, u32[]{:S(2)}, u32[]{:S(2)}) %collective-permute-start.2) | collective-permute-done | bytes 786464 | tf_op jit(solution)/shard_map/ppermute | solution.py:278
  39.8 2.1 %collective-permute-done.3.refs_5_.refs_8_ = f32[768,256]{1,0:T(8,128)} collective-permute-done((f32[768,256]{1,0:T(8,128)S(1)}, f32[768,256]{1,0:T(8,128)}, u32[]{:S(2)}, u32[]{:S(2)}) %collective-permute-start.3) | collective-permute-done | bytes 786464 | tf_op jit(solution)/shard_map/ppermute | solution.py:278
  41.9 2.5 %shard_map.40.refs_1_ = f32[2,192,128]{2,1,0:T(8,128)S(1)} custom-call(s32[1]{0:T(128)} %bitcast.refs_0_.core_ref, f32[2,192,128]{2,1,0:T(8,128)S(1)} %shard_map.39.refs_1_, bf16[384,6144]{1,0:T(8,128)(2,1)S(1)} %copy-done.1, bf16[384,6144]{1,0:T(8,128)(2,1)S(1)} %copy-done.3, f32[768,256]{1,0:T(8,128)} %collective-permute-done.2.refs_4_.refs_7_, ...), custom_call_target="tpu_custom_call" | custom-call | flops 1000 | bytes 1000 | tf_op jit(solution)/shard_map/pallas_call | solution.py:188
  44.4 2.0 %collective-permute-start.8 = (f32[768,128]{1,0:T(8,128)S(1)}, f32[768,128]{1,0:T(8,128)S(1)}, u32[]{:S(2)}, u32[]{:S(2)}) collective-permute-start(f32[768,128]{1,0:T(8,128)S(1)} %copy-done.5), channel_id=1, source_target_pairs={{0,16},{8,24},{16,0},{24,8},{1,17},{9,25},{17,1},{25,9},{2,18},{10... | collective-permute-start | bytes 1179656 | tf_op jit(solution)/shard_map/ppermute | solution.py:278
  46.4 12.3 %collective-permute-done.4.refs_4_.refs_9_ = f32[768,256]{1,0:T(8,128)} collective-permute-done((f32[768,256]{1,0:T(8,128)S(1)}, f32[768,256]{1,0:T(8,128)}, u32[]{:S(2)}, u32[]{:S(2)}) %collective-permute-start.4) | collective-permute-done | bytes 786464 | tf_op jit(solution)/shard_map/ppermute | solution.py:278
  58.7 2.5 %shard_map.41 = (f32[192,128]{1,0:T(8,128)S(1)}, f32[192,128]{1,0:T(8,128)S(1)}) custom-call(s32[1]{0:T(128)} %bitcast.refs_0_.core_ref, f32[2,192,128]{2,1,0:T(8,128)S(1)} %shard_map.40.refs_1_, bf16[384,6144]{1,0:T(8,128)(2,1)S(1)} %copy-done.1, bf16[384,6144]{1,0:T(8,128)(2,1)S(1)} %copy-done.3, f32[768,256]{1,0:T(8,128)} %collective-permute-done.4.refs_4_.refs_9_, ...), custom_call_target="tpu_custom_call" | custom-call | flops 1000 | bytes 1000 | tf_op jit(solution)/shard_map/pallas_call | solution.py:188
  62.7 2.0 %collective-permute-start.11 = (f32[768,128]{1,0:T(8,128)S(1)}, f32[768,128]{1,0:T(8,128)S(1)}, u32[]{:S(2)}, u32[]{:S(2)}) collective-permute-start(f32[768,128]{1,0:T(8,128)S(1)} %get-tuple-element.70.refs_3_.refs_4_), channel_id=1, source_target_pairs={{0,16},{8,24},{16,0},{24,8},{1,17},{9,25},{17,1},{25,9},{2,18},{10... | collective-permute-start | bytes 1179656 | tf_op jit(solution)/shard_map/ppermute | solution.py:278
  65.6 1.5 %shard_map.43.refs_1_ = f32[2,192,64]{2,1,0:T(8,128)S(1)} custom-call(s32[1]{0:T(128)} %bitcast.refs_0_.core_ref, bf16[384,6144]{1,0:T(8,128)(2,1)S(1)} %copy-done.1, bf16[384,6144]{1,0:T(8,128)(2,1)S(1)} %copy-done.3, f32[768,128]{1,0:T(8,128)S(1)} %get-tuple-element.70.refs_3_.refs_4_, f32[768,128]{1,0:T(8,128)S(1)} %copy-done.5, ...), custom_call_target="tpu_custom_call" | custom-call | flops 1000 | bytes 1000 | tf_op jit(solution)/shard_map/pallas_call | solution.py:188
  67.2 1.5 %collective-permute-start.14 = (f32[768,128]{1,0:T(8,128)S(1)}, f32[768,128]{1,0:T(8,128)S(1)}, u32[]{:S(2)}, u32[]{:S(2)}) collective-permute-start(f32[768,128]{1,0:T(8,128)S(1)} %collective-permute-done.7.refs_5_.refs_6_), channel_id=1, source_target_pairs={{0,16},{8,24},{16,0},{24,8},{1,17},{9,25},{17,1},{25,9},{2,18},{10... | collective-permute-start | bytes 1179656 | tf_op jit(solution)/shard_map/ppermute | solution.py:278
  68.7 1.6 %collective-permute-start.9 = (f32[192,128]{1,0:T(8,128)S(1)}, f32[192,128]{1,0:T(8,128)S(1)}, u32[]{:S(2)}, u32[]{:S(2)}) collective-permute-start(f32[192,128]{1,0:T(8,128)S(1)} %add.51), channel_id=1, source_target_pairs={{0,2},{1,3},{2,0},{3,1},{4,6},{5,7},{6,4},{7,5},{8,10},{9,11},{10,... | collective-permute-start | bytes 294920 | tf_op jit(solution)/shard_map/ppermute | solution.py:278
  75.6 2.1 %collective-permute-start.18 = (f32[768,128]{1,0:T(8,128)S(1)}, f32[768,128]{1,0:T(8,128)S(1)}, u32[]{:S(2)}, u32[]{:S(2)}) collective-permute-start(f32[768,128]{1,0:T(8,128)S(1)} %get-tuple-element.90.refs_3_), channel_id=1, source_target_pairs={{0,8},{8,0},{16,24},{24,16},{1,9},{9,1},{17,25},{25,17},{2,10},{10... | collective-permute-start | bytes 1179656 | tf_op jit(solution)/shard_map/ppermute | solution.py:278
  79.2 2.6 %collective-permute-start.12 = (f32[192,128]{1,0:T(8,128)S(1)}, f32[192,128]{1,0:T(8,128)S(1)}, u32[]{:S(2)}, u32[]{:S(2)}) collective-permute-start(f32[192,128]{1,0:T(8,128)S(1)} %add.52), channel_id=1, source_target_pairs={{0,4},{1,5},{2,6},{3,7},{4,0},{5,1},{6,2},{7,3},{8,12},{9,13},{10,... | collective-permute-start | bytes 294920 | tf_op jit(solution)/shard_map/ppermute | solution.py:278
  81.8 2.9 %collective-permute-done.12 = f32[192,128]{1,0:T(8,128)S(1)} collective-permute-done((f32[192,128]{1,0:T(8,128)S(1)}, f32[192,128]{1,0:T(8,128)S(1)}, u32[]{:S(2)}, u32[]{:S(2)}) %collective-permute-start.12) | collective-permute-done | bytes 98336 | tf_op jit(solution)/shard_map/ppermute | solution.py:278
  87.2 1.7 %collective-permute-start.17 = (f32[96,128]{1,0:T(8,128)S(1)}, f32[96,128]{1,0:T(8,128)S(1)}, u32[]{:S(2)}, u32[]{:S(2)}) collective-permute-start(f32[96,128]{1,0:T(8,128)S(1)} %add.54), channel_id=1, source_target_pairs={{0,2},{1,3},{2,0},{3,1},{4,6},{5,7},{6,4},{7,5},{8,10},{9,11},{10,... | collective-permute-start | bytes 147464 | tf_op jit(solution)/shard_map/ppermute | solution.py:278
  90.6 5.7 %shard_map.45.refs_0_ = f32[2,192,6144]{2,1,0:T(8,128)S(1)} custom-call(s32[1]{0:T(128)} %bitcast.refs_0_.core_ref, f32[192,128]{1,0:T(8,128)S(1)} %add.53.refs_0_, f32[192,128]{1,0:T(8,128)S(1)} %collective-permute-done.13.refs_1_, f32[192,128]{1,0:T(8,128)S(1)} %slice.9.refs_2_, f32[768,256]{1,0:T(8,128)S(1)} %get-tuple-element.57.refs_3_, ...), custom_call_target="tpu_custom_call" | custom-call | flops 1000 | bytes 1000 | tf_op jit(solution)/shard_map/pallas_call | solution.py:235
  96.4 1.5 %shard_map.48.refs_1_ = f32[2,192,64]{2,1,0:T(8,128)S(1)} custom-call(s32[1]{0:T(128)} %bitcast.refs_0_.core_ref, bf16[384,6144]{1,0:T(8,128)(2,1)S(1)} %bitcast.10, bf16[384,6144]{1,0:T(8,128)(2,1)S(1)} %bitcast.12, f32[768,128]{1,0:T(8,128)S(1)} %get-tuple-element.90.refs_3_, f32[768,128]{1,0:T(8,128)S(1)} %get-tuple-element.87.refs_4_, ...), custom_call_target="tpu_custom_call" | custom-call | flops 1000 | bytes 1000 | tf_op jit(solution)/shard_map/pallas_call | solution.py:188
  100.5 3.4 %collective-permute-start.20 = (f32[96,128]{1,0:T(8,128)S(1)}, f32[96,128]{1,0:T(8,128)S(1)}, u32[]{:S(2)}, u32[]{:S(2)}) collective-permute-start(f32[96,128]{1,0:T(8,128)S(1)} %add.55), channel_id=1, source_target_pairs={{0,4},{1,5},{2,6},{3,7},{4,0},{5,1},{6,2},{7,3},{8,12},{9,13},{10,... | collective-permute-start | bytes 147464 | tf_op jit(solution)/shard_map/ppermute | solution.py:278
  103.9 2.1 %collective-permute-done.20 = f32[96,128]{1,0:T(8,128)S(1)} collective-permute-done((f32[96,128]{1,0:T(8,128)S(1)}, f32[96,128]{1,0:T(8,128)S(1)}, u32[]{:S(2)}, u32[]{:S(2)}) %collective-permute-start.20) | collective-permute-done | bytes 49184 | tf_op jit(solution)/shard_map/ppermute | solution.py:278
  107.1 1.7 %collective-permute-done.23.refs_4_.refs_9_ = f32[768,128]{1,0:T(8,128)S(1)} collective-permute-done((f32[768,128]{1,0:T(8,128)S(1)}, f32[768,128]{1,0:T(8,128)S(1)}, u32[]{:S(2)}, u32[]{:S(2)}) %collective-permute-start.23) | collective-permute-done | bytes 393248 | tf_op jit(solution)/shard_map/ppermute | solution.py:278
  111.6 3.2 %collective-permute-start.29 = (f32[96,128]{1,0:T(8,128)S(1)}, f32[96,128]{1,0:T(8,128)S(1)}, u32[]{:S(2)}, u32[]{:S(2)}) collective-permute-start(f32[96,128]{1,0:T(8,128)S(1)} %add.57), channel_id=1, source_target_pairs={{0,6},{1,7},{2,4},{3,5},{4,2},{5,3},{6,0},{7,1},{8,14},{9,15},{10,... | collective-permute-start | bytes 147464 | tf_op jit(solution)/shard_map/ppermute | solution.py:278
  116.1 2.9 %shard_map.51.part_ref = f32[2,192,6144]{2,1,0:T(8,128)S(1)} custom-call(s32[1]{0:T(128)} %bitcast.refs_0_.core_ref, f32[2,192,6144]{2,1,0:T(8,128)S(1)} %shard_map.45.refs_0_, f32[96,128]{1,0:T(8,128)S(1)} %add.56.refs_1_, f32[96,128]{1,0:T(8,128)S(1)} %collective-permute-done.24.refs_2_, ...), custom_call_target="tpu_custom_call", output_to_operand_aliasing={{}: (1, {})} | custom-call | flops 1000 | bytes 1000 | tf_op jit(solution)/shard_map/pallas_call | solution.py:235
  121.3 4.9 %shard_map.52 = f32[2,192,6144]{2,1,0:T(8,128)} custom-call(s32[1]{0:T(128)} %bitcast.refs_0_.core_ref, s32[8]{0:T(128)S(1)} %stack.35.order_ref, f32[2,192,6144]{2,1,0:T(8,128)S(1)} %shard_map.51.part_ref, f32[96,128]{1,0:T(8,128)S(1)} %add_add_fusion.refs_0_, f32[96,128]{1,0:T(8,128)S(1)} %collective-permute-done.30.refs_1_, ...), custom_call_target="tpu_custom_call" | custom-call | flops 1000 | bytes 1000 | tf_op jit(solution)/shard_map/pallas_call | solution.py:266
  (81 shorter events, 30.0 us)
Async XLA Ops:
  1.4 21.4 %collective-permute-start = (f32[768,256]{1,0:T(8,128)S(1)}, f32[768,256]{1,0:T(8,128)S(1)}, u32[]{:S(2)}, u32[]{:S(2)}) collective-permute-start(f32[768,256]{1,0:T(8,128)S(1)} %get-tuple-element.57.refs_3_), channel_id=1, source_target_pairs={{0,8},{8,0},{16,24},{24,16},{1,9},{9,1},{17,25},{25,17},{2,10},{10... | collective-permute-start | bytes 2359304 | tf_op jit(solution)/shard_map/ppermute | solution.py:278
  4.4 20.5 %collective-permute-start.1 = (f32[768,256]{1,0:T(8,128)S(1)}, f32[768,256]{1,0:T(8,128)S(1)}, u32[]{:S(2)}, u32[]{:S(2)}) collective-permute-start(f32[768,256]{1,0:T(8,128)S(1)} %get-tuple-element.58.refs_4_), channel_id=1, source_target_pairs={{0,16},{8,24},{16,0},{24,8},{1,17},{9,25},{17,1},{25,9},{2,18},{10... | collective-permute-start | bytes 2359304 | tf_op jit(solution)/shard_map/ppermute | solution.py:278
  6.0 33.8 %collective-permute-start.2 = (f32[768,256]{1,0:T(8,128)S(1)}, f32[768,256]{1,0:T(8,128)}, u32[]{:S(2)}, u32[]{:S(2)}) collective-permute-start(f32[768,256]{1,0:T(8,128)S(1)} %get-tuple-element.58.refs_4_), channel_id=1, source_target_pairs={{0,8},{8,0},{16,24},{24,16},{1,9},{9,1},{17,25},{25,17},{2,10},{10... | collective-permute-start | bytes 2359304 | tf_op jit(solution)/shard_map/ppermute | solution.py:278
  6.5 35.4 %collective-permute-start.3 = (f32[768,256]{1,0:T(8,128)S(1)}, f32[768,256]{1,0:T(8,128)}, u32[]{:S(2)}, u32[]{:S(2)}) collective-permute-start(f32[768,256]{1,0:T(8,128)S(1)} %get-tuple-element.57.refs_3_), channel_id=1, source_target_pairs={{0,16},{8,24},{16,0},{24,8},{1,17},{9,25},{17,1},{25,9},{2,18},{10... | collective-permute-start | bytes 2359304 | tf_op jit(solution)/shard_map/ppermute | solution.py:278
  24.9 33.8 %collective-permute-start.4 = (f32[768,256]{1,0:T(8,128)S(1)}, f32[768,256]{1,0:T(8,128)}, u32[]{:S(2)}, u32[]{:S(2)}) collective-permute-start(f32[768,256]{1,0:T(8,128)S(1)} %collective-permute-done.refs_5_), channel_id=1, source_target_pairs={{0,16},{8,24},{16,0},{24,8},{1,17},{9,25},{17,1},{25,9},{2,18},{10... | collective-permute-start | bytes 2359304 | tf_op jit(solution)/shard_map/ppermute | solution.py:278
  26.4 32.3 %collective-permute-start.5 = (f32[768,256]{1,0:T(8,128)S(1)}, f32[768,256]{1,0:T(8,128)}, u32[]{:S(2)}, u32[]{:S(2)}) collective-permute-start(f32[768,256]{1,0:T(8,128)S(1)} %collective-permute-done.1.refs_6_), channel_id=1, source_target_pairs={{0,8},{8,0},{16,24},{24,16},{1,9},{9,1},{17,25},{25,17},{2,10},{10... | collective-permute-start | bytes 2359304 | tf_op jit(solution)/shard_map/ppermute | solution.py:278
  44.3 20.4 %collective-permute-start.7 = (f32[768,128]{1,0:T(8,128)S(1)}, f32[768,128]{1,0:T(8,128)S(1)}, u32[]{:S(2)}, u32[]{:S(2)}) collective-permute-start(f32[768,128]{1,0:T(8,128)S(1)} %get-tuple-element.70.refs_3_.refs_4_), channel_id=1, source_target_pairs={{0,8},{8,0},{16,24},{24,16},{1,9},{9,1},{17,25},{25,17},{2,10},{10... | collective-permute-start | bytes 1179656 | tf_op jit(solution)/shard_map/ppermute | solution.py:278
  44.4 21.2 %collective-permute-start.8 = (f32[768,128]{1,0:T(8,128)S(1)}, f32[768,128]{1,0:T(8,128)S(1)}, u32[]{:S(2)}, u32[]{:S(2)}) collective-permute-start(f32[768,128]{1,0:T(8,128)S(1)} %copy-done.5), channel_id=1, source_target_pairs={{0,16},{8,24},{16,0},{24,8},{1,17},{9,25},{17,1},{25,9},{2,18},{10... | collective-permute-start | bytes 1179656 | tf_op jit(solution)/shard_map/ppermute | solution.py:278
  61.2 1.4 %collective-permute-start.6 = (f32[192,128]{1,0:T(8,128)S(1)}, f32[192,128]{1,0:T(8,128)S(1)}, u32[]{:S(2)}, u32[]{:S(2)}) collective-permute-start(f32[192,128]{1,0:T(8,128)S(1)} %get-tuple-element.62), channel_id=1, source_target_pairs={{0,1},{1,0},{2,3},{3,2},{4,5},{5,4},{6,7},{7,6},{8,9},{9,8},{10,11... | collective-permute-start | bytes 294920 | tf_op jit(solution)/shard_map/ppermute | solution.py:278
  62.6 12.0 %collective-permute-start.10 = (f32[768,128]{1,0:T(8,128)S(1)}, f32[768,128]{1,0:T(8,128)S(1)}, u32[]{:S(2)}, u32[]{:S(2)}) collective-permute-start(f32[768,128]{1,0:T(8,128)S(1)} %copy-done.5), channel_id=1, source_target_pairs={{0,8},{8,0},{16,24},{24,16},{1,9},{9,1},{17,25},{25,17},{2,10},{10... | collective-permute-start | bytes 1179656 | tf_op jit(solution)/shard_map/ppermute | solution.py:278
  62.7 12.0 %collective-permute-start.11 = (f32[768,128]{1,0:T(8,128)S(1)}, f32[768,128]{1,0:T(8,128)S(1)}, u32[]{:S(2)}, u32[]{:S(2)}) collective-permute-start(f32[768,128]{1,0:T(8,128)S(1)} %get-tuple-element.70.refs_3_.refs_4_), channel_id=1, source_target_pairs={{0,16},{8,24},{16,0},{24,8},{1,17},{9,25},{17,1},{25,9},{2,18},{10... | collective-permute-start | bytes 1179656 | tf_op jit(solution)/shard_map/ppermute | solution.py:278
  67.2 17.6 %collective-permute-start.14 = (f32[768,128]{1,0:T(8,128)S(1)}, f32[768,128]{1,0:T(8,128)S(1)}, u32[]{:S(2)}, u32[]{:S(2)}) collective-permute-start(f32[768,128]{1,0:T(8,128)S(1)} %collective-permute-done.7.refs_5_.refs_6_), channel_id=1, source_target_pairs={{0,16},{8,24},{16,0},{24,8},{1,17},{9,25},{17,1},{25,9},{2,18},{10... | collective-permute-start | bytes 1179656 | tf_op jit(solution)/shard_map/ppermute | solution.py:278
  68.7 4.6 %collective-permute-start.9 = (f32[192,128]{1,0:T(8,128)S(1)}, f32[192,128]{1,0:T(8,128)S(1)}, u32[]{:S(2)}, u32[]{:S(2)}) collective-permute-start(f32[192,128]{1,0:T(8,128)S(1)} %add.51), channel_id=1, source_target_pairs={{0,2},{1,3},{2,0},{3,1},{4,6},{5,7},{6,4},{7,5},{8,10},{9,11},{10,... | collective-permute-start | bytes 294920 | tf_op jit(solution)/shard_map/ppermute | solution.py:278
  70.3 14.5 %collective-permute-start.15 = (f32[768,128]{1,0:T(8,128)S(1)}, f32[768,128]{1,0:T(8,128)S(1)}, u32[]{:S(2)}, u32[]{:S(2)}) collective-permute-start(f32[768,128]{1,0:T(8,128)S(1)} %collective-permute-done.8.refs_6_.refs_7_), channel_id=1, source_target_pairs={{0,8},{8,0},{16,24},{24,16},{1,9},{9,1},{17,25},{25,17},{2,10},{10... | collective-permute-start | bytes 1179656 | tf_op jit(solution)/shard_map/ppermute | solution.py:278
  73.3 15.6 %copy-start.6 = (f32[192,256]{1,0:T(8,128)S(1)}, f32[192,256]{1,0:T(8,128)}, u32[]{:S(2)}) copy-start(f32[192,256]{1,0:T(8,128)} %param.5) | copy-start | bytes 589828
  75.6 20.8 %collective-permute-start.18 = (f32[768,128]{1,0:T(8,128)S(1)}, f32[768,128]{1,0:T(8,128)S(1)}, u32[]{:S(2)}, u32[]{:S(2)}) collective-permute-start(f32[768,128]{1,0:T(8,128)S(1)} %get-tuple-element.90.refs_3_), channel_id=1, source_target_pairs={{0,8},{8,0},{16,24},{24,16},{1,9},{9,1},{17,25},{25,17},{2,10},{10... | collective-permute-start | bytes 1179656 | tf_op jit(solution)/shard_map/ppermute | solution.py:278
  77.6 18.7 %collective-permute-start.19 = (f32[768,128]{1,0:T(8,128)S(1)}, f32[768,128]{1,0:T(8,128)S(1)}, u32[]{:S(2)}, u32[]{:S(2)}) collective-permute-start(f32[768,128]{1,0:T(8,128)S(1)} %get-tuple-element.87.refs_4_), channel_id=1, source_target_pairs={{0,16},{8,24},{16,0},{24,8},{1,17},{9,25},{17,1},{25,9},{2,18},{10... | collective-permute-start | bytes 1179656 | tf_op jit(solution)/shard_map/ppermute | solution.py:278
  79.2 5.5 %collective-permute-start.12 = (f32[192,128]{1,0:T(8,128)S(1)}, f32[192,128]{1,0:T(8,128)S(1)}, u32[]{:S(2)}, u32[]{:S(2)}) collective-permute-start(f32[192,128]{1,0:T(8,128)S(1)} %add.52), channel_id=1, source_target_pairs={{0,4},{1,5},{2,6},{3,7},{4,0},{5,1},{6,2},{7,3},{8,12},{9,13},{10,... | collective-permute-start | bytes 294920 | tf_op jit(solution)/shard_map/ppermute | solution.py:278
  84.7 4.8 %collective-permute-start.13 = (f32[192,128]{1,0:T(8,128)S(1)}, f32[192,128]{1,0:T(8,128)S(1)}, u32[]{:S(2)}, u32[]{:S(2)}) collective-permute-start(f32[192,128]{1,0:T(8,128)S(1)} %add.53.refs_0_), channel_id=1, source_target_pairs={{0,1},{1,0},{2,3},{3,2},{4,5},{5,4},{6,7},{7,6},{8,9},{9,8},{10,11... | collective-permute-start | bytes 294920 | tf_op jit(solution)/shard_map/ppermute | solution.py:278
  85.8 1.4 %collective-permute-start.16 = (f32[96,128]{1,0:T(8,128)S(1)}, f32[96,128]{1,0:T(8,128)S(1)}, u32[]{:S(2)}, u32[]{:S(2)}) collective-permute-start(f32[96,128]{1,0:T(8,128)S(1)} %get-tuple-element.78), channel_id=1, source_target_pairs={{0,1},{1,0},{2,3},{3,2},{4,5},{5,4},{6,7},{7,6},{8,9},{9,8},{10,11... | collective-permute-start | bytes 147464 | tf_op jit(solution)/shard_map/ppermute | solution.py:278
  87.2 9.1 %collective-permute-start.17 = (f32[96,128]{1,0:T(8,128)S(1)}, f32[96,128]{1,0:T(8,128)S(1)}, u32[]{:S(2)}, u32[]{:S(2)}) collective-permute-start(f32[96,128]{1,0:T(8,128)S(1)} %add.54), channel_id=1, source_target_pairs={{0,2},{1,3},{2,0},{3,1},{4,6},{5,7},{6,4},{7,5},{8,10},{9,11},{10,... | collective-permute-start | bytes 147464 | tf_op jit(solution)/shard_map/ppermute | solution.py:278
  88.9 17.2 %collective-permute-start.21 = (f32[768,128]{1,0:T(8,128)S(1)}, f32[768,128]{1,0:T(8,128)S(1)}, u32[]{:S(2)}, u32[]{:S(2)}) collective-permute-start(f32[768,128]{1,0:T(8,128)S(1)} %get-tuple-element.87.refs_4_), channel_id=1, source_target_pairs={{0,8},{8,0},{16,24},{24,16},{1,9},{9,1},{17,25},{25,17},{2,10},{10... | collective-permute-start | bytes 1179656 | tf_op jit(solution)/shard_map/ppermute | solution.py:278
  89.6 16.7 %collective-permute-start.22 = (f32[768,128]{1,0:T(8,128)S(1)}, f32[768,128]{1,0:T(8,128)S(1)}, u32[]{:S(2)}, u32[]{:S(2)}) collective-permute-start(f32[768,128]{1,0:T(8,128)S(1)} %get-tuple-element.90.refs_3_), channel_id=1, source_target_pairs={{0,16},{8,24},{16,0},{24,8},{1,17},{9,25},{17,1},{25,9},{2,18},{10... | collective-permute-start | bytes 1179656 | tf_op jit(solution)/shard_map/ppermute | solution.py:278
  98.0 10.9 %collective-permute-start.23 = (f32[768,128]{1,0:T(8,128)S(1)}, f32[768,128]{1,0:T(8,128)S(1)}, u32[]{:S(2)}, u32[]{:S(2)}) collective-permute-start(f32[768,128]{1,0:T(8,128)S(1)} %collective-permute-done.18.refs_5_), channel_id=1, source_target_pairs={{0,16},{8,24},{16,0},{24,8},{1,17},{9,25},{17,1},{25,9},{2,18},{10... | collective-permute-start | bytes 1179656 | tf_op jit(solution)/shard_map/ppermute | solution.py:278
  99.0 10.3 %collective-permute-start.25 = (f32[768,128]{1,0:T(8,128)S(1)}, f32[768,128]{1,0:T(8,128)S(1)}, u32[]{:S(2)}, u32[]{:S(2)}) collective-permute-start(f32[768,128]{1,0:T(8,128)S(1)} %collective-permute-done.19.refs_6_), channel_id=1, source_target_pairs={{0,8},{8,0},{16,24},{24,16},{1,9},{9,1},{17,25},{25,17},{2,10},{10... | collective-permute-start | bytes 1179656 | tf_op jit(solution)/shard_map/ppermute | solution.py:278
  100.5 5.4 %collective-permute-start.20 = (f32[96,128]{1,0:T(8,128)S(1)}, f32[96,128]{1,0:T(8,128)S(1)}, u32[]{:S(2)}, u32[]{:S(2)}) collective-permute-start(f32[96,128]{1,0:T(8,128)S(1)} %add.55), channel_id=1, source_target_pairs={{0,4},{1,5},{2,6},{3,7},{4,0},{5,1},{6,2},{7,3},{8,12},{9,13},{10,... | collective-permute-start | bytes 147464 | tf_op jit(solution)/shard_map/ppermute | solution.py:278
  105.9 2.9 %collective-permute-start.24 = (f32[96,128]{1,0:T(8,128)S(1)}, f32[96,128]{1,0:T(8,128)S(1)}, u32[]{:S(2)}, u32[]{:S(2)}) collective-permute-start(f32[96,128]{1,0:T(8,128)S(1)} %add.56.refs_1_), channel_id=1, source_target_pairs={{0,1},{1,0},{2,3},{3,2},{4,5},{5,4},{6,7},{7,6},{8,9},{9,8},{10,11... | collective-permute-start | bytes 147464 | tf_op jit(solution)/shard_map/ppermute | solution.py:278
  110.3 1.3 %collective-permute-start.26 = (f32[96,128]{1,0:T(8,128)S(1)}, f32[96,128]{1,0:T(8,128)S(1)}, u32[]{:S(2)}, u32[]{:S(2)}) collective-permute-start(f32[96,128]{1,0:T(8,128)S(1)} %get-tuple-element.100), channel_id=1, source_target_pairs={{0,1},{1,0},{2,3},{3,2},{4,5},{5,4},{6,7},{7,6},{8,9},{9,8},{10,11... | collective-permute-start | bytes 147464 | tf_op jit(solution)/shard_map/ppermute | solution.py:278
  111.6 7.4 %collective-permute-start.29 = (f32[96,128]{1,0:T(8,128)S(1)}, f32[96,128]{1,0:T(8,128)S(1)}, u32[]{:S(2)}, u32[]{:S(2)}) collective-permute-start(f32[96,128]{1,0:T(8,128)S(1)} %add.57), channel_id=1, source_target_pairs={{0,6},{1,7},{2,4},{3,5},{4,2},{5,3},{6,0},{7,1},{8,14},{9,15},{10,... | collective-permute-start | bytes 147464 | tf_op jit(solution)/shard_map/ppermute | solution.py:278
  114.7 5.2 %collective-permute-start.28 = (f32[96,128]{1,0:T(8,128)S(1)}, f32[96,128]{1,0:T(8,128)S(1)}, u32[]{:S(2)}, u32[]{:S(2)}) collective-permute-start(f32[96,128]{1,0:T(8,128)S(1)} %add.57), channel_id=1, source_target_pairs={{0,4},{1,5},{2,6},{3,7},{4,0},{5,1},{6,2},{7,3},{8,12},{9,13},{10,... | collective-permute-start | bytes 147464 | tf_op jit(solution)/shard_map/ppermute | solution.py:278
  115.1 4.9 %collective-permute-start.27 = (f32[96,128]{1,0:T(8,128)S(1)}, f32[96,128]{1,0:T(8,128)S(1)}, u32[]{:S(2)}, u32[]{:S(2)}) collective-permute-start(f32[96,128]{1,0:T(8,128)S(1)} %add.57), channel_id=1, source_target_pairs={{0,2},{1,3},{2,0},{3,1},{4,6},{5,7},{6,4},{7,5},{8,10},{9,11},{10,... | collective-permute-start | bytes 147464 | tf_op jit(solution)/shard_map/ppermute | solution.py:278
  120.0 1.3 %collective-permute-start.30 = (f32[96,128]{1,0:T(8,128)S(1)}, f32[96,128]{1,0:T(8,128)S(1)}, u32[]{:S(2)}, u32[]{:S(2)}) collective-permute-start(f32[96,128]{1,0:T(8,128)S(1)} %add_add_fusion.refs_0_), channel_id=1, source_target_pairs={{0,1},{1,0},{2,3},{3,2},{4,5},{5,4},{6,7},{7,6},{8,9},{9,8},{10,11... | collective-permute-start | bytes 147464 | tf_op jit(solution)/shard_map/ppermute | solution.py:278
  (10 other events, 56.4 us)

commit v2 on v1

--- a/solution.py
+++ b/solution.py
@@ -334,22 +334,23 @@
             if not last:
                 near_total = fields(chunk, near, 0)
                 total = in_order(total, near_total)
-            arrived = mode_exchange(total, mode_size, bits[0])
-            if part is not None:
-                arrived = in_order(arrived, part)
-            total = total + arrived
+            total = total + mode_exchange(total, mode_size, bits[0])
             if last:
                 tied(chunk, near[2:], total)
                 near_total = fields(chunk, near, 0)
         else:
             near_total = fields(chunk, near, 0)
-        send(chunk, 2, *([near_total] if c else matrix), *([] if part is None else [part]))
+        send(chunk, 2, *([] if last else [near_total] if c else matrix))
         if c:
             tied(chunk, side, total)
             if last:
+                if cut:
+                    before = in_order(sums[0][0], near_total), *sums[0][1:]
+                    part = gradient_part(core, before, [chunks[0][place] for place in places], count)
                 total = in_order(total, near_total)
                 for mask in bits[1:]:
-                    total = total + mode_exchange(total, mode_size, mask)
+                    arrived = mode_exchange(total, mode_size, mask)
+                    total = total + (in_order(arrived, part) if cut else arrived)
                 tied(chunk, side, total)
         side_total = fields(chunk, side, len(near), total=near_total)
         if c:
@@ -362,8 +363,6 @@
             if last:
                 tied(chunk, far, other)
             sums[-1] = total, other, intensity[:, slice(*spans[c - 1])]
-        if c == 1 and cut:
-            part = gradient_part(core, sums[0], [chunks[0][place] for place in places], count)
         kept, sent = fields(chunk, far, len(near + side), total=side_total, last=True)
         waits = [side_total, *(chunks[c + 1][place] for place in near[:2])] if not last else []
         sums.append(kept + mode_exchange(sent, mode_size, 1))

time: 127 us -> 126 us (level)
  transfers between devices with their start and end apart: 31 -> 31, of which waited for: 18 -> 16; matrix products, arithmetic and copies ran while one was open for 0% -> 0% of each run, Pallas kernels for 25% -> 25%
where the time goes in v2:
time: 126 us; the launch traced here: 125 us
  waiting for transfers between devices  40.4 us (32%)
  Pallas kernels  39.1 us (31%)
  starting transfers between devices  35.4 us (28%)
  local copies, waits for them, and re-layouts  9.99 us (8%)
    ppermute x31, waiting for transfers between devices, exchange(): return lax.ppermute(value, axis, [(i, i ^ mask) for i in range(size)])  40.4 us
    ppermute x31, starting transfers between devices, exchange(): return lax.ppermute(value, axis, [(i, i ^ mask) for i in range(size)])  35.4 us
    pallas_call x9, Pallas kernels, add_fields(): pl.pallas_call(functools.partial(fields_kernel, first, widths, total is n...  13.7 us
    unnamed x22, local copies, waits for them, and re-layouts  9.82 us
    pallas_call x2, Pallas kernels, gradient_part(): pl.pallas_call(functools.partial(part_kernel, 1.0 / count, part is not No...  8.78 us
    pallas_call x1, Pallas kernels, matrix_halves(): pl.pallas_call(matrix_kernel, grid_spec=pltpu.PrefetchScalarGridSpec(num_...  7.24 us
    pallas_call x1, Pallas kernels, last_gradient(): pl.pallas_call(functools.partial(last_kernel, 1.0 / count), in_specs=[SME...  4.94 us
    pallas_call x3, Pallas kernels, probe_chunk(): pl.pallas_call(functools.partial(chunk_kernel, low, high), in_specs=[pl.B...  4.45 us
  transfers between devices with their start and end apart: 31, of which 16 were waited for; matrix products, arithmetic and copies ran while one was open for 0% of the time, Pallas kernels for 25%

profile of v2, /device:TPU:0, one launch (start us, length us, event | category | flops | bytes accessed | tf_op | source)
XLA Modules:
  0.0 125.5 jit_solution(5496128858045986359)
XLA Ops:
  1.4 3.0 %collective-permute-start = (f32[768,256]{1,0:T(8,128)S(1)}, f32[768,256]{1,0:T(8,128)S(1)}, u32[]{:S(2)}, u32[]{:S(2)}) collective-permute-start(f32[768,256]{1,0:T(8,128)S(1)} %get-tuple-element.58.refs_3_), channel_id=1, source_target_pairs={{0,8},{8,0},{16,24},{24,16},{1,9},{9,1},{17,25},{25,17},{2,10},{10... | collective-permute-start | bytes 2359304 | tf_op jit(solution)/shard_map/ppermute | solution.py:278
  6.6 7.2 %shard_map.37 = (bf16[384,6144]{1,0:T(8,128)(2,1)S(1)}, bf16[384,6144]{1,0:T(8,128)(2,1)S(1)}) custom-call(s32[8]{0:T(128)S(1)} %stack.35.order_ref, f32[2,192,6144]{2,1,0:T(8,128)} %matrix_ref.1), custom_call_target="tpu_custom_call" | custom-call | flops 1000 | bytes 1000 | tf_op jit(solution)/shard_map/pallas_call | solution.py:104
  13.9 2.2 %copy-done = bf16[384,6144]{1,0:T(8,128)(2,1)} copy-done((bf16[384,6144]{1,0:T(8,128)(2,1)}, bf16[384,6144]{1,0:T(8,128)(2,1)S(1)}, u32[]{:S(2)}) %copy-start) | copy-done | bytes 4718616
  16.1 2.2 %copy-done.2 = bf16[384,6144]{1,0:T(8,128)(2,1)} copy-done((bf16[384,6144]{1,0:T(8,128)(2,1)}, bf16[384,6144]{1,0:T(8,128)(2,1)S(1)}, u32[]{:S(2)}) %copy-start.2) | copy-done | bytes 4718616
  18.2 4.6 %collective-permute-done.refs_5_ = f32[768,256]{1,0:T(8,128)S(1)} collective-permute-done((f32[768,256]{1,0:T(8,128)S(1)}, f32[768,256]{1,0:T(8,128)S(1)}, u32[]{:S(2)}, u32[]{:S(2)}) %collective-permute-start) | collective-permute-done | bytes 786464 | tf_op jit(solution)/shard_map/ppermute | solution.py:278
  22.8 2.1 %collective-permute-done.1.refs_6_ = f32[768,256]{1,0:T(8,128)S(1)} collective-permute-done((f32[768,256]{1,0:T(8,128)S(1)}, f32[768,256]{1,0:T(8,128)S(1)}, u32[]{:S(2)}, u32[]{:S(2)}) %collective-permute-start.1) | collective-permute-done | bytes 786464 | tf_op jit(solution)/shard_map/ppermute | solution.py:278
  27.0 1.6 %shard_map.42 = (f32[768,128]{1,0:T(8,128)S(1)}, f32[768,128]{1,0:T(8,128)S(1)}) custom-call(f32[2,1536,256]{2,1,0:T(8,128)} %probes_ref.5), custom_call_target="tpu_custom_call" | custom-call | flops 1000 | bytes 1000 | tf_op jit(solution)/shard_map/pallas_call | solution.py:81
  29.3 2.3 %copy-done.1 = bf16[384,6144]{1,0:T(8,128)(2,1)S(1)} copy-done((bf16[384,6144]{1,0:T(8,128)(2,1)S(1)}, bf16[384,6144]{1,0:T(8,128)(2,1)}, u32[]{:S(2)}) %copy-start.1) | copy-done | bytes 4718616
  31.6 2.3 %copy-done.3 = bf16[384,6144]{1,0:T(8,128)(2,1)S(1)} copy-done((bf16[384,6144]{1,0:T(8,128)(2,1)S(1)}, bf16[384,6144]{1,0:T(8,128)(2,1)}, u32[]{:S(2)}) %copy-start.3) | copy-done | bytes 4718616
  34.0 2.0 %shard_map.39.refs_1_ = f32[2,192,128]{2,1,0:T(8,128)S(1)} custom-call(s32[1]{0:T(128)} %bitcast.refs_0_.core_ref, bf16[384,6144]{1,0:T(8,128)(2,1)S(1)} %copy-done.1, bf16[384,6144]{1,0:T(8,128)(2,1)S(1)} %copy-done.3, f32[768,256]{1,0:T(8,128)S(1)} %get-tuple-element.58.refs_3_, f32[768,256]{1,0:T(8,128)S(1)} %get-tuple-element.59.refs_4_, ...), custom_call_target="tpu_custom_call" | custom-call | flops 1000 | bytes 1000 | tf_op jit(solution)/shard_map/pallas_call | solution.py:188
  36.0 3.8 %collective-permute-done.2.refs_4_.refs_7_ = f32[768,256]{1,0:T(8,128)} collective-permute-done((f32[768,256]{1,0:T(8,128)S(1)}, f32[768,256]{1,0:T(8,128)}, u32[]{:S(2)}, u32[]{:S(2)}) %collective-permute-start.2) | collective-permute-done | bytes 786464 | tf_op jit(solution)/shard_map/ppermute | solution.py:278
  39.8 2.1 %collective-permute-done.3.refs_5_.refs_8_ = f32[768,256]{1,0:T(8,128)} collective-permute-done((f32[768,256]{1,0:T(8,128)S(1)}, f32[768,256]{1,0:T(8,128)}, u32[]{:S(2)}, u32[]{:S(2)}) %collective-permute-start.3) | collective-permute-done | bytes 786464 | tf_op jit(solution)/shard_map/ppermute | solution.py:278
  41.9 2.5 %shard_map.40.refs_1_ = f32[2,192,128]{2,1,0:T(8,128)S(1)} custom-call(s32[1]{0:T(128)} %bitcast.refs_0_.core_ref, f32[2,192,128]{2,1,0:T(8,128)S(1)} %shard_map.39.refs_1_, bf16[384,6144]{1,0:T(8,128)(2,1)S(1)} %copy-done.1, bf16[384,6144]{1,0:T(8,128)(2,1)S(1)} %copy-done.3, f32[768,256]{1,0:T(8,128)} %collective-permute-done.2.refs_4_.refs_7_, ...), custom_call_target="tpu_custom_call" | custom-call | flops 1000 | bytes 1000 | tf_op jit(solution)/shard_map/pallas_call | solution.py:188
  44.4 2.0 %collective-permute-start.8 = (f32[768,128]{1,0:T(8,128)S(1)}, f32[768,128]{1,0:T(8,128)S(1)}, u32[]{:S(2)}, u32[]{:S(2)}) collective-permute-start(f32[768,128]{1,0:T(8,128)S(1)} %copy-done.5), channel_id=1, source_target_pairs={{0,16},{8,24},{16,0},{24,8},{1,17},{9,25},{17,1},{25,9},{2,18},{10... | collective-permute-start | bytes 1179656 | tf_op jit(solution)/shard_map/ppermute | solution.py:278
  46.4 12.3 %collective-permute-done.4.refs_4_.refs_9_ = f32[768,256]{1,0:T(8,128)} collective-permute-done((f32[768,256]{1,0:T(8,128)S(1)}, f32[768,256]{1,0:T(8,128)}, u32[]{:S(2)}, u32[]{:S(2)}) %collective-permute-start.4) | collective-permute-done | bytes 786464 | tf_op jit(solution)/shard_map/ppermute | solution.py:278
  58.7 2.5 %shard_map.41 = (f32[192,128]{1,0:T(8,128)S(1)}, f32[192,128]{1,0:T(8,128)S(1)}) custom-call(s32[1]{0:T(128)} %bitcast.refs_0_.core_ref, f32[2,192,128]{2,1,0:T(8,128)S(1)} %shard_map.40.refs_1_, bf16[384,6144]{1,0:T(8,128)(2,1)S(1)} %copy-done.1, bf16[384,6144]{1,0:T(8,128)(2,1)S(1)} %copy-done.3, f32[768,256]{1,0:T(8,128)} %collective-permute-done.4.refs_4_.refs_9_, ...), custom_call_target="tpu_custom_call" | custom-call | flops 1000 | bytes 1000 | tf_op jit(solution)/shard_map/pallas_call | solution.py:188
  62.7 2.0 %collective-permute-start.11 = (f32[768,128]{1,0:T(8,128)S(1)}, f32[768,128]{1,0:T(8,128)S(1)}, u32[]{:S(2)}, u32[]{:S(2)}) collective-permute-start(f32[768,128]{1,0:T(8,128)S(1)} %get-tuple-element.71.refs_3_.refs_4_), channel_id=1, source_target_pairs={{0,16},{8,24},{16,0},{24,8},{1,17},{9,25},{17,1},{25,9},{2,18},{10... | collective-permute-start | bytes 1179656 | tf_op jit(solution)/shard_map/ppermute | solution.py:278
  65.6 1.5 %shard_map.43.refs_1_ = f32[2,192,64]{2,1,0:T(8,128)S(1)} custom-call(s32[1]{0:T(128)} %bitcast.refs_0_.core_ref, bf16[384,6144]{1,0:T(8,128)(2,1)S(1)} %copy-done.1, bf16[384,6144]{1,0:T(8,128)(2,1)S(1)} %copy-done.3, f32[768,128]{1,0:T(8,128)S(1)} %get-tuple-element.71.refs_3_.refs_4_, f32[768,128]{1,0:T(8,128)S(1)} %copy-done.5, ...), custom_call_target="tpu_custom_call" | custom-call | flops 1000 | bytes 1000 | tf_op jit(solution)/shard_map/pallas_call | solution.py:188
  67.2 1.6 %collective-permute-start.9 = (f32[192,128]{1,0:T(8,128)S(1)}, f32[192,128]{1,0:T(8,128)S(1)}, u32[]{:S(2)}, u32[]{:S(2)}) collective-permute-start(f32[192,128]{1,0:T(8,128)S(1)} %add.51), channel_id=1, source_target_pairs={{0,2},{1,3},{2,0},{3,1},{4,6},{5,7},{6,4},{7,5},{8,10},{9,11},{10,... | collective-permute-start | bytes 294920 | tf_op jit(solution)/shard_map/ppermute | solution.py:278
  72.3 2.3 %collective-permute-done.10.refs_4_.refs_8_ = f32[768,128]{1,0:T(8,128)S(1)} collective-permute-done((f32[768,128]{1,0:T(8,128)S(1)}, f32[768,128]{1,0:T(8,128)S(1)}, u32[]{:S(2)}, u32[]{:S(2)}) %collective-permute-start.10) | collective-permute-done | bytes 393248 | tf_op jit(solution)/shard_map/ppermute | solution.py:278
  75.6 2.1 %collective-permute-start.13 = (f32[768,128]{1,0:T(8,128)S(1)}, f32[768,128]{1,0:T(8,128)S(1)}, u32[]{:S(2)}, u32[]{:S(2)}) collective-permute-start(f32[768,128]{1,0:T(8,128)S(1)} %get-tuple-element.92.refs_3_), channel_id=1, source_target_pairs={{0,8},{8,0},{16,24},{24,16},{1,9},{9,1},{17,25},{25,17},{2,10},{10... | collective-permute-start | bytes 1179656 | tf_op jit(solution)/shard_map/ppermute | solution.py:278
  79.2 2.6 %collective-permute-start.12 = (f32[192,128]{1,0:T(8,128)S(1)}, f32[192,128]{1,0:T(8,128)S(1)}, u32[]{:S(2)}, u32[]{:S(2)}) collective-permute-start(f32[192,128]{1,0:T(8,128)S(1)} %add.52), channel_id=1, source_target_pairs={{0,4},{1,5},{2,6},{3,7},{4,0},{5,1},{6,2},{7,3},{8,12},{9,13},{10,... | collective-permute-start | bytes 294920 | tf_op jit(solution)/shard_map/ppermute | solution.py:278
  81.8 2.9 %collective-permute-done.12 = f32[192,128]{1,0:T(8,128)S(1)} collective-permute-done((f32[192,128]{1,0:T(8,128)S(1)}, f32[192,128]{1,0:T(8,128)S(1)}, u32[]{:S(2)}, u32[]{:S(2)}) %collective-permute-start.12) | collective-permute-done | bytes 98336 | tf_op jit(solution)/shard_map/ppermute | solution.py:278
  87.0 1.8 %collective-permute-start.17 = (f32[96,128]{1,0:T(8,128)S(1)}, f32[96,128]{1,0:T(8,128)S(1)}, u32[]{:S(2)}, u32[]{:S(2)}) collective-permute-start(f32[96,128]{1,0:T(8,128)S(1)} %add.54), channel_id=1, source_target_pairs={{0,2},{1,3},{2,0},{3,1},{4,6},{5,7},{6,4},{7,5},{8,10},{9,11},{10,... | collective-permute-start | bytes 147464 | tf_op jit(solution)/shard_map/ppermute | solution.py:278
  92.6 1.7 %collective-permute-start.25 = (f32[768,128]{1,0:T(8,128)S(1)}, f32[768,128]{1,0:T(8,128)S(1)}, u32[]{:S(2)}, u32[]{:S(2)}) collective-permute-start(f32[768,128]{1,0:T(8,128)S(1)} %collective-permute-done.18.refs_6_), channel_id=1, source_target_pairs={{0,8},{8,0},{16,24},{24,16},{1,9},{9,1},{17,25},{25,17},{2,10},{10... | collective-permute-start | bytes 1179656 | tf_op jit(solution)/shard_map/ppermute | solution.py:278
  94.3 1.5 %shard_map.47.refs_1_ = f32[2,192,64]{2,1,0:T(8,128)S(1)} custom-call(s32[1]{0:T(128)} %bitcast.refs_0_.core_ref, bf16[384,6144]{1,0:T(8,128)(2,1)S(1)} %copy-done.1, bf16[384,6144]{1,0:T(8,128)(2,1)S(1)} %copy-done.3, f32[768,128]{1,0:T(8,128)S(1)} %get-tuple-element.92.refs_3_, f32[768,128]{1,0:T(8,128)S(1)} %get-tuple-element.89.refs_4_, ...), custom_call_target="tpu_custom_call" | custom-call | flops 1000 | bytes 1000 | tf_op jit(solution)/shard_map/pallas_call | solution.py:188
  95.9 2.2 %collective-permute-start.20 = (f32[96,128]{1,0:T(8,128)S(1)}, f32[96,128]{1,0:T(8,128)S(1)}, u32[]{:S(2)}, u32[]{:S(2)}) collective-permute-start(f32[96,128]{1,0:T(8,128)S(1)} %add.55), channel_id=1, source_target_pairs={{0,4},{1,5},{2,6},{3,7},{4,0},{5,1},{6,2},{7,3},{8,12},{9,13},{10,... | collective-permute-start | bytes 147464 | tf_op jit(solution)/shard_map/ppermute | solution.py:278
  98.2 5.9 %shard_map.48.refs_0_ = f32[2,192,6144]{2,1,0:T(8,128)S(1)} custom-call(s32[1]{0:T(128)} %bitcast.refs_0_.core_ref, f32[192,128]{1,0:T(8,128)S(1)} %add.53.refs_0_, f32[192,128]{1,0:T(8,128)S(1)} %collective-permute-done.19.refs_1_, f32[192,128]{1,0:T(8,128)S(1)} %slice.9.refs_2_, f32[768,256]{1,0:T(8,128)S(1)} %get-tuple-element.58.refs_3_, ...), custom_call_target="tpu_custom_call" | custom-call | flops 1000 | bytes 1000 | tf_op jit(solution)/shard_map/pallas_call | solution.py:235
  105.7 2.6 %collective-permute-done.23.refs_4_.refs_9_ = f32[768,128]{1,0:T(8,128)S(1)} collective-permute-done((f32[768,128]{1,0:T(8,128)S(1)}, f32[768,128]{1,0:T(8,128)S(1)}, u32[]{:S(2)}, u32[]{:S(2)}) %collective-permute-start.23) | collective-permute-done | bytes 393248 | tf_op jit(solution)/shard_map/ppermute | solution.py:278
  110.5 3.2 %collective-permute-start.29 = (f32[96,128]{1,0:T(8,128)S(1)}, f32[96,128]{1,0:T(8,128)S(1)}, u32[]{:S(2)}, u32[]{:S(2)}) collective-permute-start(f32[96,128]{1,0:T(8,128)S(1)} %add.57), channel_id=1, source_target_pairs={{0,6},{1,7},{2,4},{3,5},{4,2},{5,3},{6,0},{7,1},{8,14},{9,15},{10,... | collective-permute-start | bytes 147464 | tf_op jit(solution)/shard_map/ppermute | solution.py:278
  115.1 2.9 %shard_map.51.part_ref = f32[2,192,6144]{2,1,0:T(8,128)S(1)} custom-call(s32[1]{0:T(128)} %bitcast.refs_0_.core_ref, f32[2,192,6144]{2,1,0:T(8,128)S(1)} %shard_map.48.refs_0_, f32[96,128]{1,0:T(8,128)S(1)} %add.56.refs_1_, f32[96,128]{1,0:T(8,128)S(1)} %collective-permute-done.24.refs_2_, ...), custom_call_target="tpu_custom_call", output_to_operand_aliasing={{}: (1, {})} | custom-call | flops 1000 | bytes 1000 | tf_op jit(solution)/shard_map/pallas_call | solution.py:235
  120.4 4.9 %shard_map.52 = f32[2,192,6144]{2,1,0:T(8,128)} custom-call(s32[1]{0:T(128)} %bitcast.refs_0_.core_ref, s32[8]{0:T(128)S(1)} %stack.35.order_ref, f32[2,192,6144]{2,1,0:T(8,128)S(1)} %shard_map.51.part_ref, f32[96,128]{1,0:T(8,128)S(1)} %add_add_fusion.refs_0_, f32[96,128]{1,0:T(8,128)S(1)} %collective-permute-done.30.refs_1_, ...), custom_call_target="tpu_custom_call" | custom-call | flops 1000 | bytes 1000 | tf_op jit(solution)/shard_map/pallas_call | solution.py:266
  (81 shorter events, 28.6 us)
Async XLA Ops:
  1.4 21.4 %collective-permute-start = (f32[768,256]{1,0:T(8,128)S(1)}, f32[768,256]{1,0:T(8,128)S(1)}, u32[]{:S(2)}, u32[]{:S(2)}) collective-permute-start(f32[768,256]{1,0:T(8,128)S(1)} %get-tuple-element.58.refs_3_), channel_id=1, source_target_pairs={{0,8},{8,0},{16,24},{24,16},{1,9},{9,1},{17,25},{25,17},{2,10},{10... | collective-permute-start | bytes 2359304 | tf_op jit(solution)/shard_map/ppermute | solution.py:278
  4.4 20.5 %collective-permute-start.1 = (f32[768,256]{1,0:T(8,128)S(1)}, f32[768,256]{1,0:T(8,128)S(1)}, u32[]{:S(2)}, u32[]{:S(2)}) collective-permute-start(f32[768,256]{1,0:T(8,128)S(1)} %get-tuple-element.59.refs_4_), channel_id=1, source_target_pairs={{0,16},{8,24},{16,0},{24,8},{1,17},{9,25},{17,1},{25,9},{2,18},{10... | collective-permute-start | bytes 2359304 | tf_op jit(solution)/shard_map/ppermute | solution.py:278
  6.0 33.8 %collective-permute-start.2 = (f32[768,256]{1,0:T(8,128)S(1)}, f32[768,256]{1,0:T(8,128)}, u32[]{:S(2)}, u32[]{:S(2)}) collective-permute-start(f32[768,256]{1,0:T(8,128)S(1)} %get-tuple-element.59.refs_4_), channel_id=1, source_target_pairs={{0,8},{8,0},{16,24},{24,16},{1,9},{9,1},{17,25},{25,17},{2,10},{10... | collective-permute-start | bytes 2359304 | tf_op jit(solution)/shard_map/ppermute | solution.py:278
  6.5 35.4 %collective-permute-start.3 = (f32[768,256]{1,0:T(8,128)S(1)}, f32[768,256]{1,0:T(8,128)}, u32[]{:S(2)}, u32[]{:S(2)}) collective-permute-start(f32[768,256]{1,0:T(8,128)S(1)} %get-tuple-element.58.refs_3_), channel_id=1, source_target_pairs={{0,16},{8,24},{16,0},{24,8},{1,17},{9,25},{17,1},{25,9},{2,18},{10... | collective-permute-start | bytes 2359304 | tf_op jit(solution)/shard_map/ppermute | solution.py:278
  24.9 33.8 %collective-permute-start.4 = (f32[768,256]{1,0:T(8,128)S(1)}, f32[768,256]{1,0:T(8,128)}, u32[]{:S(2)}, u32[]{:S(2)}) collective-permute-start(f32[768,256]{1,0:T(8,128)S(1)} %collective-permute-done.refs_5_), channel_id=1, source_target_pairs={{0,16},{8,24},{16,0},{24,8},{1,17},{9,25},{17,1},{25,9},{2,18},{10... | collective-permute-start | bytes 2359304 | tf_op jit(solution)/shard_map/ppermute | solution.py:278
  26.4 32.3 %collective-permute-start.5 = (f32[768,256]{1,0:T(8,128)S(1)}, f32[768,256]{1,0:T(8,128)}, u32[]{:S(2)}, u32[]{:S(2)}) collective-permute-start(f32[768,256]{1,0:T(8,128)S(1)} %collective-permute-done.1.refs_6_), channel_id=1, source_target_pairs={{0,8},{8,0},{16,24},{24,16},{1,9},{9,1},{17,25},{25,17},{2,10},{10... | collective-permute-start | bytes 2359304 | tf_op jit(solution)/shard_map/ppermute | solution.py:278
  44.3 20.4 %collective-permute-start.7 = (f32[768,128]{1,0:T(8,128)S(1)}, f32[768,128]{1,0:T(8,128)S(1)}, u32[]{:S(2)}, u32[]{:S(2)}) collective-permute-start(f32[768,128]{1,0:T(8,128)S(1)} %get-tuple-element.71.refs_3_.refs_4_), channel_id=1, source_target_pairs={{0,8},{8,0},{16,24},{24,16},{1,9},{9,1},{17,25},{25,17},{2,10},{10... | collective-permute-start | bytes 1179656 | tf_op jit(solution)/shard_map/ppermute | solution.py:278
  44.4 21.2 %collective-permute-start.8 = (f32[768,128]{1,0:T(8,128)S(1)}, f32[768,128]{1,0:T(8,128)S(1)}, u32[]{:S(2)}, u32[]{:S(2)}) collective-permute-start(f32[768,128]{1,0:T(8,128)S(1)} %copy-done.5), channel_id=1, source_target_pairs={{0,16},{8,24},{16,0},{24,8},{1,17},{9,25},{17,1},{25,9},{2,18},{10... | collective-permute-start | bytes 1179656 | tf_op jit(solution)/shard_map/ppermute | solution.py:278
  61.2 1.4 %collective-permute-start.6 = (f32[192,128]{1,0:T(8,128)S(1)}, f32[192,128]{1,0:T(8,128)S(1)}, u32[]{:S(2)}, u32[]{:S(2)}) collective-permute-start(f32[192,128]{1,0:T(8,128)S(1)} %get-tuple-element.63), channel_id=1, source_target_pairs={{0,1},{1,0},{2,3},{3,2},{4,5},{5,4},{6,7},{7,6},{8,9},{9,8},{10,11... | collective-permute-start | bytes 294920 | tf_op jit(solution)/shard_map/ppermute | solution.py:278
  62.6 12.0 %collective-permute-start.10 = (f32[768,128]{1,0:T(8,128)S(1)}, f32[768,128]{1,0:T(8,128)S(1)}, u32[]{:S(2)}, u32[]{:S(2)}) collective-permute-start(f32[768,128]{1,0:T(8,128)S(1)} %copy-done.5), channel_id=1, source_target_pairs={{0,8},{8,0},{16,24},{24,16},{1,9},{9,1},{17,25},{25,17},{2,10},{10... | collective-permute-start | bytes 1179656 | tf_op jit(solution)/shard_map/ppermute | solution.py:278
  62.7 12.0 %collective-permute-start.11 = (f32[768,128]{1,0:T(8,128)S(1)}, f32[768,128]{1,0:T(8,128)S(1)}, u32[]{:S(2)}, u32[]{:S(2)}) collective-permute-start(f32[768,128]{1,0:T(8,128)S(1)} %get-tuple-element.71.refs_3_.refs_4_), channel_id=1, source_target_pairs={{0,16},{8,24},{16,0},{24,8},{1,17},{9,25},{17,1},{25,9},{2,18},{10... | collective-permute-start | bytes 1179656 | tf_op jit(solution)/shard_map/ppermute | solution.py:278
  67.2 5.1 %collective-permute-start.9 = (f32[192,128]{1,0:T(8,128)S(1)}, f32[192,128]{1,0:T(8,128)S(1)}, u32[]{:S(2)}, u32[]{:S(2)}) collective-permute-start(f32[192,128]{1,0:T(8,128)S(1)} %add.51), channel_id=1, source_target_pairs={{0,2},{1,3},{2,0},{3,1},{4,6},{5,7},{6,4},{7,5},{8,10},{9,11},{10,... | collective-permute-start | bytes 294920 | tf_op jit(solution)/shard_map/ppermute | solution.py:278
  68.7 16.0 %collective-permute-start.14 = (f32[768,128]{1,0:T(8,128)S(1)}, f32[768,128]{1,0:T(8,128)S(1)}, u32[]{:S(2)}, u32[]{:S(2)}) collective-permute-start(f32[768,128]{1,0:T(8,128)S(1)} %collective-permute-done.7.refs_5_.refs_6_), channel_id=1, source_target_pairs={{0,16},{8,24},{16,0},{24,8},{1,17},{9,25},{17,1},{25,9},{2,18},{10... | collective-permute-start | bytes 1179656 | tf_op jit(solution)/shard_map/ppermute | solution.py:278
  70.3 14.5 %collective-permute-start.15 = (f32[768,128]{1,0:T(8,128)S(1)}, f32[768,128]{1,0:T(8,128)S(1)}, u32[]{:S(2)}, u32[]{:S(2)}) collective-permute-start(f32[768,128]{1,0:T(8,128)S(1)} %collective-permute-done.8.refs_6_.refs_7_), channel_id=1, source_target_pairs={{0,8},{8,0},{16,24},{24,16},{1,9},{9,1},{17,25},{25,17},{2,10},{10... | collective-permute-start | bytes 1179656 | tf_op jit(solution)/shard_map/ppermute | solution.py:278
  75.6 15.6 %collective-permute-start.13 = (f32[768,128]{1,0:T(8,128)S(1)}, f32[768,128]{1,0:T(8,128)S(1)}, u32[]{:S(2)}, u32[]{:S(2)}) collective-permute-start(f32[768,128]{1,0:T(8,128)S(1)} %get-tuple-element.92.refs_3_), channel_id=1, source_target_pairs={{0,8},{8,0},{16,24},{24,16},{1,9},{9,1},{17,25},{25,17},{2,10},{10... | collective-permute-start | bytes 1179656 | tf_op jit(solution)/shard_map/ppermute | solution.py:278
  77.6 13.5 %collective-permute-start.18 = (f32[768,128]{1,0:T(8,128)S(1)}, f32[768,128]{1,0:T(8,128)S(1)}, u32[]{:S(2)}, u32[]{:S(2)}) collective-permute-start(f32[768,128]{1,0:T(8,128)S(1)} %get-tuple-element.89.refs_4_), channel_id=1, source_target_pairs={{0,16},{8,24},{16,0},{24,8},{1,17},{9,25},{17,1},{25,9},{2,18},{10... | collective-permute-start | bytes 1179656 | tf_op jit(solution)/shard_map/ppermute | solution.py:278
  79.2 5.5 %collective-permute-start.12 = (f32[192,128]{1,0:T(8,128)S(1)}, f32[192,128]{1,0:T(8,128)S(1)}, u32[]{:S(2)}, u32[]{:S(2)}) collective-permute-start(f32[192,128]{1,0:T(8,128)S(1)} %add.52), channel_id=1, source_target_pairs={{0,4},{1,5},{2,6},{3,7},{4,0},{5,1},{6,2},{7,3},{8,12},{9,13},{10,... | collective-permute-start | bytes 294920 | tf_op jit(solution)/shard_map/ppermute | solution.py:278
  84.7 13.4 %copy-start.6 = (f32[192,256]{1,0:T(8,128)S(1)}, f32[192,256]{1,0:T(8,128)}, u32[]{:S(2)}) copy-start(f32[192,256]{1,0:T(8,128)} %param.5) | copy-start | bytes 589828
  85.7 1.3 %collective-permute-start.16 = (f32[96,128]{1,0:T(8,128)S(1)}, f32[96,128]{1,0:T(8,128)S(1)}, u32[]{:S(2)}, u32[]{:S(2)}) collective-permute-start(f32[96,128]{1,0:T(8,128)S(1)} %get-tuple-element.82), channel_id=1, source_target_pairs={{0,1},{1,0},{2,3},{3,2},{4,5},{5,4},{6,7},{7,6},{8,9},{9,8},{10,11... | collective-permute-start | bytes 147464 | tf_op jit(solution)/shard_map/ppermute | solution.py:278
  87.0 4.2 %collective-permute-start.17 = (f32[96,128]{1,0:T(8,128)S(1)}, f32[96,128]{1,0:T(8,128)S(1)}, u32[]{:S(2)}, u32[]{:S(2)}) collective-permute-start(f32[96,128]{1,0:T(8,128)S(1)} %add.54), channel_id=1, source_target_pairs={{0,2},{1,3},{2,0},{3,1},{4,6},{5,7},{6,4},{7,5},{8,10},{9,11},{10,... | collective-permute-start | bytes 147464 | tf_op jit(solution)/shard_map/ppermute | solution.py:278
  88.8 15.9 %collective-permute-start.21 = (f32[768,128]{1,0:T(8,128)S(1)}, f32[768,128]{1,0:T(8,128)S(1)}, u32[]{:S(2)}, u32[]{:S(2)}) collective-permute-start(f32[768,128]{1,0:T(8,128)S(1)} %get-tuple-element.89.refs_4_), channel_id=1, source_target_pairs={{0,8},{8,0},{16,24},{24,16},{1,9},{9,1},{17,25},{25,17},{2,10},{10... | collective-permute-start | bytes 1179656 | tf_op jit(solution)/shard_map/ppermute | solution.py:278
  89.3 15.4 %collective-permute-start.22 = (f32[768,128]{1,0:T(8,128)S(1)}, f32[768,128]{1,0:T(8,128)S(1)}, u32[]{:S(2)}, u32[]{:S(2)}) collective-permute-start(f32[768,128]{1,0:T(8,128)S(1)} %get-tuple-element.92.refs_3_), channel_id=1, source_target_pairs={{0,16},{8,24},{16,0},{24,8},{1,17},{9,25},{17,1},{25,9},{2,18},{10... | collective-permute-start | bytes 1179656 | tf_op jit(solution)/shard_map/ppermute | solution.py:278
  91.2 17.1 %collective-permute-start.23 = (f32[768,128]{1,0:T(8,128)S(1)}, f32[768,128]{1,0:T(8,128)S(1)}, u32[]{:S(2)}, u32[]{:S(2)}) collective-permute-start(f32[768,128]{1,0:T(8,128)S(1)} %collective-permute-done.13.refs_5_), channel_id=1, source_target_pairs={{0,16},{8,24},{16,0},{24,8},{1,17},{9,25},{17,1},{25,9},{2,18},{10... | collective-permute-start | bytes 1179656 | tf_op jit(solution)/shard_map/ppermute | solution.py:278
  92.6 15.7 %collective-permute-start.25 = (f32[768,128]{1,0:T(8,128)S(1)}, f32[768,128]{1,0:T(8,128)S(1)}, u32[]{:S(2)}, u32[]{:S(2)}) collective-permute-start(f32[768,128]{1,0:T(8,128)S(1)} %collective-permute-done.18.refs_6_), channel_id=1, source_target_pairs={{0,8},{8,0},{16,24},{24,16},{1,9},{9,1},{17,25},{25,17},{2,10},{10... | collective-permute-start | bytes 1179656 | tf_op jit(solution)/shard_map/ppermute | solution.py:278
  94.3 1.6 %collective-permute-start.19 = (f32[192,128]{1,0:T(8,128)S(1)}, f32[192,128]{1,0:T(8,128)S(1)}, u32[]{:S(2)}, u32[]{:S(2)}) collective-permute-start(f32[192,128]{1,0:T(8,128)S(1)} %add.53.refs_0_), channel_id=1, source_target_pairs={{0,1},{1,0},{2,3},{3,2},{4,5},{5,4},{6,7},{7,6},{8,9},{9,8},{10,11... | collective-permute-start | bytes 294920 | tf_op jit(solution)/shard_map/ppermute | solution.py:278
  95.9 8.2 %collective-permute-start.20 = (f32[96,128]{1,0:T(8,128)S(1)}, f32[96,128]{1,0:T(8,128)S(1)}, u32[]{:S(2)}, u32[]{:S(2)}) collective-permute-start(f32[96,128]{1,0:T(8,128)S(1)} %add.55), channel_id=1, source_target_pairs={{0,4},{1,5},{2,6},{3,7},{4,0},{5,1},{6,2},{7,3},{8,12},{9,13},{10,... | collective-permute-start | bytes 147464 | tf_op jit(solution)/shard_map/ppermute | solution.py:278
  104.1 4.2 %collective-permute-start.24 = (f32[96,128]{1,0:T(8,128)S(1)}, f32[96,128]{1,0:T(8,128)S(1)}, u32[]{:S(2)}, u32[]{:S(2)}) collective-permute-start(f32[96,128]{1,0:T(8,128)S(1)} %add.56.refs_1_), channel_id=1, source_target_pairs={{0,1},{1,0},{2,3},{3,2},{4,5},{5,4},{6,7},{7,6},{8,9},{9,8},{10,11... | collective-permute-start | bytes 147464 | tf_op jit(solution)/shard_map/ppermute | solution.py:278
  109.2 1.3 %collective-permute-start.26 = (f32[96,128]{1,0:T(8,128)S(1)}, f32[96,128]{1,0:T(8,128)S(1)}, u32[]{:S(2)}, u32[]{:S(2)}) collective-permute-start(f32[96,128]{1,0:T(8,128)S(1)} %get-tuple-element.102), channel_id=1, source_target_pairs={{0,1},{1,0},{2,3},{3,2},{4,5},{5,4},{6,7},{7,6},{8,9},{9,8},{10,11... | collective-permute-start | bytes 147464 | tf_op jit(solution)/shard_map/ppermute | solution.py:278
  110.5 7.4 %collective-permute-start.29 = (f32[96,128]{1,0:T(8,128)S(1)}, f32[96,128]{1,0:T(8,128)S(1)}, u32[]{:S(2)}, u32[]{:S(2)}) collective-permute-start(f32[96,128]{1,0:T(8,128)S(1)} %add.57), channel_id=1, source_target_pairs={{0,6},{1,7},{2,4},{3,5},{4,2},{5,3},{6,0},{7,1},{8,14},{9,15},{10,... | collective-permute-start | bytes 147464 | tf_op jit(solution)/shard_map/ppermute | solution.py:278
  113.7 5.3 %collective-permute-start.28 = (f32[96,128]{1,0:T(8,128)S(1)}, f32[96,128]{1,0:T(8,128)S(1)}, u32[]{:S(2)}, u32[]{:S(2)}) collective-permute-start(f32[96,128]{1,0:T(8,128)S(1)} %add.57), channel_id=1, source_target_pairs={{0,4},{1,5},{2,6},{3,7},{4,0},{5,1},{6,2},{7,3},{8,12},{9,13},{10,... | collective-permute-start | bytes 147464 | tf_op jit(solution)/shard_map/ppermute | solution.py:278
  114.0 5.0 %collective-permute-start.27 = (f32[96,128]{1,0:T(8,128)S(1)}, f32[96,128]{1,0:T(8,128)S(1)}, u32[]{:S(2)}, u32[]{:S(2)}) collective-permute-start(f32[96,128]{1,0:T(8,128)S(1)} %add.57), channel_id=1, source_target_pairs={{0,2},{1,3},{2,0},{3,1},{4,6},{5,7},{6,4},{7,5},{8,10},{9,11},{10,... | collective-permute-start | bytes 147464 | tf_op jit(solution)/shard_map/ppermute | solution.py:278
  119.1 1.3 %collective-permute-start.30 = (f32[96,128]{1,0:T(8,128)S(1)}, f32[96,128]{1,0:T(8,128)S(1)}, u32[]{:S(2)}, u32[]{:S(2)}) collective-permute-start(f32[96,128]{1,0:T(8,128)S(1)} %add_add_fusion.refs_0_), channel_id=1, source_target_pairs={{0,1},{1,0},{2,3},{3,2},{4,5},{5,4},{6,7},{7,6},{8,9},{9,8},{10,11... | collective-permute-start | bytes 147464 | tf_op jit(solution)/shard_map/ppermute | solution.py:278
  (10 other events, 51.0 us)

commit v3 on v1

--- a/solution.py
+++ b/solution.py
@@ -221,23 +221,26 @@
         yield product.reshape(2, -1, size), slice(place * size, (place + 1) * size)
 
 
-def part_kernel(scale, has_part, core_ref, *refs):
+def part_kernel(scale, parts, core_ref, *refs):
     out_ref = refs[-1]
-    part_ref = refs[0] if has_part else None
-    sums, pieces = refs[has_part : has_part + 3], refs[has_part + 3 : -1]
-    for product, modes in gradient_tiles(scale, core_ref, sums, pieces):
-        out_ref[:, :, modes] = product + part_ref[:, :, modes] if has_part else product
-
-
-def gradient_part(core, sums, pieces, count, part=None):
-    operands = [*sums, *pieces] if part is None else [part, *sums, *pieces]
+    sums, pieces = refs[parts : parts + 3], refs[parts + 3 : -1]
+    tiles = [
+        part_ref.at[:, :, pl.ds(first, pieces[0].shape[0])]
+        for part_ref in refs[:parts]
+        for first in range(0, part_ref.shape[2], pieces[0].shape[0])
+    ]
+    for place, (product, modes) in enumerate(gradient_tiles(scale, core_ref, sums, pieces)):
+        out_ref[:, :, modes] = product + tiles[place][...] if parts else product
+
+
+def gradient_part(core, sums, pieces, count, parts=()):
+    operands = [*parts, *sums, *pieces]
     modes = len(pieces) * pieces[0].shape[0]
     return pl.pallas_call(
-        functools.partial(part_kernel, 1.0 / count, part is not None),
+        functools.partial(part_kernel, 1.0 / count, len(parts)),
         in_specs=[SMEM] + [VMEM] * len(operands),
         out_specs=VMEM,
         out_shape=jax.ShapeDtypeStruct((2, sums[-1].shape[0], modes), jnp.float32),
-        input_output_aliases={} if part is None else {1: 0},
         compiler_params=params(12),
         cost_estimate=COST,
     )(core, *operands)
@@ -317,60 +320,58 @@
     matrix = matrix_halves(transfer_matrix, order, half)
     places = near + side + far
     bits = [1 << bit for bit in range(1, mode_size.bit_length() - 1)]
-    sums, waits = [], []
-    part = None
+    sums, waits, parts = [], [], []
 
     def tied(chunk, places, *earlier):
         for place in places:
             chunk[place] = in_order(chunk[place], *earlier)
+
+    def first_part(places, *earlier):
+        if cut:
+            before = in_order(sums[0][0], *earlier), *sums[0][1:]
+            pieces = [chunks[0][place] for place in places]
+            parts.append(gradient_part(core, before, pieces, count))
 
     for c, (low, high) in enumerate(spans):
         chunk, widths = chunks[c], group_widths(low, high)
         last = c == len(spans) - 1
         send(chunk, 0, *waits)
         send(chunk, 1, *(sums[-1:] if c else []))
-        if c:
-            total = sums[-1]
-            if not last:
-                near_total = fields(chunk, near, 0)
-                total = in_order(total, near_total)
+        if last:
+            first_part(near, sums[-1])
+            total = in_order(sums[-1], *(chunk[place] for place in near[2:]), *parts)
             arrived = mode_exchange(total, mode_size, bits[0])
-            if part is not None:
-                arrived = in_order(arrived, part)
-            total = total + arrived
-            if last:
-                tied(chunk, near[2:], total)
-                near_total = fields(chunk, near, 0)
+            near_total = fields(chunk, near, 0)
+            total = total + in_order(arrived, near_total)
+            send(chunk, 2, *parts)
+            first_part(side + far, near_total)
+            for mask in bits[1:]:
+                total = total + in_order(mode_exchange(total, mode_size, mask), *parts)
+            tied(chunk, side, total)
+            side_total = fields(chunk, side, len(near), total=near_total)
         else:
             near_total = fields(chunk, near, 0)
-        send(chunk, 2, *([near_total] if c else matrix), *([] if part is None else [part]))
-        if c:
-            tied(chunk, side, total)
-            if last:
-                total = in_order(total, near_total)
-                for mask in bits[1:]:
-                    total = total + mode_exchange(total, mode_size, mask)
+            if c:
+                total = in_order(sums[-1], near_total)
+                total = total + mode_exchange(total, mode_size, bits[0])
                 tied(chunk, side, total)
-        side_total = fields(chunk, side, len(near), total=near_total)
-        if c:
-            if not last:
+            send(chunk, 2, *([near_total] if c else matrix))
+            side_total = fields(chunk, side, len(near), total=near_total)
+            if c:
                 total = in_order(total, side_total)
                 for mask in bits[1:]:
                     total = total + mode_exchange(total, mode_size, mask)
-            tied(chunk, far, total)
+        if c:
             other = mode_exchange(total, mode_size, 1)
-            if last:
-                tied(chunk, far, other)
+            tied(chunk, far, total, *([other] if last else []))
             sums[-1] = total, other, intensity[:, slice(*spans[c - 1])]
-        if c == 1 and cut:
-            part = gradient_part(core, sums[0], [chunks[0][place] for place in places], count)
         kept, sent = fields(chunk, far, len(near + side), total=side_total, last=True)
         waits = [side_total, *(chunks[c + 1][place] for place in near[:2])] if not last else []
         sums.append(kept + mode_exchange(sent, mode_size, 1))
-    arrived = [mode_exchange(sums[-1], mode_size, mask) for mask in range(2, mode_size, 2)]
+    arrived = [mode_exchange(sums[-1], mode_size, mask) for mask in (2, *range(mode_size - 2, 2, -2))]
     pieces = [[chunk[place] for place in places] for chunk in chunks[-2:]]
     before = in_order(sums[-2][0], sums[-1]), *sums[-2][1:]
-    part = gradient_part(core, before, pieces[0], count, part)
+    part = gradient_part(core, before, pieces[0], count, parts)
     total = sum((in_order(value, part) for value in arrived), sums[-1])
     sums[-1] = total, mode_exchange(total, mode_size, 1), intensity[:, slice(*spans[-1])]
     return last_gradient(core, order, part, sums[-1], pieces[1], count)

time: 127 us -> 126 us (level)
  waiting for transfers between devices: 40.9 us -> 38.8 us
    ppermute x31, waiting for transfers between devices: 40.9 us -> 38.8 us  [exchange(): return lax.ppermute(value, axis, [(i, i ^ mask) for i in range(size)])]
    pallas_call x2 -> x3, Pallas kernels: 8.59 us -> 9.74 us  [gradient_part(): pl.pallas_call(functools.partial(part_kernel, 1.0 / count, len(parts)), i...]
  transfers between devices with their start and end apart: 31 -> 31, of which waited for: 18 -> 17; matrix products, arithmetic and copies ran while one was open for 0% -> 0% of each run, Pallas kernels for 25% -> 26%
where the time goes in v3:
time: 126 us; the launch traced here: 125 us
  Pallas kernels  40.1 us (32%)
  waiting for transfers between devices  38.8 us (31%)
  starting transfers between devices  35.8 us (28%)
  local copies, waits for them, and re-layouts  9.99 us (8%)
    ppermute x31, waiting for transfers between devices, exchange(): return lax.ppermute(value, axis, [(i, i ^ mask) for i in range(size)])  38.8 us
    ppermute x31, starting transfers between devices, exchange(): return lax.ppermute(value, axis, [(i, i ^ mask) for i in range(size)])  35.8 us
    pallas_call x9, Pallas kernels, add_fields(): pl.pallas_call(functools.partial(fields_kernel, first, widths, total is n...  13.7 us
    unnamed x22, local copies, waits for them, and re-layouts  9.81 us
    pallas_call x3, Pallas kernels, gradient_part(): pl.pallas_call(functools.partial(part_kernel, 1.0 / count, len(parts)), i...  9.74 us
    pallas_call x1, Pallas kernels, matrix_halves(): pl.pallas_call(matrix_kernel, grid_spec=pltpu.PrefetchScalarGridSpec(num_...  7.24 us
    pallas_call x1, Pallas kernels, last_gradient(): pl.pallas_call(functools.partial(last_kernel, 1.0 / count), in_specs=[SME...  4.94 us
    pallas_call x3, Pallas kernels, probe_chunk(): pl.pallas_call(functools.partial(chunk_kernel, low, high), in_specs=[pl.B...  4.45 us
  transfers between devices with their start and end apart: 31, of which 17 were waited for; matrix products, arithmetic and copies ran while one was open for 0% of the time, Pallas kernels for 26%

profile of v3, /device:TPU:0, one launch (start us, length us, event | category | flops | bytes accessed | tf_op | source)
XLA Modules:
  0.0 125.3 jit_solution(15025037803655014968)
XLA Ops:
  1.4 3.0 %collective-permute-start = (f32[768,256]{1,0:T(8,128)S(1)}, f32[768,256]{1,0:T(8,128)}, u32[]{:S(2)}, u32[]{:S(2)}) collective-permute-start(f32[768,256]{1,0:T(8,128)S(1)} %get-tuple-element.54.refs_3_), channel_id=1, source_target_pairs={{0,8},{8,0},{16,24},{24,16},{1,9},{9,1},{17,25},{25,17},{2,10},{10... | collective-permute-start | bytes 2359304 | tf_op jit(solution)/shard_map/ppermute | solution.py:281
  6.6 7.2 %shard_map.37 = (bf16[384,6144]{1,0:T(8,128)(2,1)S(1)}, bf16[384,6144]{1,0:T(8,128)(2,1)S(1)}) custom-call(s32[8]{0:T(128)S(1)} %stack.35.order_ref, f32[2,192,6144]{2,1,0:T(8,128)} %matrix_ref.1), custom_call_target="tpu_custom_call" | custom-call | flops 1000 | bytes 1000 | tf_op jit(solution)/shard_map/pallas_call | solution.py:104
  13.9 2.2 %copy-done = bf16[384,6144]{1,0:T(8,128)(2,1)} copy-done((bf16[384,6144]{1,0:T(8,128)(2,1)}, bf16[384,6144]{1,0:T(8,128)(2,1)S(1)}, u32[]{:S(2)}) %copy-start) | copy-done | bytes 4718616
  16.1 2.2 %copy-done.2 = bf16[384,6144]{1,0:T(8,128)(2,1)} copy-done((bf16[384,6144]{1,0:T(8,128)(2,1)}, bf16[384,6144]{1,0:T(8,128)(2,1)S(1)}, u32[]{:S(2)}) %copy-start.2) | copy-done | bytes 4718616
  18.2 4.7 %collective-permute-done.refs_5_ = f32[768,256]{1,0:T(8,128)} collective-permute-done((f32[768,256]{1,0:T(8,128)S(1)}, f32[768,256]{1,0:T(8,128)}, u32[]{:S(2)}, u32[]{:S(2)}) %collective-permute-start) | collective-permute-done | bytes 786464 | tf_op jit(solution)/shard_map/ppermute | solution.py:281
  22.9 2.1 %collective-permute-done.1.refs_6_ = f32[768,256]{1,0:T(8,128)} collective-permute-done((f32[768,256]{1,0:T(8,128)S(1)}, f32[768,256]{1,0:T(8,128)}, u32[]{:S(2)}, u32[]{:S(2)}) %collective-permute-start.1) | collective-permute-done | bytes 786464 | tf_op jit(solution)/shard_map/ppermute | solution.py:281
  27.1 1.6 %shard_map.42 = (f32[768,128]{1,0:T(8,128)S(1)}, f32[768,128]{1,0:T(8,128)S(1)}) custom-call(f32[2,1536,256]{2,1,0:T(8,128)} %probes_ref.5), custom_call_target="tpu_custom_call" | custom-call | flops 1000 | bytes 1000 | tf_op jit(solution)/shard_map/pallas_call | solution.py:81
  29.4 2.3 %copy-done.1 = bf16[384,6144]{1,0:T(8,128)(2,1)S(1)} copy-done((bf16[384,6144]{1,0:T(8,128)(2,1)S(1)}, bf16[384,6144]{1,0:T(8,128)(2,1)}, u32[]{:S(2)}) %copy-start.1) | copy-done | bytes 4718616
  31.7 2.3 %copy-done.3 = bf16[384,6144]{1,0:T(8,128)(2,1)S(1)} copy-done((bf16[384,6144]{1,0:T(8,128)(2,1)S(1)}, bf16[384,6144]{1,0:T(8,128)(2,1)}, u32[]{:S(2)}) %copy-start.3) | copy-done | bytes 4718616
  34.1 3.4 %shard_map.39.refs_1_ = f32[2,192,128]{2,1,0:T(8,128)S(1)} custom-call(s32[1]{0:T(128)} %bitcast.refs_0_.core_ref, bf16[384,6144]{1,0:T(8,128)(2,1)S(1)} %copy-done.1, bf16[384,6144]{1,0:T(8,128)(2,1)S(1)} %copy-done.3, f32[768,256]{1,0:T(8,128)S(1)} %get-tuple-element.54.refs_3_, f32[768,256]{1,0:T(8,128)S(1)} %get-tuple-element.55.refs_4_, ...), custom_call_target="tpu_custom_call" | custom-call | flops 1000 | bytes 1000 | tf_op jit(solution)/shard_map/pallas_call | solution.py:188
  37.5 2.2 %collective-permute-done.2.refs_4_.refs_3_ = f32[768,256]{1,0:T(8,128)S(1)} collective-permute-done((f32[768,256]{1,0:T(8,128)S(1)}, f32[768,256]{1,0:T(8,128)S(1)}, u32[]{:S(2)}, u32[]{:S(2)}) %collective-permute-start.2) | collective-permute-done | bytes 786464 | tf_op jit(solution)/shard_map/ppermute | solution.py:281
  39.7 2.1 %collective-permute-done.3.refs_5_.refs_4_ = f32[768,256]{1,0:T(8,128)S(1)} collective-permute-done((f32[768,256]{1,0:T(8,128)S(1)}, f32[768,256]{1,0:T(8,128)S(1)}, u32[]{:S(2)}, u32[]{:S(2)}) %collective-permute-start.3) | collective-permute-done | bytes 786464 | tf_op jit(solution)/shard_map/ppermute | solution.py:281
  43.0 2.0 %collective-permute-start.8 = (f32[768,128]{1,0:T(8,128)S(1)}, f32[768,128]{1,0:T(8,128)S(1)}, u32[]{:S(2)}, u32[]{:S(2)}) collective-permute-start(f32[768,128]{1,0:T(8,128)S(1)} %copy-done.5), channel_id=1, source_target_pairs={{0,16},{8,24},{16,0},{24,8},{1,17},{9,25},{17,1},{25,9},{2,18},{10... | collective-permute-start | bytes 1179656 | tf_op jit(solution)/shard_map/ppermute | solution.py:281
  45.0 13.7 %collective-permute-done.4.refs_4_.refs_5_ = f32[768,256]{1,0:T(8,128)} collective-permute-done((f32[768,256]{1,0:T(8,128)}, f32[768,256]{1,0:T(8,128)}, u32[]{:S(2)}, u32[]{:S(2)}) %collective-permute-start.4) | collective-permute-done | bytes 786464 | tf_op jit(solution)/shard_map/ppermute | solution.py:281
  58.7 2.5 %shard_map.41 = (f32[192,128]{1,0:T(8,128)S(1)}, f32[192,128]{1,0:T(8,128)S(1)}) custom-call(s32[1]{0:T(128)} %bitcast.refs_0_.core_ref, f32[2,192,128]{2,1,0:T(8,128)S(1)} %shard_map.40.refs_1_, bf16[384,6144]{1,0:T(8,128)(2,1)S(1)} %copy-done.1, bf16[384,6144]{1,0:T(8,128)(2,1)S(1)} %copy-done.3, f32[768,256]{1,0:T(8,128)} %collective-permute-done.4.refs_4_.refs_5_, ...), custom_call_target="tpu_custom_call" | custom-call | flops 1000 | bytes 1000 | tf_op jit(solution)/shard_map/pallas_call | solution.py:188
  62.7 2.0 %collective-permute-start.11 = (f32[768,128]{1,0:T(8,128)S(1)}, f32[768,128]{1,0:T(8,128)S(1)}, u32[]{:S(2)}, u32[]{:S(2)}) collective-permute-start(f32[768,128]{1,0:T(8,128)S(1)} %get-tuple-element.67.refs_3_.refs_5_), channel_id=1, source_target_pairs={{0,16},{8,24},{16,0},{24,8},{1,17},{9,25},{17,1},{25,9},{2,18},{10... | collective-permute-start | bytes 1179656 | tf_op jit(solution)/shard_map/ppermute | solution.py:281
  65.6 1.5 %shard_map.43.refs_1_ = f32[2,192,64]{2,1,0:T(8,128)S(1)} custom-call(s32[1]{0:T(128)} %bitcast.refs_0_.core_ref, bf16[384,6144]{1,0:T(8,128)(2,1)S(1)} %copy-done.1, bf16[384,6144]{1,0:T(8,128)(2,1)S(1)} %copy-done.3, f32[768,128]{1,0:T(8,128)S(1)} %get-tuple-element.67.refs_3_.refs_5_, f32[768,128]{1,0:T(8,128)S(1)} %copy-done.5, ...), custom_call_target="tpu_custom_call" | custom-call | flops 1000 | bytes 1000 | tf_op jit(solution)/shard_map/pallas_call | solution.py:188
  67.2 1.6 %collective-permute-start.9 = (f32[192,128]{1,0:T(8,128)S(1)}, f32[192,128]{1,0:T(8,128)S(1)}, u32[]{:S(2)}, u32[]{:S(2)}) collective-permute-start(f32[192,128]{1,0:T(8,128)S(1)} %add.51), channel_id=1, source_target_pairs={{0,2},{1,3},{2,0},{3,1},{4,6},{5,7},{6,4},{7,5},{8,10},{9,11},{10,... | collective-permute-start | bytes 294920 | tf_op jit(solution)/shard_map/ppermute | solution.py:281
  72.3 2.3 %collective-permute-done.10.refs_4_.refs_9_ = f32[768,128]{1,0:T(8,128)S(1)} collective-permute-done((f32[768,128]{1,0:T(8,128)S(1)}, f32[768,128]{1,0:T(8,128)S(1)}, u32[]{:S(2)}, u32[]{:S(2)}) %collective-permute-start.10) | collective-permute-done | bytes 393248 | tf_op jit(solution)/shard_map/ppermute | solution.py:281
  75.6 2.1 %collective-permute-start.17 = (f32[768,128]{1,0:T(8,128)S(1)}, f32[768,128]{1,0:T(8,128)S(1)}, u32[]{:S(2)}, u32[]{:S(2)}) collective-permute-start(f32[768,128]{1,0:T(8,128)S(1)} %get-tuple-element.87.refs_3_), channel_id=1, source_target_pairs={{0,8},{8,0},{16,24},{24,16},{1,9},{9,1},{17,25},{25,17},{2,10},{10... | collective-permute-start | bytes 1179656 | tf_op jit(solution)/shard_map/ppermute | solution.py:281
  79.2 2.6 %collective-permute-start.12 = (f32[192,128]{1,0:T(8,128)S(1)}, f32[192,128]{1,0:T(8,128)S(1)}, u32[]{:S(2)}, u32[]{:S(2)}) collective-permute-start(f32[192,128]{1,0:T(8,128)S(1)} %add.52), channel_id=1, source_target_pairs={{0,4},{1,5},{2,6},{3,7},{4,0},{5,1},{6,2},{7,3},{8,12},{9,13},{10,... | collective-permute-start | bytes 294920 | tf_op jit(solution)/shard_map/ppermute | solution.py:281
  81.8 2.9 %collective-permute-done.12 = f32[192,128]{1,0:T(8,128)S(1)} collective-permute-done((f32[192,128]{1,0:T(8,128)S(1)}, f32[192,128]{1,0:T(8,128)S(1)}, u32[]{:S(2)}, u32[]{:S(2)}) %collective-permute-start.12) | collective-permute-done | bytes 98336 | tf_op jit(solution)/shard_map/ppermute | solution.py:281
  88.9 3.4 %shard_map.46.refs_0_ = f32[2,192,3072]{2,1,0:T(8,128)S(1)} custom-call(s32[1]{0:T(128)} %bitcast.refs_0_.core_ref, f32[192,128]{1,0:T(8,128)S(1)} %add.53.refs_0_, f32[192,128]{1,0:T(8,128)S(1)} %collective-permute-done.16.refs_1_, f32[192,128]{1,0:T(8,128)S(1)} %slice.9.refs_2_, f32[768,256]{1,0:T(8,128)S(1)} %get-tuple-element.54.refs_3_, ...), custom_call_target="tpu_custom_call" | custom-call | flops 1000 | bytes 1000 | tf_op jit(solution)/shard_map/pallas_call | solution.py:239
  93.4 1.6 %collective-permute-start.25 = (f32[768,128]{1,0:T(8,128)S(1)}, f32[768,128]{1,0:T(8,128)S(1)}, u32[]{:S(2)}, u32[]{:S(2)}) collective-permute-start(f32[768,128]{1,0:T(8,128)S(1)} %collective-permute-done.18.refs_6_), channel_id=1, source_target_pairs={{0,8},{8,0},{16,24},{24,16},{1,9},{9,1},{17,25},{25,17},{2,10},{10... | collective-permute-start | bytes 1179656 | tf_op jit(solution)/shard_map/ppermute | solution.py:281
  95.0 1.6 %collective-permute-start.19 = (f32[96,128]{1,0:T(8,128)S(1)}, f32[96,128]{1,0:T(8,128)S(1)}, u32[]{:S(2)}, u32[]{:S(2)}) collective-permute-start(f32[96,128]{1,0:T(8,128)S(1)} %add.54), channel_id=1, source_target_pairs={{0,2},{1,3},{2,0},{3,1},{4,6},{5,7},{6,4},{7,5},{8,10},{9,11},{10,... | collective-permute-start | bytes 147464 | tf_op jit(solution)/shard_map/ppermute | solution.py:281
  96.6 1.5 %shard_map.48.refs_1_ = f32[2,192,64]{2,1,0:T(8,128)S(1)} custom-call(s32[1]{0:T(128)} %bitcast.refs_0_.core_ref, bf16[384,6144]{1,0:T(8,128)(2,1)S(1)} %bitcast.10, bf16[384,6144]{1,0:T(8,128)(2,1)S(1)} %bitcast.12, f32[768,128]{1,0:T(8,128)S(1)} %get-tuple-element.87.refs_3_, f32[768,128]{1,0:T(8,128)S(1)} %get-tuple-element.85.refs_4_, ...), custom_call_target="tpu_custom_call" | custom-call | flops 1000 | bytes 1000 | tf_op jit(solution)/shard_map/pallas_call | solution.py:188
  99.1 2.9 %collective-permute-start.20 = (f32[96,128]{1,0:T(8,128)S(1)}, f32[96,128]{1,0:T(8,128)S(1)}, u32[]{:S(2)}, u32[]{:S(2)}) collective-permute-start(f32[96,128]{1,0:T(8,128)S(1)} %add.55), channel_id=1, source_target_pairs={{0,4},{1,5},{2,6},{3,7},{4,0},{5,1},{6,2},{7,3},{8,12},{9,13},{10,... | collective-permute-start | bytes 147464 | tf_op jit(solution)/shard_map/ppermute | solution.py:281
  102.1 3.6 %shard_map.49.refs_1_ = f32[2,192,3072]{2,1,0:T(8,128)S(1)} custom-call(s32[1]{0:T(128)} %bitcast.refs_0_.core_ref, f32[192,128]{1,0:T(8,128)S(1)} %add.53.refs_0_, f32[192,128]{1,0:T(8,128)S(1)} %collective-permute-done.16.refs_1_, f32[192,128]{1,0:T(8,128)S(1)} %slice.9.refs_2_, f32[768,256]{1,0:T(8,128)S(1)} %collective-permute-done.2.refs_4_.refs_3_, ...), custom_call_target="tpu_custom_call" | custom-call | flops 1000 | bytes 1000 | tf_op jit(solution)/shard_map/pallas_call | solution.py:239
  109.9 2.7 %collective-permute-start.29 = (f32[96,128]{1,0:T(8,128)S(1)}, f32[96,128]{1,0:T(8,128)S(1)}, u32[]{:S(2)}, u32[]{:S(2)}) collective-permute-start(f32[96,128]{1,0:T(8,128)S(1)} %add.57), channel_id=1, source_target_pairs={{0,4},{1,5},{2,6},{3,7},{4,0},{5,1},{6,2},{7,3},{8,12},{9,13},{10,... | collective-permute-start | bytes 147464 | tf_op jit(solution)/shard_map/ppermute | solution.py:281
  112.6 1.6 %collective-permute-start.28 = (f32[96,128]{1,0:T(8,128)S(1)}, f32[96,128]{1,0:T(8,128)S(1)}, u32[]{:S(2)}, u32[]{:S(2)}) collective-permute-start(f32[96,128]{1,0:T(8,128)S(1)} %add.57), channel_id=1, source_target_pairs={{0,6},{1,7},{2,4},{3,5},{4,2},{5,3},{6,0},{7,1},{8,14},{9,15},{10,... | collective-permute-start | bytes 147464 | tf_op jit(solution)/shard_map/ppermute | solution.py:281
  114.8 2.7 %shard_map.52.part_ref = f32[2,192,6144]{2,1,0:T(8,128)S(1)} custom-call(s32[1]{0:T(128)} %bitcast.refs_0_.core_ref, f32[2,192,3072]{2,1,0:T(8,128)S(1)} %shard_map.46.refs_0_, f32[2,192,3072]{2,1,0:T(8,128)S(1)} %shard_map.49.refs_1_, f32[96,128]{1,0:T(8,128)S(1)} %add.56.refs_2_, f32[96,128]{1,0:T(8,128)S(1)} %collective-permute-done.24.refs_3_, ...), custom_call_target="tpu_custom_call" | custom-call | flops 1000 | bytes 1000 | tf_op jit(solution)/shard_map/pallas_call | solution.py:239
  120.2 4.9 %shard_map.53 = f32[2,192,6144]{2,1,0:T(8,128)} custom-call(s32[1]{0:T(128)} %bitcast.refs_0_.core_ref, s32[8]{0:T(128)S(1)} %stack.35.order_ref, f32[2,192,6144]{2,1,0:T(8,128)S(1)} %shard_map.52.part_ref, f32[96,128]{1,0:T(8,128)S(1)} %add_add_fusion.refs_0_, f32[96,128]{1,0:T(8,128)S(1)} %collective-permute-done.30.refs_1_, ...), custom_call_target="tpu_custom_call" | custom-call | flops 1000 | bytes 1000 | tf_op jit(solution)/shard_map/pallas_call | solution.py:269
  (82 shorter events, 29.6 us)
Async XLA Ops:
  1.4 21.5 %collective-permute-start = (f32[768,256]{1,0:T(8,128)S(1)}, f32[768,256]{1,0:T(8,128)}, u32[]{:S(2)}, u32[]{:S(2)}) collective-permute-start(f32[768,256]{1,0:T(8,128)S(1)} %get-tuple-element.54.refs_3_), channel_id=1, source_target_pairs={{0,8},{8,0},{16,24},{24,16},{1,9},{9,1},{17,25},{25,17},{2,10},{10... | collective-permute-start | bytes 2359304 | tf_op jit(solution)/shard_map/ppermute | solution.py:281
  4.4 20.6 %collective-permute-start.1 = (f32[768,256]{1,0:T(8,128)S(1)}, f32[768,256]{1,0:T(8,128)}, u32[]{:S(2)}, u32[]{:S(2)}) collective-permute-start(f32[768,256]{1,0:T(8,128)S(1)} %get-tuple-element.55.refs_4_), channel_id=1, source_target_pairs={{0,16},{8,24},{16,0},{24,8},{1,17},{9,25},{17,1},{25,9},{2,18},{10... | collective-permute-start | bytes 2359304 | tf_op jit(solution)/shard_map/ppermute | solution.py:281
  6.0 33.7 %collective-permute-start.2 = (f32[768,256]{1,0:T(8,128)S(1)}, f32[768,256]{1,0:T(8,128)S(1)}, u32[]{:S(2)}, u32[]{:S(2)}) collective-permute-start(f32[768,256]{1,0:T(8,128)S(1)} %get-tuple-element.55.refs_4_), channel_id=1, source_target_pairs={{0,8},{8,0},{16,24},{24,16},{1,9},{9,1},{17,25},{25,17},{2,10},{10... | collective-permute-start | bytes 2359304 | tf_op jit(solution)/shard_map/ppermute | solution.py:281
  6.5 35.3 %collective-permute-start.3 = (f32[768,256]{1,0:T(8,128)S(1)}, f32[768,256]{1,0:T(8,128)S(1)}, u32[]{:S(2)}, u32[]{:S(2)}) collective-permute-start(f32[768,256]{1,0:T(8,128)S(1)} %get-tuple-element.54.refs_3_), channel_id=1, source_target_pairs={{0,16},{8,24},{16,0},{24,8},{1,17},{9,25},{17,1},{25,9},{2,18},{10... | collective-permute-start | bytes 2359304 | tf_op jit(solution)/shard_map/ppermute | solution.py:281
  25.0 33.7 %collective-permute-start.4 = (f32[768,256]{1,0:T(8,128)}, f32[768,256]{1,0:T(8,128)}, u32[]{:S(2)}, u32[]{:S(2)}) collective-permute-start(f32[768,256]{1,0:T(8,128)} %collective-permute-done.refs_5_), channel_id=1, source_target_pairs={{0,16},{8,24},{16,0},{24,8},{1,17},{9,25},{17,1},{25,9},{2,18},{10... | collective-permute-start | bytes 2359304 | tf_op jit(solution)/shard_map/ppermute | solution.py:281
  26.5 32.2 %collective-permute-start.5 = (f32[768,256]{1,0:T(8,128)}, f32[768,256]{1,0:T(8,128)}, u32[]{:S(2)}, u32[]{:S(2)}) collective-permute-start(f32[768,256]{1,0:T(8,128)} %collective-permute-done.1.refs_6_), channel_id=1, source_target_pairs={{0,8},{8,0},{16,24},{24,16},{1,9},{9,1},{17,25},{25,17},{2,10},{10... | collective-permute-start | bytes 2359304 | tf_op jit(solution)/shard_map/ppermute | solution.py:281
  42.8 21.8 %collective-permute-start.7 = (f32[768,128]{1,0:T(8,128)S(1)}, f32[768,128]{1,0:T(8,128)S(1)}, u32[]{:S(2)}, u32[]{:S(2)}) collective-permute-start(f32[768,128]{1,0:T(8,128)S(1)} %get-tuple-element.67.refs_3_.refs_5_), channel_id=1, source_target_pairs={{0,8},{8,0},{16,24},{24,16},{1,9},{9,1},{17,25},{25,17},{2,10},{10... | collective-permute-start | bytes 1179656 | tf_op jit(solution)/shard_map/ppermute | solution.py:281
  43.0 22.7 %collective-permute-start.8 = (f32[768,128]{1,0:T(8,128)S(1)}, f32[768,128]{1,0:T(8,128)S(1)}, u32[]{:S(2)}, u32[]{:S(2)}) collective-permute-start(f32[768,128]{1,0:T(8,128)S(1)} %copy-done.5), channel_id=1, source_target_pairs={{0,16},{8,24},{16,0},{24,8},{1,17},{9,25},{17,1},{25,9},{2,18},{10... | collective-permute-start | bytes 1179656 | tf_op jit(solution)/shard_map/ppermute | solution.py:281
  61.2 1.4 %collective-permute-start.6 = (f32[192,128]{1,0:T(8,128)S(1)}, f32[192,128]{1,0:T(8,128)S(1)}, u32[]{:S(2)}, u32[]{:S(2)}) collective-permute-start(f32[192,128]{1,0:T(8,128)S(1)} %get-tuple-element.59), channel_id=1, source_target_pairs={{0,1},{1,0},{2,3},{3,2},{4,5},{5,4},{6,7},{7,6},{8,9},{9,8},{10,11... | collective-permute-start | bytes 294920 | tf_op jit(solution)/shard_map/ppermute | solution.py:281
  62.6 12.0 %collective-permute-start.10 = (f32[768,128]{1,0:T(8,128)S(1)}, f32[768,128]{1,0:T(8,128)S(1)}, u32[]{:S(2)}, u32[]{:S(2)}) collective-permute-start(f32[768,128]{1,0:T(8,128)S(1)} %copy-done.5), channel_id=1, source_target_pairs={{0,8},{8,0},{16,24},{24,16},{1,9},{9,1},{17,25},{25,17},{2,10},{10... | collective-permute-start | bytes 1179656 | tf_op jit(solution)/shard_map/ppermute | solution.py:281
  62.7 12.0 %collective-permute-start.11 = (f32[768,128]{1,0:T(8,128)S(1)}, f32[768,128]{1,0:T(8,128)S(1)}, u32[]{:S(2)}, u32[]{:S(2)}) collective-permute-start(f32[768,128]{1,0:T(8,128)S(1)} %get-tuple-element.67.refs_3_.refs_5_), channel_id=1, source_target_pairs={{0,16},{8,24},{16,0},{24,8},{1,17},{9,25},{17,1},{25,9},{2,18},{10... | collective-permute-start | bytes 1179656 | tf_op jit(solution)/shard_map/ppermute | solution.py:281
  67.2 5.1 %collective-permute-start.9 = (f32[192,128]{1,0:T(8,128)S(1)}, f32[192,128]{1,0:T(8,128)S(1)}, u32[]{:S(2)}, u32[]{:S(2)}) collective-permute-start(f32[192,128]{1,0:T(8,128)S(1)} %add.51), channel_id=1, source_target_pairs={{0,2},{1,3},{2,0},{3,1},{4,6},{5,7},{6,4},{7,5},{8,10},{9,11},{10,... | collective-permute-start | bytes 294920 | tf_op jit(solution)/shard_map/ppermute | solution.py:281
  68.7 16.1 %collective-permute-start.13 = (f32[768,128]{1,0:T(8,128)S(1)}, f32[768,128]{1,0:T(8,128)S(1)}, u32[]{:S(2)}, u32[]{:S(2)}) collective-permute-start(f32[768,128]{1,0:T(8,128)S(1)} %collective-permute-done.7.refs_5_.refs_7_), channel_id=1, source_target_pairs={{0,16},{8,24},{16,0},{24,8},{1,17},{9,25},{17,1},{25,9},{2,18},{10... | collective-permute-start | bytes 1179656 | tf_op jit(solution)/shard_map/ppermute | solution.py:281
  70.3 14.6 %collective-permute-start.14 = (f32[768,128]{1,0:T(8,128)S(1)}, f32[768,128]{1,0:T(8,128)S(1)}, u32[]{:S(2)}, u32[]{:S(2)}) collective-permute-start(f32[768,128]{1,0:T(8,128)S(1)} %collective-permute-done.8.refs_6_.refs_8_), channel_id=1, source_target_pairs={{0,8},{8,0},{16,24},{24,16},{1,9},{9,1},{17,25},{25,17},{2,10},{10... | collective-permute-start | bytes 1179656 | tf_op jit(solution)/shard_map/ppermute | solution.py:281
  75.6 16.8 %collective-permute-start.17 = (f32[768,128]{1,0:T(8,128)S(1)}, f32[768,128]{1,0:T(8,128)S(1)}, u32[]{:S(2)}, u32[]{:S(2)}) collective-permute-start(f32[768,128]{1,0:T(8,128)S(1)} %get-tuple-element.87.refs_3_), channel_id=1, source_target_pairs={{0,8},{8,0},{16,24},{24,16},{1,9},{9,1},{17,25},{25,17},{2,10},{10... | collective-permute-start | bytes 1179656 | tf_op jit(solution)/shard_map/ppermute | solution.py:281
  77.6 14.7 %collective-permute-start.18 = (f32[768,128]{1,0:T(8,128)S(1)}, f32[768,128]{1,0:T(8,128)S(1)}, u32[]{:S(2)}, u32[]{:S(2)}) collective-permute-start(f32[768,128]{1,0:T(8,128)S(1)} %get-tuple-element.85.refs_4_), channel_id=1, source_target_pairs={{0,16},{8,24},{16,0},{24,8},{1,17},{9,25},{17,1},{25,9},{2,18},{10... | collective-permute-start | bytes 1179656 | tf_op jit(solution)/shard_map/ppermute | solution.py:281
  79.2 5.5 %collective-permute-start.12 = (f32[192,128]{1,0:T(8,128)S(1)}, f32[192,128]{1,0:T(8,128)S(1)}, u32[]{:S(2)}, u32[]{:S(2)}) collective-permute-start(f32[192,128]{1,0:T(8,128)S(1)} %add.52), channel_id=1, source_target_pairs={{0,4},{1,5},{2,6},{3,7},{4,0},{5,1},{6,2},{7,3},{8,12},{9,13},{10,... | collective-permute-start | bytes 294920 | tf_op jit(solution)/shard_map/ppermute | solution.py:281
  84.7 11.9 %slice-start.2 = ((s8[4718592]{0:T(1024)(128)(4,1)}), s8[4194304]{0:T(1024)(128)(4,1)S(1)}, s32[]{:S(2)}) async-start(s8[4718592]{0:T(1024)(128)(4,1)} %bitcast.11), calls=%async_computation.2 | async-start | bytes 8388608
  84.7 4.2 %collective-permute-start.16 = (f32[192,128]{1,0:T(8,128)S(1)}, f32[192,128]{1,0:T(8,128)S(1)}, u32[]{:S(2)}, u32[]{:S(2)}) collective-permute-start(f32[192,128]{1,0:T(8,128)S(1)} %add.53.refs_0_), channel_id=1, source_target_pairs={{0,1},{1,0},{2,3},{3,2},{4,5},{5,4},{6,7},{7,6},{8,9},{9,8},{10,11... | collective-permute-start | bytes 294920 | tf_op jit(solution)/shard_map/ppermute | solution.py:281
  85.8 1.4 %collective-permute-start.15 = (f32[96,128]{1,0:T(8,128)S(1)}, f32[96,128]{1,0:T(8,128)S(1)}, u32[]{:S(2)}, u32[]{:S(2)}) collective-permute-start(f32[96,128]{1,0:T(8,128)S(1)} %get-tuple-element.75), channel_id=1, source_target_pairs={{0,1},{1,0},{2,3},{3,2},{4,5},{5,4},{6,7},{7,6},{8,9},{9,8},{10,11... | collective-permute-start | bytes 147464 | tf_op jit(solution)/shard_map/ppermute | solution.py:281
  87.2 18.6 %collective-permute-start.21 = (f32[768,128]{1,0:T(8,128)S(1)}, f32[768,128]{1,0:T(8,128)S(1)}, u32[]{:S(2)}, u32[]{:S(2)}) collective-permute-start(f32[768,128]{1,0:T(8,128)S(1)} %get-tuple-element.85.refs_4_), channel_id=1, source_target_pairs={{0,8},{8,0},{16,24},{24,16},{1,9},{9,1},{17,25},{25,17},{2,10},{10... | collective-permute-start | bytes 1179656 | tf_op jit(solution)/shard_map/ppermute | solution.py:281
  87.8 18.0 %collective-permute-start.22 = (f32[768,128]{1,0:T(8,128)S(1)}, f32[768,128]{1,0:T(8,128)S(1)}, u32[]{:S(2)}, u32[]{:S(2)}) collective-permute-start(f32[768,128]{1,0:T(8,128)S(1)} %get-tuple-element.87.refs_3_), channel_id=1, source_target_pairs={{0,16},{8,24},{16,0},{24,8},{1,17},{9,25},{17,1},{25,9},{2,18},{10... | collective-permute-start | bytes 1179656 | tf_op jit(solution)/shard_map/ppermute | solution.py:281
  92.4 15.3 %collective-permute-start.23 = (f32[768,128]{1,0:T(8,128)S(1)}, f32[768,128]{1,0:T(8,128)S(1)}, u32[]{:S(2)}, u32[]{:S(2)}) collective-permute-start(f32[768,128]{1,0:T(8,128)S(1)} %collective-permute-done.17.refs_5_), channel_id=1, source_target_pairs={{0,16},{8,24},{16,0},{24,8},{1,17},{9,25},{17,1},{25,9},{2,18},{10... | collective-permute-start | bytes 1179656 | tf_op jit(solution)/shard_map/ppermute | solution.py:281
  93.4 14.3 %collective-permute-start.25 = (f32[768,128]{1,0:T(8,128)S(1)}, f32[768,128]{1,0:T(8,128)S(1)}, u32[]{:S(2)}, u32[]{:S(2)}) collective-permute-start(f32[768,128]{1,0:T(8,128)S(1)} %collective-permute-done.18.refs_6_), channel_id=1, source_target_pairs={{0,8},{8,0},{16,24},{24,16},{1,9},{9,1},{17,25},{25,17},{2,10},{10... | collective-permute-start | bytes 1179656 | tf_op jit(solution)/shard_map/ppermute | solution.py:281
  95.0 4.1 %collective-permute-start.19 = (f32[96,128]{1,0:T(8,128)S(1)}, f32[96,128]{1,0:T(8,128)S(1)}, u32[]{:S(2)}, u32[]{:S(2)}) collective-permute-start(f32[96,128]{1,0:T(8,128)S(1)} %add.54), channel_id=1, source_target_pairs={{0,2},{1,3},{2,0},{3,1},{4,6},{5,7},{6,4},{7,5},{8,10},{9,11},{10,... | collective-permute-start | bytes 147464 | tf_op jit(solution)/shard_map/ppermute | solution.py:281
  99.1 6.6 %collective-permute-start.20 = (f32[96,128]{1,0:T(8,128)S(1)}, f32[96,128]{1,0:T(8,128)S(1)}, u32[]{:S(2)}, u32[]{:S(2)}) collective-permute-start(f32[96,128]{1,0:T(8,128)S(1)} %add.55), channel_id=1, source_target_pairs={{0,4},{1,5},{2,6},{3,7},{4,0},{5,1},{6,2},{7,3},{8,12},{9,13},{10,... | collective-permute-start | bytes 147464 | tf_op jit(solution)/shard_map/ppermute | solution.py:281
  105.7 1.3 %collective-permute-start.24 = (f32[96,128]{1,0:T(8,128)S(1)}, f32[96,128]{1,0:T(8,128)S(1)}, u32[]{:S(2)}, u32[]{:S(2)}) collective-permute-start(f32[96,128]{1,0:T(8,128)S(1)} %add.56.refs_2_), channel_id=1, source_target_pairs={{0,1},{1,0},{2,3},{3,2},{4,5},{5,4},{6,7},{7,6},{8,9},{9,8},{10,11... | collective-permute-start | bytes 147464 | tf_op jit(solution)/shard_map/ppermute | solution.py:281
  108.6 1.3 %collective-permute-start.26 = (f32[96,128]{1,0:T(8,128)S(1)}, f32[96,128]{1,0:T(8,128)S(1)}, u32[]{:S(2)}, u32[]{:S(2)}) collective-permute-start(f32[96,128]{1,0:T(8,128)S(1)} %get-tuple-element.94), channel_id=1, source_target_pairs={{0,1},{1,0},{2,3},{3,2},{4,5},{5,4},{6,7},{7,6},{8,9},{9,8},{10,11... | collective-permute-start | bytes 147464 | tf_op jit(solution)/shard_map/ppermute | solution.py:281
  109.9 7.7 %collective-permute-start.29 = (f32[96,128]{1,0:T(8,128)S(1)}, f32[96,128]{1,0:T(8,128)S(1)}, u32[]{:S(2)}, u32[]{:S(2)}) collective-permute-start(f32[96,128]{1,0:T(8,128)S(1)} %add.57), channel_id=1, source_target_pairs={{0,4},{1,5},{2,6},{3,7},{4,0},{5,1},{6,2},{7,3},{8,12},{9,13},{10,... | collective-permute-start | bytes 147464 | tf_op jit(solution)/shard_map/ppermute | solution.py:281
  112.6 6.2 %collective-permute-start.28 = (f32[96,128]{1,0:T(8,128)S(1)}, f32[96,128]{1,0:T(8,128)S(1)}, u32[]{:S(2)}, u32[]{:S(2)}) collective-permute-start(f32[96,128]{1,0:T(8,128)S(1)} %add.57), channel_id=1, source_target_pairs={{0,6},{1,7},{2,4},{3,5},{4,2},{5,3},{6,0},{7,1},{8,14},{9,15},{10,... | collective-permute-start | bytes 147464 | tf_op jit(solution)/shard_map/ppermute | solution.py:281
  114.3 4.6 %collective-permute-start.27 = (f32[96,128]{1,0:T(8,128)S(1)}, f32[96,128]{1,0:T(8,128)S(1)}, u32[]{:S(2)}, u32[]{:S(2)}) collective-permute-start(f32[96,128]{1,0:T(8,128)S(1)} %add.57), channel_id=1, source_target_pairs={{0,2},{1,3},{2,0},{3,1},{4,6},{5,7},{6,4},{7,5},{8,10},{9,11},{10,... | collective-permute-start | bytes 147464 | tf_op jit(solution)/shard_map/ppermute | solution.py:281
  118.9 1.3 %collective-permute-start.30 = (f32[96,128]{1,0:T(8,128)S(1)}, f32[96,128]{1,0:T(8,128)S(1)}, u32[]{:S(2)}, u32[]{:S(2)}) collective-permute-start(f32[96,128]{1,0:T(8,128)S(1)} %add_add_fusion.refs_0_), channel_id=1, source_target_pairs={{0,1},{1,0},{2,3},{3,2},{4,5},{5,4},{6,7},{7,6},{8,9},{9,8},{10,11... | collective-permute-start | bytes 147464 | tf_op jit(solution)/shard_map/ppermute | solution.py:281
  (10 other events, 49.0 us)

commit v4 on v3

--- a/solution.py
+++ b/solution.py
@@ -363,7 +363,7 @@
                     total = total + mode_exchange(total, mode_size, mask)
         if c:
             other = mode_exchange(total, mode_size, 1)
-            tied(chunk, far, total, *([other] if last else []))
+            tied(chunk, far, total)
             sums[-1] = total, other, intensity[:, slice(*spans[c - 1])]
         kept, sent = fields(chunk, far, len(near + side), total=side_total, last=True)
         waits = [side_total, *(chunks[c + 1][place] for place in near[:2])] if not last else []
@@ -400,7 +400,7 @@
         square = (
             row_size == 4
             and mode_size & (mode_size - 1) == 0
-            and mode_size > 1
+            and mode_size > 2
             and probes.shape[1] % (2 * LANES) == 0
             and probes.shape[2] % LANES == 0
             and probes.shape[2] >= 2 * LAST_PROBES

time: 126 us -> 126 us (level)
  transfers between devices with their start and end apart: 31 -> 31, of which waited for: 17 -> 16; matrix products, arithmetic and copies ran while one was open for 0% -> 0% of each run, Pallas kernels for 26% -> 26%
where the time goes in v4:
time: 126 us; the launch traced here: 125 us
  Pallas kernels  40.1 us (32%)
  waiting for transfers between devices  38.4 us (30%)
  starting transfers between devices  36.2 us (29%)
  local copies, waits for them, and re-layouts  9.99 us (8%)
    ppermute x31, waiting for transfers between devices, exchange(): return lax.ppermute(value, axis, [(i, i ^ mask) for i in range(size)])  38.4 us
    ppermute x31, starting transfers between devices, exchange(): return lax.ppermute(value, axis, [(i, i ^ mask) for i in range(size)])  36.2 us
    pallas_call x9, Pallas kernels, add_fields(): pl.pallas_call(functools.partial(fields_kernel, first, widths, total is n...  13.7 us
    unnamed x22, local copies, waits for them, and re-layouts  9.81 us
    pallas_call x3, Pallas kernels, gradient_part(): pl.pallas_call(functools.partial(part_kernel, 1.0 / count, len(parts)), i...  9.74 us
    pallas_call x1, Pallas kernels, matrix_halves(): pl.pallas_call(matrix_kernel, grid_spec=pltpu.PrefetchScalarGridSpec(num_...  7.24 us
    pallas_call x1, Pallas kernels, last_gradient(): pl.pallas_call(functools.partial(last_kernel, 1.0 / count), in_specs=[SME...  4.94 us
    pallas_call x3, Pallas kernels, probe_chunk(): pl.pallas_call(functools.partial(chunk_kernel, low, high), in_specs=[pl.B...  4.45 us
  transfers between devices with their start and end apart: 31, of which 16 were waited for; matrix products, arithmetic and copies ran while one was open for 0% of the time, Pallas kernels for 26%

profile of v4, /device:TPU:0, one launch (start us, length us, event | category | flops | bytes accessed | tf_op | source)
XLA Modules:
  0.0 125.3 jit_solution(5029608011991462534)
XLA Ops:
  1.4 3.0 %collective-permute-start = (f32[768,256]{1,0:T(8,128)S(1)}, f32[768,256]{1,0:T(8,128)}, u32[]{:S(2)}, u32[]{:S(2)}) collective-permute-start(f32[768,256]{1,0:T(8,128)S(1)} %get-tuple-element.54.refs_3_), channel_id=1, source_target_pairs={{0,8},{8,0},{16,24},{24,16},{1,9},{9,1},{17,25},{25,17},{2,10},{10... | collective-permute-start | bytes 2359304 | tf_op jit(solution)/shard_map/ppermute | solution.py:281
  6.6 7.2 %shard_map.37 = (bf16[384,6144]{1,0:T(8,128)(2,1)S(1)}, bf16[384,6144]{1,0:T(8,128)(2,1)S(1)}) custom-call(s32[8]{0:T(128)S(1)} %stack.35.order_ref, f32[2,192,6144]{2,1,0:T(8,128)} %matrix_ref.1), custom_call_target="tpu_custom_call" | custom-call | flops 1000 | bytes 1000 | tf_op jit(solution)/shard_map/pallas_call | solution.py:104
  13.9 2.2 %copy-done = bf16[384,6144]{1,0:T(8,128)(2,1)} copy-done((bf16[384,6144]{1,0:T(8,128)(2,1)}, bf16[384,6144]{1,0:T(8,128)(2,1)S(1)}, u32[]{:S(2)}) %copy-start) | copy-done | bytes 4718616
  16.1 2.2 %copy-done.2 = bf16[384,6144]{1,0:T(8,128)(2,1)} copy-done((bf16[384,6144]{1,0:T(8,128)(2,1)}, bf16[384,6144]{1,0:T(8,128)(2,1)S(1)}, u32[]{:S(2)}) %copy-start.2) | copy-done | bytes 4718616
  18.2 4.7 %collective-permute-done.refs_5_ = f32[768,256]{1,0:T(8,128)} collective-permute-done((f32[768,256]{1,0:T(8,128)S(1)}, f32[768,256]{1,0:T(8,128)}, u32[]{:S(2)}, u32[]{:S(2)}) %collective-permute-start) | collective-permute-done | bytes 786464 | tf_op jit(solution)/shard_map/ppermute | solution.py:281
  22.9 2.1 %collective-permute-done.1.refs_6_ = f32[768,256]{1,0:T(8,128)} collective-permute-done((f32[768,256]{1,0:T(8,128)S(1)}, f32[768,256]{1,0:T(8,128)}, u32[]{:S(2)}, u32[]{:S(2)}) %collective-permute-start.1) | collective-permute-done | bytes 786464 | tf_op jit(solution)/shard_map/ppermute | solution.py:281
  27.1 1.6 %shard_map.42 = (f32[768,128]{1,0:T(8,128)S(1)}, f32[768,128]{1,0:T(8,128)S(1)}) custom-call(f32[2,1536,256]{2,1,0:T(8,128)} %probes_ref.5), custom_call_target="tpu_custom_call" | custom-call | flops 1000 | bytes 1000 | tf_op jit(solution)/shard_map/pallas_call | solution.py:81
  29.4 2.3 %copy-done.1 = bf16[384,6144]{1,0:T(8,128)(2,1)S(1)} copy-done((bf16[384,6144]{1,0:T(8,128)(2,1)S(1)}, bf16[384,6144]{1,0:T(8,128)(2,1)}, u32[]{:S(2)}) %copy-start.1) | copy-done | bytes 4718616
  31.7 2.3 %copy-done.3 = bf16[384,6144]{1,0:T(8,128)(2,1)S(1)} copy-done((bf16[384,6144]{1,0:T(8,128)(2,1)S(1)}, bf16[384,6144]{1,0:T(8,128)(2,1)}, u32[]{:S(2)}) %copy-start.3) | copy-done | bytes 4718616
  34.1 3.4 %shard_map.39.refs_1_ = f32[2,192,128]{2,1,0:T(8,128)S(1)} custom-call(s32[1]{0:T(128)} %bitcast.refs_0_.core_ref, bf16[384,6144]{1,0:T(8,128)(2,1)S(1)} %copy-done.1, bf16[384,6144]{1,0:T(8,128)(2,1)S(1)} %copy-done.3, f32[768,256]{1,0:T(8,128)S(1)} %get-tuple-element.54.refs_3_, f32[768,256]{1,0:T(8,128)S(1)} %get-tuple-element.55.refs_4_, ...), custom_call_target="tpu_custom_call" | custom-call | flops 1000 | bytes 1000 | tf_op jit(solution)/shard_map/pallas_call | solution.py:188
  37.5 2.2 %collective-permute-done.2.refs_4_.refs_3_ = f32[768,256]{1,0:T(8,128)S(1)} collective-permute-done((f32[768,256]{1,0:T(8,128)S(1)}, f32[768,256]{1,0:T(8,128)S(1)}, u32[]{:S(2)}, u32[]{:S(2)}) %collective-permute-start.2) | collective-permute-done | bytes 786464 | tf_op jit(solution)/shard_map/ppermute | solution.py:281
  39.7 2.1 %collective-permute-done.3.refs_5_.refs_4_ = f32[768,256]{1,0:T(8,128)S(1)} collective-permute-done((f32[768,256]{1,0:T(8,128)S(1)}, f32[768,256]{1,0:T(8,128)S(1)}, u32[]{:S(2)}, u32[]{:S(2)}) %collective-permute-start.3) | collective-permute-done | bytes 786464 | tf_op jit(solution)/shard_map/ppermute | solution.py:281
  43.0 2.0 %collective-permute-start.8 = (f32[768,128]{1,0:T(8,128)S(1)}, f32[768,128]{1,0:T(8,128)S(1)}, u32[]{:S(2)}, u32[]{:S(2)}) collective-permute-start(f32[768,128]{1,0:T(8,128)S(1)} %copy-done.5), channel_id=1, source_target_pairs={{0,16},{8,24},{16,0},{24,8},{1,17},{9,25},{17,1},{25,9},{2,18},{10... | collective-permute-start | bytes 1179656 | tf_op jit(solution)/shard_map/ppermute | solution.py:281
  45.0 13.7 %collective-permute-done.4.refs_4_.refs_5_ = f32[768,256]{1,0:T(8,128)} collective-permute-done((f32[768,256]{1,0:T(8,128)}, f32[768,256]{1,0:T(8,128)}, u32[]{:S(2)}, u32[]{:S(2)}) %collective-permute-start.4) | collective-permute-done | bytes 786464 | tf_op jit(solution)/shard_map/ppermute | solution.py:281
  58.7 2.5 %shard_map.41 = (f32[192,128]{1,0:T(8,128)S(1)}, f32[192,128]{1,0:T(8,128)S(1)}) custom-call(s32[1]{0:T(128)} %bitcast.refs_0_.core_ref, f32[2,192,128]{2,1,0:T(8,128)S(1)} %shard_map.40.refs_1_, bf16[384,6144]{1,0:T(8,128)(2,1)S(1)} %copy-done.1, bf16[384,6144]{1,0:T(8,128)(2,1)S(1)} %copy-done.3, f32[768,256]{1,0:T(8,128)} %collective-permute-done.4.refs_4_.refs_5_, ...), custom_call_target="tpu_custom_call" | custom-call | flops 1000 | bytes 1000 | tf_op jit(solution)/shard_map/pallas_call | solution.py:188
  62.7 2.0 %collective-permute-start.11 = (f32[768,128]{1,0:T(8,128)S(1)}, f32[768,128]{1,0:T(8,128)S(1)}, u32[]{:S(2)}, u32[]{:S(2)}) collective-permute-start(f32[768,128]{1,0:T(8,128)S(1)} %get-tuple-element.67.refs_3_.refs_5_), channel_id=1, source_target_pairs={{0,16},{8,24},{16,0},{24,8},{1,17},{9,25},{17,1},{25,9},{2,18},{10... | collective-permute-start | bytes 1179656 | tf_op jit(solution)/shard_map/ppermute | solution.py:281
  65.6 1.5 %shard_map.43.refs_1_ = f32[2,192,64]{2,1,0:T(8,128)S(1)} custom-call(s32[1]{0:T(128)} %bitcast.refs_0_.core_ref, bf16[384,6144]{1,0:T(8,128)(2,1)S(1)} %copy-done.1, bf16[384,6144]{1,0:T(8,128)(2,1)S(1)} %copy-done.3, f32[768,128]{1,0:T(8,128)S(1)} %get-tuple-element.67.refs_3_.refs_5_, f32[768,128]{1,0:T(8,128)S(1)} %copy-done.5, ...), custom_call_target="tpu_custom_call" | custom-call | flops 1000 | bytes 1000 | tf_op jit(solution)/shard_map/pallas_call | solution.py:188
  67.2 1.6 %collective-permute-start.9 = (f32[192,128]{1,0:T(8,128)S(1)}, f32[192,128]{1,0:T(8,128)S(1)}, u32[]{:S(2)}, u32[]{:S(2)}) collective-permute-start(f32[192,128]{1,0:T(8,128)S(1)} %add.51), channel_id=1, source_target_pairs={{0,2},{1,3},{2,0},{3,1},{4,6},{5,7},{6,4},{7,5},{8,10},{9,11},{10,... | collective-permute-start | bytes 294920 | tf_op jit(solution)/shard_map/ppermute | solution.py:281
  72.3 2.3 %collective-permute-done.10.refs_4_.refs_9_ = f32[768,128]{1,0:T(8,128)S(1)} collective-permute-done((f32[768,128]{1,0:T(8,128)S(1)}, f32[768,128]{1,0:T(8,128)S(1)}, u32[]{:S(2)}, u32[]{:S(2)}) %collective-permute-start.10) | collective-permute-done | bytes 393248 | tf_op jit(solution)/shard_map/ppermute | solution.py:281
  75.6 2.1 %collective-permute-start.17 = (f32[768,128]{1,0:T(8,128)S(1)}, f32[768,128]{1,0:T(8,128)S(1)}, u32[]{:S(2)}, u32[]{:S(2)}) collective-permute-start(f32[768,128]{1,0:T(8,128)S(1)} %get-tuple-element.87.refs_3_), channel_id=1, source_target_pairs={{0,8},{8,0},{16,24},{24,16},{1,9},{9,1},{17,25},{25,17},{2,10},{10... | collective-permute-start | bytes 1179656 | tf_op jit(solution)/shard_map/ppermute | solution.py:281
  79.2 2.6 %collective-permute-start.12 = (f32[192,128]{1,0:T(8,128)S(1)}, f32[192,128]{1,0:T(8,128)S(1)}, u32[]{:S(2)}, u32[]{:S(2)}) collective-permute-start(f32[192,128]{1,0:T(8,128)S(1)} %add.52), channel_id=1, source_target_pairs={{0,4},{1,5},{2,6},{3,7},{4,0},{5,1},{6,2},{7,3},{8,12},{9,13},{10,... | collective-permute-start | bytes 294920 | tf_op jit(solution)/shard_map/ppermute | solution.py:281
  81.8 2.9 %collective-permute-done.12 = f32[192,128]{1,0:T(8,128)S(1)} collective-permute-done((f32[192,128]{1,0:T(8,128)S(1)}, f32[192,128]{1,0:T(8,128)S(1)}, u32[]{:S(2)}, u32[]{:S(2)}) %collective-permute-start.12) | collective-permute-done | bytes 98336 | tf_op jit(solution)/shard_map/ppermute | solution.py:281
  88.9 3.4 %shard_map.46.refs_0_ = f32[2,192,3072]{2,1,0:T(8,128)S(1)} custom-call(s32[1]{0:T(128)} %bitcast.refs_0_.core_ref, f32[192,128]{1,0:T(8,128)S(1)} %add.53.refs_0_, f32[192,128]{1,0:T(8,128)S(1)} %collective-permute-done.16.refs_1_, f32[192,128]{1,0:T(8,128)S(1)} %slice.9.refs_2_, f32[768,256]{1,0:T(8,128)S(1)} %get-tuple-element.54.refs_3_, ...), custom_call_target="tpu_custom_call" | custom-call | flops 1000 | bytes 1000 | tf_op jit(solution)/shard_map/pallas_call | solution.py:239
  93.4 1.6 %collective-permute-start.24 = (f32[768,128]{1,0:T(8,128)S(1)}, f32[768,128]{1,0:T(8,128)S(1)}, u32[]{:S(2)}, u32[]{:S(2)}) collective-permute-start(f32[768,128]{1,0:T(8,128)S(1)} %collective-permute-done.18.refs_6_), channel_id=1, source_target_pairs={{0,8},{8,0},{16,24},{24,16},{1,9},{9,1},{17,25},{25,17},{2,10},{10... | collective-permute-start | bytes 1179656 | tf_op jit(solution)/shard_map/ppermute | solution.py:281
  95.0 1.6 %collective-permute-start.19 = (f32[96,128]{1,0:T(8,128)S(1)}, f32[96,128]{1,0:T(8,128)S(1)}, u32[]{:S(2)}, u32[]{:S(2)}) collective-permute-start(f32[96,128]{1,0:T(8,128)S(1)} %add.54), channel_id=1, source_target_pairs={{0,2},{1,3},{2,0},{3,1},{4,6},{5,7},{6,4},{7,5},{8,10},{9,11},{10,... | collective-permute-start | bytes 147464 | tf_op jit(solution)/shard_map/ppermute | solution.py:281
  96.6 1.5 %shard_map.48.refs_1_ = f32[2,192,64]{2,1,0:T(8,128)S(1)} custom-call(s32[1]{0:T(128)} %bitcast.refs_0_.core_ref, bf16[384,6144]{1,0:T(8,128)(2,1)S(1)} %bitcast.10, bf16[384,6144]{1,0:T(8,128)(2,1)S(1)} %bitcast.12, f32[768,128]{1,0:T(8,128)S(1)} %get-tuple-element.87.refs_3_, f32[768,128]{1,0:T(8,128)S(1)} %get-tuple-element.85.refs_4_, ...), custom_call_target="tpu_custom_call" | custom-call | flops 1000 | bytes 1000 | tf_op jit(solution)/shard_map/pallas_call | solution.py:188
  99.1 2.9 %collective-permute-start.20 = (f32[96,128]{1,0:T(8,128)S(1)}, f32[96,128]{1,0:T(8,128)S(1)}, u32[]{:S(2)}, u32[]{:S(2)}) collective-permute-start(f32[96,128]{1,0:T(8,128)S(1)} %add.55), channel_id=1, source_target_pairs={{0,4},{1,5},{2,6},{3,7},{4,0},{5,1},{6,2},{7,3},{8,12},{9,13},{10,... | collective-permute-start | bytes 147464 | tf_op jit(solution)/shard_map/ppermute | solution.py:281
  102.1 3.6 %shard_map.49.refs_1_ = f32[2,192,3072]{2,1,0:T(8,128)S(1)} custom-call(s32[1]{0:T(128)} %bitcast.refs_0_.core_ref, f32[192,128]{1,0:T(8,128)S(1)} %add.53.refs_0_, f32[192,128]{1,0:T(8,128)S(1)} %collective-permute-done.16.refs_1_, f32[192,128]{1,0:T(8,128)S(1)} %slice.9.refs_2_, f32[768,256]{1,0:T(8,128)S(1)} %collective-permute-done.2.refs_4_.refs_3_, ...), custom_call_target="tpu_custom_call" | custom-call | flops 1000 | bytes 1000 | tf_op jit(solution)/shard_map/pallas_call | solution.py:239
  109.9 2.7 %collective-permute-start.29 = (f32[96,128]{1,0:T(8,128)S(1)}, f32[96,128]{1,0:T(8,128)S(1)}, u32[]{:S(2)}, u32[]{:S(2)}) collective-permute-start(f32[96,128]{1,0:T(8,128)S(1)} %add.57), channel_id=1, source_target_pairs={{0,4},{1,5},{2,6},{3,7},{4,0},{5,1},{6,2},{7,3},{8,12},{9,13},{10,... | collective-permute-start | bytes 147464 | tf_op jit(solution)/shard_map/ppermute | solution.py:281
  112.6 1.6 %collective-permute-start.28 = (f32[96,128]{1,0:T(8,128)S(1)}, f32[96,128]{1,0:T(8,128)S(1)}, u32[]{:S(2)}, u32[]{:S(2)}) collective-permute-start(f32[96,128]{1,0:T(8,128)S(1)} %add.57), channel_id=1, source_target_pairs={{0,6},{1,7},{2,4},{3,5},{4,2},{5,3},{6,0},{7,1},{8,14},{9,15},{10,... | collective-permute-start | bytes 147464 | tf_op jit(solution)/shard_map/ppermute | solution.py:281
  114.8 2.7 %shard_map.52.part_ref = f32[2,192,6144]{2,1,0:T(8,128)S(1)} custom-call(s32[1]{0:T(128)} %bitcast.refs_0_.core_ref, f32[2,192,3072]{2,1,0:T(8,128)S(1)} %shard_map.46.refs_0_, f32[2,192,3072]{2,1,0:T(8,128)S(1)} %shard_map.49.refs_1_, f32[96,128]{1,0:T(8,128)S(1)} %add.56.refs_2_, f32[96,128]{1,0:T(8,128)S(1)} %collective-permute-done.26.refs_3_, ...), custom_call_target="tpu_custom_call" | custom-call | flops 1000 | bytes 1000 | tf_op jit(solution)/shard_map/pallas_call | solution.py:239
  120.2 4.9 %shard_map.53 = f32[2,192,6144]{2,1,0:T(8,128)} custom-call(s32[1]{0:T(128)} %bitcast.refs_0_.core_ref, s32[8]{0:T(128)S(1)} %stack.35.order_ref, f32[2,192,6144]{2,1,0:T(8,128)S(1)} %shard_map.52.part_ref, f32[96,128]{1,0:T(8,128)S(1)} %add_add_fusion.refs_0_, f32[96,128]{1,0:T(8,128)S(1)} %collective-permute-done.30.refs_1_, ...), custom_call_target="tpu_custom_call" | custom-call | flops 1000 | bytes 1000 | tf_op jit(solution)/shard_map/pallas_call | solution.py:269
  (82 shorter events, 29.6 us)
Async XLA Ops:
  1.4 21.5 %collective-permute-start = (f32[768,256]{1,0:T(8,128)S(1)}, f32[768,256]{1,0:T(8,128)}, u32[]{:S(2)}, u32[]{:S(2)}) collective-permute-start(f32[768,256]{1,0:T(8,128)S(1)} %get-tuple-element.54.refs_3_), channel_id=1, source_target_pairs={{0,8},{8,0},{16,24},{24,16},{1,9},{9,1},{17,25},{25,17},{2,10},{10... | collective-permute-start | bytes 2359304 | tf_op jit(solution)/shard_map/ppermute | solution.py:281
  4.4 20.6 %collective-permute-start.1 = (f32[768,256]{1,0:T(8,128)S(1)}, f32[768,256]{1,0:T(8,128)}, u32[]{:S(2)}, u32[]{:S(2)}) collective-permute-start(f32[768,256]{1,0:T(8,128)S(1)} %get-tuple-element.55.refs_4_), channel_id=1, source_target_pairs={{0,16},{8,24},{16,0},{24,8},{1,17},{9,25},{17,1},{25,9},{2,18},{10... | collective-permute-start | bytes 2359304 | tf_op jit(solution)/shard_map/ppermute | solution.py:281
  6.0 33.7 %collective-permute-start.2 = (f32[768,256]{1,0:T(8,128)S(1)}, f32[768,256]{1,0:T(8,128)S(1)}, u32[]{:S(2)}, u32[]{:S(2)}) collective-permute-start(f32[768,256]{1,0:T(8,128)S(1)} %get-tuple-element.55.refs_4_), channel_id=1, source_target_pairs={{0,8},{8,0},{16,24},{24,16},{1,9},{9,1},{17,25},{25,17},{2,10},{10... | collective-permute-start | bytes 2359304 | tf_op jit(solution)/shard_map/ppermute | solution.py:281
  6.5 35.3 %collective-permute-start.3 = (f32[768,256]{1,0:T(8,128)S(1)}, f32[768,256]{1,0:T(8,128)S(1)}, u32[]{:S(2)}, u32[]{:S(2)}) collective-permute-start(f32[768,256]{1,0:T(8,128)S(1)} %get-tuple-element.54.refs_3_), channel_id=1, source_target_pairs={{0,16},{8,24},{16,0},{24,8},{1,17},{9,25},{17,1},{25,9},{2,18},{10... | collective-permute-start | bytes 2359304 | tf_op jit(solution)/shard_map/ppermute | solution.py:281
  25.0 33.7 %collective-permute-start.4 = (f32[768,256]{1,0:T(8,128)}, f32[768,256]{1,0:T(8,128)}, u32[]{:S(2)}, u32[]{:S(2)}) collective-permute-start(f32[768,256]{1,0:T(8,128)} %collective-permute-done.refs_5_), channel_id=1, source_target_pairs={{0,16},{8,24},{16,0},{24,8},{1,17},{9,25},{17,1},{25,9},{2,18},{10... | collective-permute-start | bytes 2359304 | tf_op jit(solution)/shard_map/ppermute | solution.py:281
  26.5 32.2 %collective-permute-start.5 = (f32[768,256]{1,0:T(8,128)}, f32[768,256]{1,0:T(8,128)}, u32[]{:S(2)}, u32[]{:S(2)}) collective-permute-start(f32[768,256]{1,0:T(8,128)} %collective-permute-done.1.refs_6_), channel_id=1, source_target_pairs={{0,8},{8,0},{16,24},{24,16},{1,9},{9,1},{17,25},{25,17},{2,10},{10... | collective-permute-start | bytes 2359304 | tf_op jit(solution)/shard_map/ppermute | solution.py:281
  42.8 21.8 %collective-permute-start.7 = (f32[768,128]{1,0:T(8,128)S(1)}, f32[768,128]{1,0:T(8,128)S(1)}, u32[]{:S(2)}, u32[]{:S(2)}) collective-permute-start(f32[768,128]{1,0:T(8,128)S(1)} %get-tuple-element.67.refs_3_.refs_5_), channel_id=1, source_target_pairs={{0,8},{8,0},{16,24},{24,16},{1,9},{9,1},{17,25},{25,17},{2,10},{10... | collective-permute-start | bytes 1179656 | tf_op jit(solution)/shard_map/ppermute | solution.py:281
  43.0 22.7 %collective-permute-start.8 = (f32[768,128]{1,0:T(8,128)S(1)}, f32[768,128]{1,0:T(8,128)S(1)}, u32[]{:S(2)}, u32[]{:S(2)}) collective-permute-start(f32[768,128]{1,0:T(8,128)S(1)} %copy-done.5), channel_id=1, source_target_pairs={{0,16},{8,24},{16,0},{24,8},{1,17},{9,25},{17,1},{25,9},{2,18},{10... | collective-permute-start | bytes 1179656 | tf_op jit(solution)/shard_map/ppermute | solution.py:281
  61.2 1.4 %collective-permute-start.6 = (f32[192,128]{1,0:T(8,128)S(1)}, f32[192,128]{1,0:T(8,128)S(1)}, u32[]{:S(2)}, u32[]{:S(2)}) collective-permute-start(f32[192,128]{1,0:T(8,128)S(1)} %get-tuple-element.59), channel_id=1, source_target_pairs={{0,1},{1,0},{2,3},{3,2},{4,5},{5,4},{6,7},{7,6},{8,9},{9,8},{10,11... | collective-permute-start | bytes 294920 | tf_op jit(solution)/shard_map/ppermute | solution.py:281
  62.6 12.0 %collective-permute-start.10 = (f32[768,128]{1,0:T(8,128)S(1)}, f32[768,128]{1,0:T(8,128)S(1)}, u32[]{:S(2)}, u32[]{:S(2)}) collective-permute-start(f32[768,128]{1,0:T(8,128)S(1)} %copy-done.5), channel_id=1, source_target_pairs={{0,8},{8,0},{16,24},{24,16},{1,9},{9,1},{17,25},{25,17},{2,10},{10... | collective-permute-start | bytes 1179656 | tf_op jit(solution)/shard_map/ppermute | solution.py:281
  62.7 12.0 %collective-permute-start.11 = (f32[768,128]{1,0:T(8,128)S(1)}, f32[768,128]{1,0:T(8,128)S(1)}, u32[]{:S(2)}, u32[]{:S(2)}) collective-permute-start(f32[768,128]{1,0:T(8,128)S(1)} %get-tuple-element.67.refs_3_.refs_5_), channel_id=1, source_target_pairs={{0,16},{8,24},{16,0},{24,8},{1,17},{9,25},{17,1},{25,9},{2,18},{10... | collective-permute-start | bytes 1179656 | tf_op jit(solution)/shard_map/ppermute | solution.py:281
  67.2 5.1 %collective-permute-start.9 = (f32[192,128]{1,0:T(8,128)S(1)}, f32[192,128]{1,0:T(8,128)S(1)}, u32[]{:S(2)}, u32[]{:S(2)}) collective-permute-start(f32[192,128]{1,0:T(8,128)S(1)} %add.51), channel_id=1, source_target_pairs={{0,2},{1,3},{2,0},{3,1},{4,6},{5,7},{6,4},{7,5},{8,10},{9,11},{10,... | collective-permute-start | bytes 294920 | tf_op jit(solution)/shard_map/ppermute | solution.py:281
  68.7 16.1 %collective-permute-start.13 = (f32[768,128]{1,0:T(8,128)S(1)}, f32[768,128]{1,0:T(8,128)S(1)}, u32[]{:S(2)}, u32[]{:S(2)}) collective-permute-start(f32[768,128]{1,0:T(8,128)S(1)} %collective-permute-done.7.refs_5_.refs_7_), channel_id=1, source_target_pairs={{0,16},{8,24},{16,0},{24,8},{1,17},{9,25},{17,1},{25,9},{2,18},{10... | collective-permute-start | bytes 1179656 | tf_op jit(solution)/shard_map/ppermute | solution.py:281
  70.3 14.6 %collective-permute-start.14 = (f32[768,128]{1,0:T(8,128)S(1)}, f32[768,128]{1,0:T(8,128)S(1)}, u32[]{:S(2)}, u32[]{:S(2)}) collective-permute-start(f32[768,128]{1,0:T(8,128)S(1)} %collective-permute-done.8.refs_6_.refs_8_), channel_id=1, source_target_pairs={{0,8},{8,0},{16,24},{24,16},{1,9},{9,1},{17,25},{25,17},{2,10},{10... | collective-permute-start | bytes 1179656 | tf_op jit(solution)/shard_map/ppermute | solution.py:281
  75.6 16.8 %collective-permute-start.17 = (f32[768,128]{1,0:T(8,128)S(1)}, f32[768,128]{1,0:T(8,128)S(1)}, u32[]{:S(2)}, u32[]{:S(2)}) collective-permute-start(f32[768,128]{1,0:T(8,128)S(1)} %get-tuple-element.87.refs_3_), channel_id=1, source_target_pairs={{0,8},{8,0},{16,24},{24,16},{1,9},{9,1},{17,25},{25,17},{2,10},{10... | collective-permute-start | bytes 1179656 | tf_op jit(solution)/shard_map/ppermute | solution.py:281
  77.6 14.7 %collective-permute-start.18 = (f32[768,128]{1,0:T(8,128)S(1)}, f32[768,128]{1,0:T(8,128)S(1)}, u32[]{:S(2)}, u32[]{:S(2)}) collective-permute-start(f32[768,128]{1,0:T(8,128)S(1)} %get-tuple-element.85.refs_4_), channel_id=1, source_target_pairs={{0,16},{8,24},{16,0},{24,8},{1,17},{9,25},{17,1},{25,9},{2,18},{10... | collective-permute-start | bytes 1179656 | tf_op jit(solution)/shard_map/ppermute | solution.py:281
  79.2 5.5 %collective-permute-start.12 = (f32[192,128]{1,0:T(8,128)S(1)}, f32[192,128]{1,0:T(8,128)S(1)}, u32[]{:S(2)}, u32[]{:S(2)}) collective-permute-start(f32[192,128]{1,0:T(8,128)S(1)} %add.52), channel_id=1, source_target_pairs={{0,4},{1,5},{2,6},{3,7},{4,0},{5,1},{6,2},{7,3},{8,12},{9,13},{10,... | collective-permute-start | bytes 294920 | tf_op jit(solution)/shard_map/ppermute | solution.py:281
  84.7 11.9 %slice-start.2 = ((s8[4718592]{0:T(1024)(128)(4,1)}), s8[4194304]{0:T(1024)(128)(4,1)S(1)}, s32[]{:S(2)}) async-start(s8[4718592]{0:T(1024)(128)(4,1)} %bitcast.11), calls=%async_computation.2 | async-start | bytes 8388608
  84.7 4.2 %collective-permute-start.16 = (f32[192,128]{1,0:T(8,128)S(1)}, f32[192,128]{1,0:T(8,128)S(1)}, u32[]{:S(2)}, u32[]{:S(2)}) collective-permute-start(f32[192,128]{1,0:T(8,128)S(1)} %add.53.refs_0_), channel_id=1, source_target_pairs={{0,1},{1,0},{2,3},{3,2},{4,5},{5,4},{6,7},{7,6},{8,9},{9,8},{10,11... | collective-permute-start | bytes 294920 | tf_op jit(solution)/shard_map/ppermute | solution.py:281
  85.8 1.4 %collective-permute-start.15 = (f32[96,128]{1,0:T(8,128)S(1)}, f32[96,128]{1,0:T(8,128)S(1)}, u32[]{:S(2)}, u32[]{:S(2)}) collective-permute-start(f32[96,128]{1,0:T(8,128)S(1)} %get-tuple-element.75), channel_id=1, source_target_pairs={{0,1},{1,0},{2,3},{3,2},{4,5},{5,4},{6,7},{7,6},{8,9},{9,8},{10,11... | collective-permute-start | bytes 147464 | tf_op jit(solution)/shard_map/ppermute | solution.py:281
  87.2 18.5 %collective-permute-start.21 = (f32[768,128]{1,0:T(8,128)S(1)}, f32[768,128]{1,0:T(8,128)S(1)}, u32[]{:S(2)}, u32[]{:S(2)}) collective-permute-start(f32[768,128]{1,0:T(8,128)S(1)} %get-tuple-element.85.refs_4_), channel_id=1, source_target_pairs={{0,8},{8,0},{16,24},{24,16},{1,9},{9,1},{17,25},{25,17},{2,10},{10... | collective-permute-start | bytes 1179656 | tf_op jit(solution)/shard_map/ppermute | solution.py:281
  87.8 17.9 %collective-permute-start.22 = (f32[768,128]{1,0:T(8,128)S(1)}, f32[768,128]{1,0:T(8,128)S(1)}, u32[]{:S(2)}, u32[]{:S(2)}) collective-permute-start(f32[768,128]{1,0:T(8,128)S(1)} %get-tuple-element.87.refs_3_), channel_id=1, source_target_pairs={{0,16},{8,24},{16,0},{24,8},{1,17},{9,25},{17,1},{25,9},{2,18},{10... | collective-permute-start | bytes 1179656 | tf_op jit(solution)/shard_map/ppermute | solution.py:281
  92.4 15.3 %collective-permute-start.23 = (f32[768,128]{1,0:T(8,128)S(1)}, f32[768,128]{1,0:T(8,128)S(1)}, u32[]{:S(2)}, u32[]{:S(2)}) collective-permute-start(f32[768,128]{1,0:T(8,128)S(1)} %collective-permute-done.17.refs_5_), channel_id=1, source_target_pairs={{0,16},{8,24},{16,0},{24,8},{1,17},{9,25},{17,1},{25,9},{2,18},{10... | collective-permute-start | bytes 1179656 | tf_op jit(solution)/shard_map/ppermute | solution.py:281
  93.4 14.3 %collective-permute-start.24 = (f32[768,128]{1,0:T(8,128)S(1)}, f32[768,128]{1,0:T(8,128)S(1)}, u32[]{:S(2)}, u32[]{:S(2)}) collective-permute-start(f32[768,128]{1,0:T(8,128)S(1)} %collective-permute-done.18.refs_6_), channel_id=1, source_target_pairs={{0,8},{8,0},{16,24},{24,16},{1,9},{9,1},{17,25},{25,17},{2,10},{10... | collective-permute-start | bytes 1179656 | tf_op jit(solution)/shard_map/ppermute | solution.py:281
  95.0 4.1 %collective-permute-start.19 = (f32[96,128]{1,0:T(8,128)S(1)}, f32[96,128]{1,0:T(8,128)S(1)}, u32[]{:S(2)}, u32[]{:S(2)}) collective-permute-start(f32[96,128]{1,0:T(8,128)S(1)} %add.54), channel_id=1, source_target_pairs={{0,2},{1,3},{2,0},{3,1},{4,6},{5,7},{6,4},{7,5},{8,10},{9,11},{10,... | collective-permute-start | bytes 147464 | tf_op jit(solution)/shard_map/ppermute | solution.py:281
  99.1 6.6 %collective-permute-start.20 = (f32[96,128]{1,0:T(8,128)S(1)}, f32[96,128]{1,0:T(8,128)S(1)}, u32[]{:S(2)}, u32[]{:S(2)}) collective-permute-start(f32[96,128]{1,0:T(8,128)S(1)} %add.55), channel_id=1, source_target_pairs={{0,4},{1,5},{2,6},{3,7},{4,0},{5,1},{6,2},{7,3},{8,12},{9,13},{10,... | collective-permute-start | bytes 147464 | tf_op jit(solution)/shard_map/ppermute | solution.py:281
  108.6 1.3 %collective-permute-start.25 = (f32[96,128]{1,0:T(8,128)S(1)}, f32[96,128]{1,0:T(8,128)S(1)}, u32[]{:S(2)}, u32[]{:S(2)}) collective-permute-start(f32[96,128]{1,0:T(8,128)S(1)} %get-tuple-element.94), channel_id=1, source_target_pairs={{0,1},{1,0},{2,3},{3,2},{4,5},{5,4},{6,7},{7,6},{8,9},{9,8},{10,11... | collective-permute-start | bytes 147464 | tf_op jit(solution)/shard_map/ppermute | solution.py:281
  108.7 6.1 %collective-permute-start.26 = (f32[96,128]{1,0:T(8,128)S(1)}, f32[96,128]{1,0:T(8,128)S(1)}, u32[]{:S(2)}, u32[]{:S(2)}) collective-permute-start(f32[96,128]{1,0:T(8,128)S(1)} %add.56.refs_2_), channel_id=1, source_target_pairs={{0,1},{1,0},{2,3},{3,2},{4,5},{5,4},{6,7},{7,6},{8,9},{9,8},{10,11... | collective-permute-start | bytes 147464 | tf_op jit(solution)/shard_map/ppermute | solution.py:281
  109.9 7.7 %collective-permute-start.29 = (f32[96,128]{1,0:T(8,128)S(1)}, f32[96,128]{1,0:T(8,128)S(1)}, u32[]{:S(2)}, u32[]{:S(2)}) collective-permute-start(f32[96,128]{1,0:T(8,128)S(1)} %add.57), channel_id=1, source_target_pairs={{0,4},{1,5},{2,6},{3,7},{4,0},{5,1},{6,2},{7,3},{8,12},{9,13},{10,... | collective-permute-start | bytes 147464 | tf_op jit(solution)/shard_map/ppermute | solution.py:281
  112.6 6.2 %collective-permute-start.28 = (f32[96,128]{1,0:T(8,128)S(1)}, f32[96,128]{1,0:T(8,128)S(1)}, u32[]{:S(2)}, u32[]{:S(2)}) collective-permute-start(f32[96,128]{1,0:T(8,128)S(1)} %add.57), channel_id=1, source_target_pairs={{0,6},{1,7},{2,4},{3,5},{4,2},{5,3},{6,0},{7,1},{8,14},{9,15},{10,... | collective-permute-start | bytes 147464 | tf_op jit(solution)/shard_map/ppermute | solution.py:281
  114.3 4.6 %collective-permute-start.27 = (f32[96,128]{1,0:T(8,128)S(1)}, f32[96,128]{1,0:T(8,128)S(1)}, u32[]{:S(2)}, u32[]{:S(2)}) collective-permute-start(f32[96,128]{1,0:T(8,128)S(1)} %add.57), channel_id=1, source_target_pairs={{0,2},{1,3},{2,0},{3,1},{4,6},{5,7},{6,4},{7,5},{8,10},{9,11},{10,... | collective-permute-start | bytes 147464 | tf_op jit(solution)/shard_map/ppermute | solution.py:281
  118.9 1.3 %collective-permute-start.30 = (f32[96,128]{1,0:T(8,128)S(1)}, f32[96,128]{1,0:T(8,128)S(1)}, u32[]{:S(2)}, u32[]{:S(2)}) collective-permute-start(f32[96,128]{1,0:T(8,128)S(1)} %add_add_fusion.refs_0_), channel_id=1, source_target_pairs={{0,1},{1,0},{2,3},{3,2},{4,5},{5,4},{6,7},{7,6},{8,9},{9,8},{10,11... | collective-permute-start | bytes 147464 | tf_op jit(solution)/shard_map/ppermute | solution.py:281
  (10 other events, 49.0 us)

commit v5 on v3

--- a/solution.py
+++ b/solution.py
@@ -319,7 +319,7 @@
     chunks = [dict(zip(near[:2], probe_chunk(probes, *span))) for span in spans]
     matrix = matrix_halves(transfer_matrix, order, half)
     places = near + side + far
-    bits = [1 << bit for bit in range(1, mode_size.bit_length() - 1)]
+    bits = [1 << bit for bit in reversed(range(1, mode_size.bit_length() - 1))]
     sums, waits, parts = [], [], []
 
     def tied(chunk, places, *earlier):

time: 126 us -> 126 us (level)
  no operation moved by 1% of the time
where the time goes in v5:
time: 126 us; the launch traced here: 125 us
  Pallas kernels  40.1 us (32%)
  waiting for transfers between devices  38.5 us (31%)
  starting transfers between devices  35.9 us (28%)
  local copies, waits for them, and re-layouts  9.99 us (8%)
    ppermute x31, waiting for transfers between devices, exchange(): return lax.ppermute(value, axis, [(i, i ^ mask) for i in range(size)])  38.5 us
    ppermute x31, starting transfers between devices, exchange(): return lax.ppermute(value, axis, [(i, i ^ mask) for i in range(size)])  35.9 us
    pallas_call x9, Pallas kernels, add_fields(): pl.pallas_call(functools.partial(fields_kernel, first, widths, total is n...  13.7 us
    unnamed x22, local copies, waits for them, and re-layouts  9.81 us
    pallas_call x3, Pallas kernels, gradient_part(): pl.pallas_call(functools.partial(part_kernel, 1.0 / count, len(parts)), i...  9.74 us
    pallas_call x1, Pallas kernels, matrix_halves(): pl.pallas_call(matrix_kernel, grid_spec=pltpu.PrefetchScalarGridSpec(num_...  7.24 us
    pallas_call x1, Pallas kernels, last_gradient(): pl.pallas_call(functools.partial(last_kernel, 1.0 / count), in_specs=[SME...  4.94 us
    pallas_call x3, Pallas kernels, probe_chunk(): pl.pallas_call(functools.partial(chunk_kernel, low, high), in_specs=[pl.B...  4.45 us
  transfers between devices with their start and end apart: 31, of which 17 were waited for; matrix products, arithmetic and copies ran while one was open for 0% of the time, Pallas kernels for 26%

profile of v5, /device:TPU:0, one launch (start us, length us, event | category | flops | bytes accessed | tf_op | source)
XLA Modules:
  0.0 125.0 jit_solution(2824103187016185675)
XLA Ops:
  1.4 3.0 %collective-permute-start = (f32[768,256]{1,0:T(8,128)S(1)}, f32[768,256]{1,0:T(8,128)}, u32[]{:S(2)}, u32[]{:S(2)}) collective-permute-start(f32[768,256]{1,0:T(8,128)S(1)} %get-tuple-element.54.refs_3_), channel_id=1, source_target_pairs={{0,8},{8,0},{16,24},{24,16},{1,9},{9,1},{17,25},{25,17},{2,10},{10... | collective-permute-start | bytes 2359304 | tf_op jit(solution)/shard_map/ppermute | solution.py:281
  6.6 7.2 %shard_map.37 = (bf16[384,6144]{1,0:T(8,128)(2,1)S(1)}, bf16[384,6144]{1,0:T(8,128)(2,1)S(1)}) custom-call(s32[8]{0:T(128)S(1)} %stack.35.order_ref, f32[2,192,6144]{2,1,0:T(8,128)} %matrix_ref.1), custom_call_target="tpu_custom_call" | custom-call | flops 1000 | bytes 1000 | tf_op jit(solution)/shard_map/pallas_call | solution.py:104
  13.9 2.2 %copy-done = bf16[384,6144]{1,0:T(8,128)(2,1)} copy-done((bf16[384,6144]{1,0:T(8,128)(2,1)}, bf16[384,6144]{1,0:T(8,128)(2,1)S(1)}, u32[]{:S(2)}) %copy-start) | copy-done | bytes 4718616
  16.1 2.2 %copy-done.2 = bf16[384,6144]{1,0:T(8,128)(2,1)} copy-done((bf16[384,6144]{1,0:T(8,128)(2,1)}, bf16[384,6144]{1,0:T(8,128)(2,1)S(1)}, u32[]{:S(2)}) %copy-start.2) | copy-done | bytes 4718616
  18.2 4.7 %collective-permute-done.refs_5_ = f32[768,256]{1,0:T(8,128)} collective-permute-done((f32[768,256]{1,0:T(8,128)S(1)}, f32[768,256]{1,0:T(8,128)}, u32[]{:S(2)}, u32[]{:S(2)}) %collective-permute-start) | collective-permute-done | bytes 786464 | tf_op jit(solution)/shard_map/ppermute | solution.py:281
  22.9 2.1 %collective-permute-done.1.refs_6_ = f32[768,256]{1,0:T(8,128)} collective-permute-done((f32[768,256]{1,0:T(8,128)S(1)}, f32[768,256]{1,0:T(8,128)}, u32[]{:S(2)}, u32[]{:S(2)}) %collective-permute-start.1) | collective-permute-done | bytes 786464 | tf_op jit(solution)/shard_map/ppermute | solution.py:281
  27.1 1.6 %shard_map.42 = (f32[768,128]{1,0:T(8,128)S(1)}, f32[768,128]{1,0:T(8,128)S(1)}) custom-call(f32[2,1536,256]{2,1,0:T(8,128)} %probes_ref.5), custom_call_target="tpu_custom_call" | custom-call | flops 1000 | bytes 1000 | tf_op jit(solution)/shard_map/pallas_call | solution.py:81
  29.4 2.3 %copy-done.1 = bf16[384,6144]{1,0:T(8,128)(2,1)S(1)} copy-done((bf16[384,6144]{1,0:T(8,128)(2,1)S(1)}, bf16[384,6144]{1,0:T(8,128)(2,1)}, u32[]{:S(2)}) %copy-start.1) | copy-done | bytes 4718616
  31.7 2.3 %copy-done.3 = bf16[384,6144]{1,0:T(8,128)(2,1)S(1)} copy-done((bf16[384,6144]{1,0:T(8,128)(2,1)S(1)}, bf16[384,6144]{1,0:T(8,128)(2,1)}, u32[]{:S(2)}) %copy-start.3) | copy-done | bytes 4718616
  34.1 3.4 %shard_map.39.refs_1_ = f32[2,192,128]{2,1,0:T(8,128)S(1)} custom-call(s32[1]{0:T(128)} %bitcast.refs_0_.core_ref, bf16[384,6144]{1,0:T(8,128)(2,1)S(1)} %copy-done.1, bf16[384,6144]{1,0:T(8,128)(2,1)S(1)} %copy-done.3, f32[768,256]{1,0:T(8,128)S(1)} %get-tuple-element.54.refs_3_, f32[768,256]{1,0:T(8,128)S(1)} %get-tuple-element.55.refs_4_, ...), custom_call_target="tpu_custom_call" | custom-call | flops 1000 | bytes 1000 | tf_op jit(solution)/shard_map/pallas_call | solution.py:188
  37.5 2.2 %collective-permute-done.2.refs_4_.refs_3_ = f32[768,256]{1,0:T(8,128)S(1)} collective-permute-done((f32[768,256]{1,0:T(8,128)S(1)}, f32[768,256]{1,0:T(8,128)S(1)}, u32[]{:S(2)}, u32[]{:S(2)}) %collective-permute-start.2) | collective-permute-done | bytes 786464 | tf_op jit(solution)/shard_map/ppermute | solution.py:281
  39.7 2.1 %collective-permute-done.3.refs_5_.refs_4_ = f32[768,256]{1,0:T(8,128)S(1)} collective-permute-done((f32[768,256]{1,0:T(8,128)S(1)}, f32[768,256]{1,0:T(8,128)S(1)}, u32[]{:S(2)}, u32[]{:S(2)}) %collective-permute-start.3) | collective-permute-done | bytes 786464 | tf_op jit(solution)/shard_map/ppermute | solution.py:281
  43.0 2.0 %collective-permute-start.8 = (f32[768,128]{1,0:T(8,128)S(1)}, f32[768,128]{1,0:T(8,128)S(1)}, u32[]{:S(2)}, u32[]{:S(2)}) collective-permute-start(f32[768,128]{1,0:T(8,128)S(1)} %copy-done.5), channel_id=1, source_target_pairs={{0,16},{8,24},{16,0},{24,8},{1,17},{9,25},{17,1},{25,9},{2,18},{10... | collective-permute-start | bytes 1179656 | tf_op jit(solution)/shard_map/ppermute | solution.py:281
  45.0 13.7 %collective-permute-done.4.refs_4_.refs_5_ = f32[768,256]{1,0:T(8,128)} collective-permute-done((f32[768,256]{1,0:T(8,128)}, f32[768,256]{1,0:T(8,128)}, u32[]{:S(2)}, u32[]{:S(2)}) %collective-permute-start.4) | collective-permute-done | bytes 786464 | tf_op jit(solution)/shard_map/ppermute | solution.py:281
  58.7 2.5 %shard_map.41 = (f32[192,128]{1,0:T(8,128)S(1)}, f32[192,128]{1,0:T(8,128)S(1)}) custom-call(s32[1]{0:T(128)} %bitcast.refs_0_.core_ref, f32[2,192,128]{2,1,0:T(8,128)S(1)} %shard_map.40.refs_1_, bf16[384,6144]{1,0:T(8,128)(2,1)S(1)} %copy-done.1, bf16[384,6144]{1,0:T(8,128)(2,1)S(1)} %copy-done.3, f32[768,256]{1,0:T(8,128)} %collective-permute-done.4.refs_4_.refs_5_, ...), custom_call_target="tpu_custom_call" | custom-call | flops 1000 | bytes 1000 | tf_op jit(solution)/shard_map/pallas_call | solution.py:188
  62.7 2.0 %collective-permute-start.11 = (f32[768,128]{1,0:T(8,128)S(1)}, f32[768,128]{1,0:T(8,128)S(1)}, u32[]{:S(2)}, u32[]{:S(2)}) collective-permute-start(f32[768,128]{1,0:T(8,128)S(1)} %get-tuple-element.67.refs_3_.refs_5_), channel_id=1, source_target_pairs={{0,16},{8,24},{16,0},{24,8},{1,17},{9,25},{17,1},{25,9},{2,18},{10... | collective-permute-start | bytes 1179656 | tf_op jit(solution)/shard_map/ppermute | solution.py:281
  65.6 1.5 %shard_map.43.refs_1_ = f32[2,192,64]{2,1,0:T(8,128)S(1)} custom-call(s32[1]{0:T(128)} %bitcast.refs_0_.core_ref, bf16[384,6144]{1,0:T(8,128)(2,1)S(1)} %copy-done.1, bf16[384,6144]{1,0:T(8,128)(2,1)S(1)} %copy-done.3, f32[768,128]{1,0:T(8,128)S(1)} %get-tuple-element.67.refs_3_.refs_5_, f32[768,128]{1,0:T(8,128)S(1)} %copy-done.5, ...), custom_call_target="tpu_custom_call" | custom-call | flops 1000 | bytes 1000 | tf_op jit(solution)/shard_map/pallas_call | solution.py:188
  67.2 2.6 %collective-permute-start.9 = (f32[192,128]{1,0:T(8,128)S(1)}, f32[192,128]{1,0:T(8,128)S(1)}, u32[]{:S(2)}, u32[]{:S(2)}) collective-permute-start(f32[192,128]{1,0:T(8,128)S(1)} %add.51), channel_id=1, source_target_pairs={{0,4},{1,5},{2,6},{3,7},{4,0},{5,1},{6,2},{7,3},{8,12},{9,13},{10,... | collective-permute-start | bytes 294920 | tf_op jit(solution)/shard_map/ppermute | solution.py:281
  75.6 2.1 %collective-permute-start.17 = (f32[768,128]{1,0:T(8,128)S(1)}, f32[768,128]{1,0:T(8,128)S(1)}, u32[]{:S(2)}, u32[]{:S(2)}) collective-permute-start(f32[768,128]{1,0:T(8,128)S(1)} %get-tuple-element.87.refs_3_), channel_id=1, source_target_pairs={{0,8},{8,0},{16,24},{24,16},{1,9},{9,1},{17,25},{25,17},{2,10},{10... | collective-permute-start | bytes 1179656 | tf_op jit(solution)/shard_map/ppermute | solution.py:281
  79.2 1.6 %collective-permute-start.12 = (f32[192,128]{1,0:T(8,128)S(1)}, f32[192,128]{1,0:T(8,128)S(1)}, u32[]{:S(2)}, u32[]{:S(2)}) collective-permute-start(f32[192,128]{1,0:T(8,128)S(1)} %add.52), channel_id=1, source_target_pairs={{0,2},{1,3},{2,0},{3,1},{4,6},{5,7},{6,4},{7,5},{8,10},{9,11},{10,... | collective-permute-start | bytes 294920 | tf_op jit(solution)/shard_map/ppermute | solution.py:281
  80.7 3.0 %collective-permute-done.12 = f32[192,128]{1,0:T(8,128)S(1)} collective-permute-done((f32[192,128]{1,0:T(8,128)S(1)}, f32[192,128]{1,0:T(8,128)S(1)}, u32[]{:S(2)}, u32[]{:S(2)}) %collective-permute-start.12) | collective-permute-done | bytes 98336 | tf_op jit(solution)/shard_map/ppermute | solution.py:281
  87.4 1.5 %collective-permute-start.22 = (f32[768,128]{1,0:T(8,128)S(1)}, f32[768,128]{1,0:T(8,128)S(1)}, u32[]{:S(2)}, u32[]{:S(2)}) collective-permute-start(f32[768,128]{1,0:T(8,128)S(1)} %get-tuple-element.87.refs_3_), channel_id=1, source_target_pairs={{0,16},{8,24},{16,0},{24,8},{1,17},{9,25},{17,1},{25,9},{2,18},{10... | collective-permute-start | bytes 1179656 | tf_op jit(solution)/shard_map/ppermute | solution.py:281
  88.9 3.4 %shard_map.46.refs_0_ = f32[2,192,3072]{2,1,0:T(8,128)S(1)} custom-call(s32[1]{0:T(128)} %bitcast.refs_0_.core_ref, f32[192,128]{1,0:T(8,128)S(1)} %add.53.refs_0_, f32[192,128]{1,0:T(8,128)S(1)} %collective-permute-done.16.refs_1_, f32[192,128]{1,0:T(8,128)S(1)} %slice.9.refs_2_, f32[768,256]{1,0:T(8,128)S(1)} %get-tuple-element.54.refs_3_, ...), custom_call_target="tpu_custom_call" | custom-call | flops 1000 | bytes 1000 | tf_op jit(solution)/shard_map/pallas_call | solution.py:239
  93.4 1.6 %collective-permute-start.25 = (f32[768,128]{1,0:T(8,128)S(1)}, f32[768,128]{1,0:T(8,128)S(1)}, u32[]{:S(2)}, u32[]{:S(2)}) collective-permute-start(f32[768,128]{1,0:T(8,128)S(1)} %collective-permute-done.18.refs_6_), channel_id=1, source_target_pairs={{0,8},{8,0},{16,24},{24,16},{1,9},{9,1},{17,25},{25,17},{2,10},{10... | collective-permute-start | bytes 1179656 | tf_op jit(solution)/shard_map/ppermute | solution.py:281
  95.0 2.6 %collective-permute-start.19 = (f32[96,128]{1,0:T(8,128)S(1)}, f32[96,128]{1,0:T(8,128)S(1)}, u32[]{:S(2)}, u32[]{:S(2)}) collective-permute-start(f32[96,128]{1,0:T(8,128)S(1)} %add.54), channel_id=1, source_target_pairs={{0,4},{1,5},{2,6},{3,7},{4,0},{5,1},{6,2},{7,3},{8,12},{9,13},{10,... | collective-permute-start | bytes 147464 | tf_op jit(solution)/shard_map/ppermute | solution.py:281
  97.6 1.5 %shard_map.48.refs_1_ = f32[2,192,64]{2,1,0:T(8,128)S(1)} custom-call(s32[1]{0:T(128)} %bitcast.refs_0_.core_ref, bf16[384,6144]{1,0:T(8,128)(2,1)S(1)} %bitcast.10, bf16[384,6144]{1,0:T(8,128)(2,1)S(1)} %bitcast.12, f32[768,128]{1,0:T(8,128)S(1)} %get-tuple-element.87.refs_3_, f32[768,128]{1,0:T(8,128)S(1)} %get-tuple-element.85.refs_4_, ...), custom_call_target="tpu_custom_call" | custom-call | flops 1000 | bytes 1000 | tf_op jit(solution)/shard_map/pallas_call | solution.py:188
  100.1 1.6 %collective-permute-start.20 = (f32[96,128]{1,0:T(8,128)S(1)}, f32[96,128]{1,0:T(8,128)S(1)}, u32[]{:S(2)}, u32[]{:S(2)}) collective-permute-start(f32[96,128]{1,0:T(8,128)S(1)} %add.55), channel_id=1, source_target_pairs={{0,2},{1,3},{2,0},{3,1},{4,6},{5,7},{6,4},{7,5},{8,10},{9,11},{10,... | collective-permute-start | bytes 147464 | tf_op jit(solution)/shard_map/ppermute | solution.py:281
  101.7 3.6 %shard_map.49.refs_1_ = f32[2,192,3072]{2,1,0:T(8,128)S(1)} custom-call(s32[1]{0:T(128)} %bitcast.refs_0_.core_ref, f32[192,128]{1,0:T(8,128)S(1)} %add.53.refs_0_, f32[192,128]{1,0:T(8,128)S(1)} %collective-permute-done.16.refs_1_, f32[192,128]{1,0:T(8,128)S(1)} %slice.9.refs_2_, f32[768,256]{1,0:T(8,128)S(1)} %collective-permute-done.2.refs_4_.refs_3_, ...), custom_call_target="tpu_custom_call" | custom-call | flops 1000 | bytes 1000 | tf_op jit(solution)/shard_map/pallas_call | solution.py:239
  109.9 2.7 %collective-permute-start.29 = (f32[96,128]{1,0:T(8,128)S(1)}, f32[96,128]{1,0:T(8,128)S(1)}, u32[]{:S(2)}, u32[]{:S(2)}) collective-permute-start(f32[96,128]{1,0:T(8,128)S(1)} %add.57), channel_id=1, source_target_pairs={{0,4},{1,5},{2,6},{3,7},{4,0},{5,1},{6,2},{7,3},{8,12},{9,13},{10,... | collective-permute-start | bytes 147464 | tf_op jit(solution)/shard_map/ppermute | solution.py:281
  114.3 2.7 %shard_map.52.part_ref = f32[2,192,6144]{2,1,0:T(8,128)S(1)} custom-call(s32[1]{0:T(128)} %bitcast.refs_0_.core_ref, f32[2,192,3072]{2,1,0:T(8,128)S(1)} %shard_map.46.refs_0_, f32[2,192,3072]{2,1,0:T(8,128)S(1)} %shard_map.49.refs_1_, f32[96,128]{1,0:T(8,128)S(1)} %add.56.refs_2_, f32[96,128]{1,0:T(8,128)S(1)} %collective-permute-done.24.refs_3_, ...), custom_call_target="tpu_custom_call" | custom-call | flops 1000 | bytes 1000 | tf_op jit(solution)/shard_map/pallas_call | solution.py:239
  117.1 1.5 %collective-permute-done.28 = f32[96,128]{1,0:T(8,128)S(1)} collective-permute-done((f32[96,128]{1,0:T(8,128)S(1)}, f32[96,128]{1,0:T(8,128)S(1)}, u32[]{:S(2)}, u32[]{:S(2)}) %collective-permute-start.28) | collective-permute-done | bytes 49184 | tf_op jit(solution)/shard_map/ppermute | solution.py:281
  119.9 4.9 %shard_map.53 = f32[2,192,6144]{2,1,0:T(8,128)} custom-call(s32[1]{0:T(128)} %bitcast.refs_0_.core_ref, s32[8]{0:T(128)S(1)} %stack.35.order_ref, f32[2,192,6144]{2,1,0:T(8,128)S(1)} %shard_map.52.part_ref, f32[96,128]{1,0:T(8,128)S(1)} %add_add_fusion.refs_0_, f32[96,128]{1,0:T(8,128)S(1)} %collective-permute-done.30.refs_1_, ...), custom_call_target="tpu_custom_call" | custom-call | flops 1000 | bytes 1000 | tf_op jit(solution)/shard_map/pallas_call | solution.py:269
  (82 shorter events, 30.4 us)
Async XLA Ops:
  1.4 21.5 %collective-permute-start = (f32[768,256]{1,0:T(8,128)S(1)}, f32[768,256]{1,0:T(8,128)}, u32[]{:S(2)}, u32[]{:S(2)}) collective-permute-start(f32[768,256]{1,0:T(8,128)S(1)} %get-tuple-element.54.refs_3_), channel_id=1, source_target_pairs={{0,8},{8,0},{16,24},{24,16},{1,9},{9,1},{17,25},{25,17},{2,10},{10... | collective-permute-start | bytes 2359304 | tf_op jit(solution)/shard_map/ppermute | solution.py:281
  4.4 20.6 %collective-permute-start.1 = (f32[768,256]{1,0:T(8,128)S(1)}, f32[768,256]{1,0:T(8,128)}, u32[]{:S(2)}, u32[]{:S(2)}) collective-permute-start(f32[768,256]{1,0:T(8,128)S(1)} %get-tuple-element.55.refs_4_), channel_id=1, source_target_pairs={{0,16},{8,24},{16,0},{24,8},{1,17},{9,25},{17,1},{25,9},{2,18},{10... | collective-permute-start | bytes 2359304 | tf_op jit(solution)/shard_map/ppermute | solution.py:281
  6.0 33.7 %collective-permute-start.2 = (f32[768,256]{1,0:T(8,128)S(1)}, f32[768,256]{1,0:T(8,128)S(1)}, u32[]{:S(2)}, u32[]{:S(2)}) collective-permute-start(f32[768,256]{1,0:T(8,128)S(1)} %get-tuple-element.55.refs_4_), channel_id=1, source_target_pairs={{0,8},{8,0},{16,24},{24,16},{1,9},{9,1},{17,25},{25,17},{2,10},{10... | collective-permute-start | bytes 2359304 | tf_op jit(solution)/shard_map/ppermute | solution.py:281
  6.5 35.3 %collective-permute-start.3 = (f32[768,256]{1,0:T(8,128)S(1)}, f32[768,256]{1,0:T(8,128)S(1)}, u32[]{:S(2)}, u32[]{:S(2)}) collective-permute-start(f32[768,256]{1,0:T(8,128)S(1)} %get-tuple-element.54.refs_3_), channel_id=1, source_target_pairs={{0,16},{8,24},{16,0},{24,8},{1,17},{9,25},{17,1},{25,9},{2,18},{10... | collective-permute-start | bytes 2359304 | tf_op jit(solution)/shard_map/ppermute | solution.py:281
  25.0 33.7 %collective-permute-start.4 = (f32[768,256]{1,0:T(8,128)}, f32[768,256]{1,0:T(8,128)}, u32[]{:S(2)}, u32[]{:S(2)}) collective-permute-start(f32[768,256]{1,0:T(8,128)} %collective-permute-done.refs_5_), channel_id=1, source_target_pairs={{0,16},{8,24},{16,0},{24,8},{1,17},{9,25},{17,1},{25,9},{2,18},{10... | collective-permute-start | bytes 2359304 | tf_op jit(solution)/shard_map/ppermute | solution.py:281
  26.5 32.2 %collective-permute-start.5 = (f32[768,256]{1,0:T(8,128)}, f32[768,256]{1,0:T(8,128)}, u32[]{:S(2)}, u32[]{:S(2)}) collective-permute-start(f32[768,256]{1,0:T(8,128)} %collective-permute-done.1.refs_6_), channel_id=1, source_target_pairs={{0,8},{8,0},{16,24},{24,16},{1,9},{9,1},{17,25},{25,17},{2,10},{10... | collective-permute-start | bytes 2359304 | tf_op jit(solution)/shard_map/ppermute | solution.py:281
  42.8 21.8 %collective-permute-start.7 = (f32[768,128]{1,0:T(8,128)S(1)}, f32[768,128]{1,0:T(8,128)S(1)}, u32[]{:S(2)}, u32[]{:S(2)}) collective-permute-start(f32[768,128]{1,0:T(8,128)S(1)} %get-tuple-element.67.refs_3_.refs_5_), channel_id=1, source_target_pairs={{0,8},{8,0},{16,24},{24,16},{1,9},{9,1},{17,25},{25,17},{2,10},{10... | collective-permute-start | bytes 1179656 | tf_op jit(solution)/shard_map/ppermute | solution.py:281
  43.0 22.7 %collective-permute-start.8 = (f32[768,128]{1,0:T(8,128)S(1)}, f32[768,128]{1,0:T(8,128)S(1)}, u32[]{:S(2)}, u32[]{:S(2)}) collective-permute-start(f32[768,128]{1,0:T(8,128)S(1)} %copy-done.5), channel_id=1, source_target_pairs={{0,16},{8,24},{16,0},{24,8},{1,17},{9,25},{17,1},{25,9},{2,18},{10... | collective-permute-start | bytes 1179656 | tf_op jit(solution)/shard_map/ppermute | solution.py:281
  61.2 1.4 %collective-permute-start.6 = (f32[192,128]{1,0:T(8,128)S(1)}, f32[192,128]{1,0:T(8,128)S(1)}, u32[]{:S(2)}, u32[]{:S(2)}) collective-permute-start(f32[192,128]{1,0:T(8,128)S(1)} %get-tuple-element.59), channel_id=1, source_target_pairs={{0,1},{1,0},{2,3},{3,2},{4,5},{5,4},{6,7},{7,6},{8,9},{9,8},{10,11... | collective-permute-start | bytes 294920 | tf_op jit(solution)/shard_map/ppermute | solution.py:281
  62.6 12.0 %collective-permute-start.10 = (f32[768,128]{1,0:T(8,128)S(1)}, f32[768,128]{1,0:T(8,128)S(1)}, u32[]{:S(2)}, u32[]{:S(2)}) collective-permute-start(f32[768,128]{1,0:T(8,128)S(1)} %copy-done.5), channel_id=1, source_target_pairs={{0,8},{8,0},{16,24},{24,16},{1,9},{9,1},{17,25},{25,17},{2,10},{10... | collective-permute-start | bytes 1179656 | tf_op jit(solution)/shard_map/ppermute | solution.py:281
  62.7 12.0 %collective-permute-start.11 = (f32[768,128]{1,0:T(8,128)S(1)}, f32[768,128]{1,0:T(8,128)S(1)}, u32[]{:S(2)}, u32[]{:S(2)}) collective-permute-start(f32[768,128]{1,0:T(8,128)S(1)} %get-tuple-element.67.refs_3_.refs_5_), channel_id=1, source_target_pairs={{0,16},{8,24},{16,0},{24,8},{1,17},{9,25},{17,1},{25,9},{2,18},{10... | collective-permute-start | bytes 1179656 | tf_op jit(solution)/shard_map/ppermute | solution.py:281
  67.2 6.1 %collective-permute-start.9 = (f32[192,128]{1,0:T(8,128)S(1)}, f32[192,128]{1,0:T(8,128)S(1)}, u32[]{:S(2)}, u32[]{:S(2)}) collective-permute-start(f32[192,128]{1,0:T(8,128)S(1)} %add.51), channel_id=1, source_target_pairs={{0,4},{1,5},{2,6},{3,7},{4,0},{5,1},{6,2},{7,3},{8,12},{9,13},{10,... | collective-permute-start | bytes 294920 | tf_op jit(solution)/shard_map/ppermute | solution.py:281
  69.8 14.1 %collective-permute-start.13 = (f32[768,128]{1,0:T(8,128)S(1)}, f32[768,128]{1,0:T(8,128)S(1)}, u32[]{:S(2)}, u32[]{:S(2)}) collective-permute-start(f32[768,128]{1,0:T(8,128)S(1)} %collective-permute-done.7.refs_5_.refs_7_), channel_id=1, source_target_pairs={{0,16},{8,24},{16,0},{24,8},{1,17},{9,25},{17,1},{25,9},{2,18},{10... | collective-permute-start | bytes 1179656 | tf_op jit(solution)/shard_map/ppermute | solution.py:281
  71.3 12.6 %collective-permute-start.14 = (f32[768,128]{1,0:T(8,128)S(1)}, f32[768,128]{1,0:T(8,128)S(1)}, u32[]{:S(2)}, u32[]{:S(2)}) collective-permute-start(f32[768,128]{1,0:T(8,128)S(1)} %collective-permute-done.8.refs_6_.refs_8_), channel_id=1, source_target_pairs={{0,8},{8,0},{16,24},{24,16},{1,9},{9,1},{17,25},{25,17},{2,10},{10... | collective-permute-start | bytes 1179656 | tf_op jit(solution)/shard_map/ppermute | solution.py:281
  75.6 16.8 %collective-permute-start.17 = (f32[768,128]{1,0:T(8,128)S(1)}, f32[768,128]{1,0:T(8,128)S(1)}, u32[]{:S(2)}, u32[]{:S(2)}) collective-permute-start(f32[768,128]{1,0:T(8,128)S(1)} %get-tuple-element.87.refs_3_), channel_id=1, source_target_pairs={{0,8},{8,0},{16,24},{24,16},{1,9},{9,1},{17,25},{25,17},{2,10},{10... | collective-permute-start | bytes 1179656 | tf_op jit(solution)/shard_map/ppermute | solution.py:281
  77.6 14.7 %collective-permute-start.18 = (f32[768,128]{1,0:T(8,128)S(1)}, f32[768,128]{1,0:T(8,128)S(1)}, u32[]{:S(2)}, u32[]{:S(2)}) collective-permute-start(f32[768,128]{1,0:T(8,128)S(1)} %get-tuple-element.85.refs_4_), channel_id=1, source_target_pairs={{0,16},{8,24},{16,0},{24,8},{1,17},{9,25},{17,1},{25,9},{2,18},{10... | collective-permute-start | bytes 1179656 | tf_op jit(solution)/shard_map/ppermute | solution.py:281
  79.2 4.6 %collective-permute-start.12 = (f32[192,128]{1,0:T(8,128)S(1)}, f32[192,128]{1,0:T(8,128)S(1)}, u32[]{:S(2)}, u32[]{:S(2)}) collective-permute-start(f32[192,128]{1,0:T(8,128)S(1)} %add.52), channel_id=1, source_target_pairs={{0,2},{1,3},{2,0},{3,1},{4,6},{5,7},{6,4},{7,5},{8,10},{9,11},{10,... | collective-permute-start | bytes 294920 | tf_op jit(solution)/shard_map/ppermute | solution.py:281
  83.8 13.8 %slice-start.2 = ((s8[4718592]{0:T(1024)(128)(4,1)}), s8[4194304]{0:T(1024)(128)(4,1)S(1)}, s32[]{:S(2)}) async-start(s8[4718592]{0:T(1024)(128)(4,1)} %bitcast.11), calls=%async_computation.2 | async-start | bytes 8388608
  83.8 5.1 %collective-permute-start.16 = (f32[192,128]{1,0:T(8,128)S(1)}, f32[192,128]{1,0:T(8,128)S(1)}, u32[]{:S(2)}, u32[]{:S(2)}) collective-permute-start(f32[192,128]{1,0:T(8,128)S(1)} %add.53.refs_0_), channel_id=1, source_target_pairs={{0,1},{1,0},{2,3},{3,2},{4,5},{5,4},{6,7},{7,6},{8,9},{9,8},{10,11... | collective-permute-start | bytes 294920 | tf_op jit(solution)/shard_map/ppermute | solution.py:281
  84.9 1.4 %collective-permute-start.15 = (f32[96,128]{1,0:T(8,128)S(1)}, f32[96,128]{1,0:T(8,128)S(1)}, u32[]{:S(2)}, u32[]{:S(2)}) collective-permute-start(f32[96,128]{1,0:T(8,128)S(1)} %get-tuple-element.75), channel_id=1, source_target_pairs={{0,1},{1,0},{2,3},{3,2},{4,5},{5,4},{6,7},{7,6},{8,9},{9,8},{10,11... | collective-permute-start | bytes 147464 | tf_op jit(solution)/shard_map/ppermute | solution.py:281
  86.3 19.1 %collective-permute-start.21 = (f32[768,128]{1,0:T(8,128)S(1)}, f32[768,128]{1,0:T(8,128)S(1)}, u32[]{:S(2)}, u32[]{:S(2)}) collective-permute-start(f32[768,128]{1,0:T(8,128)S(1)} %get-tuple-element.85.refs_4_), channel_id=1, source_target_pairs={{0,8},{8,0},{16,24},{24,16},{1,9},{9,1},{17,25},{25,17},{2,10},{10... | collective-permute-start | bytes 1179656 | tf_op jit(solution)/shard_map/ppermute | solution.py:281
  87.4 18.0 %collective-permute-start.22 = (f32[768,128]{1,0:T(8,128)S(1)}, f32[768,128]{1,0:T(8,128)S(1)}, u32[]{:S(2)}, u32[]{:S(2)}) collective-permute-start(f32[768,128]{1,0:T(8,128)S(1)} %get-tuple-element.87.refs_3_), channel_id=1, source_target_pairs={{0,16},{8,24},{16,0},{24,8},{1,17},{9,25},{17,1},{25,9},{2,18},{10... | collective-permute-start | bytes 1179656 | tf_op jit(solution)/shard_map/ppermute | solution.py:281
  92.4 15.3 %collective-permute-start.23 = (f32[768,128]{1,0:T(8,128)S(1)}, f32[768,128]{1,0:T(8,128)S(1)}, u32[]{:S(2)}, u32[]{:S(2)}) collective-permute-start(f32[768,128]{1,0:T(8,128)S(1)} %collective-permute-done.17.refs_5_), channel_id=1, source_target_pairs={{0,16},{8,24},{16,0},{24,8},{1,17},{9,25},{17,1},{25,9},{2,18},{10... | collective-permute-start | bytes 1179656 | tf_op jit(solution)/shard_map/ppermute | solution.py:281
  93.4 14.3 %collective-permute-start.25 = (f32[768,128]{1,0:T(8,128)S(1)}, f32[768,128]{1,0:T(8,128)S(1)}, u32[]{:S(2)}, u32[]{:S(2)}) collective-permute-start(f32[768,128]{1,0:T(8,128)S(1)} %collective-permute-done.18.refs_6_), channel_id=1, source_target_pairs={{0,8},{8,0},{16,24},{24,16},{1,9},{9,1},{17,25},{25,17},{2,10},{10... | collective-permute-start | bytes 1179656 | tf_op jit(solution)/shard_map/ppermute | solution.py:281
  95.0 5.0 %collective-permute-start.19 = (f32[96,128]{1,0:T(8,128)S(1)}, f32[96,128]{1,0:T(8,128)S(1)}, u32[]{:S(2)}, u32[]{:S(2)}) collective-permute-start(f32[96,128]{1,0:T(8,128)S(1)} %add.54), channel_id=1, source_target_pairs={{0,4},{1,5},{2,6},{3,7},{4,0},{5,1},{6,2},{7,3},{8,12},{9,13},{10,... | collective-permute-start | bytes 147464 | tf_op jit(solution)/shard_map/ppermute | solution.py:281
  100.1 5.2 %collective-permute-start.20 = (f32[96,128]{1,0:T(8,128)S(1)}, f32[96,128]{1,0:T(8,128)S(1)}, u32[]{:S(2)}, u32[]{:S(2)}) collective-permute-start(f32[96,128]{1,0:T(8,128)S(1)} %add.55), channel_id=1, source_target_pairs={{0,2},{1,3},{2,0},{3,1},{4,6},{5,7},{6,4},{7,5},{8,10},{9,11},{10,... | collective-permute-start | bytes 147464 | tf_op jit(solution)/shard_map/ppermute | solution.py:281
  105.3 1.3 %collective-permute-start.24 = (f32[96,128]{1,0:T(8,128)S(1)}, f32[96,128]{1,0:T(8,128)S(1)}, u32[]{:S(2)}, u32[]{:S(2)}) collective-permute-start(f32[96,128]{1,0:T(8,128)S(1)} %add.56.refs_2_), channel_id=1, source_target_pairs={{0,1},{1,0},{2,3},{3,2},{4,5},{5,4},{6,7},{7,6},{8,9},{9,8},{10,11... | collective-permute-start | bytes 147464 | tf_op jit(solution)/shard_map/ppermute | solution.py:281
  108.6 1.3 %collective-permute-start.26 = (f32[96,128]{1,0:T(8,128)S(1)}, f32[96,128]{1,0:T(8,128)S(1)}, u32[]{:S(2)}, u32[]{:S(2)}) collective-permute-start(f32[96,128]{1,0:T(8,128)S(1)} %get-tuple-element.94), channel_id=1, source_target_pairs={{0,1},{1,0},{2,3},{3,2},{4,5},{5,4},{6,7},{7,6},{8,9},{9,8},{10,11... | collective-permute-start | bytes 147464 | tf_op jit(solution)/shard_map/ppermute | solution.py:281
  109.9 7.1 %collective-permute-start.29 = (f32[96,128]{1,0:T(8,128)S(1)}, f32[96,128]{1,0:T(8,128)S(1)}, u32[]{:S(2)}, u32[]{:S(2)}) collective-permute-start(f32[96,128]{1,0:T(8,128)S(1)} %add.57), channel_id=1, source_target_pairs={{0,4},{1,5},{2,6},{3,7},{4,0},{5,1},{6,2},{7,3},{8,12},{9,13},{10,... | collective-permute-start | bytes 147464 | tf_op jit(solution)/shard_map/ppermute | solution.py:281
  112.6 6.0 %collective-permute-start.28 = (f32[96,128]{1,0:T(8,128)S(1)}, f32[96,128]{1,0:T(8,128)S(1)}, u32[]{:S(2)}, u32[]{:S(2)}) collective-permute-start(f32[96,128]{1,0:T(8,128)S(1)} %add.57), channel_id=1, source_target_pairs={{0,6},{1,7},{2,4},{3,5},{4,2},{5,3},{6,0},{7,1},{8,14},{9,15},{10,... | collective-permute-start | bytes 147464 | tf_op jit(solution)/shard_map/ppermute | solution.py:281
  114.0 4.6 %collective-permute-start.27 = (f32[96,128]{1,0:T(8,128)S(1)}, f32[96,128]{1,0:T(8,128)S(1)}, u32[]{:S(2)}, u32[]{:S(2)}) collective-permute-start(f32[96,128]{1,0:T(8,128)S(1)} %add.57), channel_id=1, source_target_pairs={{0,2},{1,3},{2,0},{3,1},{4,6},{5,7},{6,4},{7,5},{8,10},{9,11},{10,... | collective-permute-start | bytes 147464 | tf_op jit(solution)/shard_map/ppermute | solution.py:281
  118.6 1.3 %collective-permute-start.30 = (f32[96,128]{1,0:T(8,128)S(1)}, f32[96,128]{1,0:T(8,128)S(1)}, u32[]{:S(2)}, u32[]{:S(2)}) collective-permute-start(f32[96,128]{1,0:T(8,128)S(1)} %add_add_fusion.refs_0_), channel_id=1, source_target_pairs={{0,1},{1,0},{2,3},{3,2},{4,5},{5,4},{6,7},{7,6},{8,9},{9,8},{10,11... | collective-permute-start | bytes 147464 | tf_op jit(solution)/shard_map/ppermute | solution.py:281
  (10 other events, 54.8 us)
